TPU v7x, 32 devices: a whole 2x2x4 slice. The times are simulated.
32 devices in a mesh: groups: 2 (over y), depth: 4 (over z), probe: 2 (over x), lat: 2 (over core).
Axes of the slice: x: 2, y: 2, z: 4, core: 2. Of those that a mesh axis runs over, the one named last changes fastest.
Arguments:
- specimen: float32 [2, 16, 768, 768], P(None, ('groups', 'depth'), 'lat'), parts along dimension 1, may hold values from -1 to 1, as said below
- illumination: float32 [2, 128, 128], replicated, may hold values from -5 to 5
- positions: int32 [1024, 2], P('groups'), parts along dimension 0, may hold values from 0 to 640
- scan_index: int32 [32, 4], P('groups', ('probe', 'lat')), parts along dimension 0, may hold values from 0 to 511
- frames: float32 [32, 4, 128, 128], P('groups', ('probe', 'lat')), parts along dimension 0, may hold values from 0 to 2
Outputs:
- specimen_grad: float32 [2, 16, 768, 768], P(None, ('groups', 'depth'), ('probe', 'lat')), parts along dimension 1
There are 2 independent parts, one for each index of `groups`. A program takes and returns all parts, laid end to end along the dimension named above; an argument that names none is the same for every part. Nothing has to cross between parts.
Inputs may be any that keep to these rules, and one draw needn't show every extreme that they name: `specimen`: every pixel's complex transmission has a magnitude of 0.99 to 1.
All inputs are finite; a program needn't handle non-finite values.
Results may differ from a plain program's by a relative error of at most 0.00055.
Values sent between devices are 32-bit elements; how exact they have to be, the bound alone decides.
No kernel may reach another device: no remote copies, remote signals or barrier semaphores. Data moves between devices by JAX's collectives and lax.ppermute only.
A program may use at most 128 MiB of HBM per device.

v0:
```python
import math

import jax
import jax.numpy as jnp
from jax import lax
from jax.sharding import PartitionSpec as P

PRECISE = lax.Precision.HIGHEST
FRESNEL = 8.0


def from_behind(shard, axis, by):
    devices = lax.axis_size(axis)
    pairs = [(i, i + by) for i in range(devices) if 0 <= i + by < devices]
    return lax.ppermute(shard, axis, pairs)


def make_tables(pixels):
    index_all = jnp.arange(pixels, dtype=jnp.int32)
    freq_all = (
        jnp.where(index_all < pixels // 2, index_all, index_all - pixels).astype(jnp.float32)
        / pixels
    )
    spread = (index_all[:, None] - index_all[None, :]).astype(jnp.float32)
    phase_all = (
        2.0 * math.pi * freq_all[None, None, :] * spread[:, :, None]
        - math.pi * FRESNEL * freq_all * freq_all
    )
    propagator = (jnp.mean(jnp.cos(phase_all), axis=-1), jnp.mean(jnp.sin(phase_all), axis=-1))
    turns = (index_all[:, None] * index_all[None, :] % pixels).astype(jnp.float32)
    angle_all = -2.0 * math.pi * turns / pixels
    norm_factor = 1.0 / math.sqrt(pixels)
    fourier = (jnp.cos(angle_all) * norm_factor, jnp.sin(angle_all) * norm_factor)
    return (propagator, fourier)


def complex_apply(pattern, matrix, fields, conjugate):
    mat_real, mat_imag = matrix
    if conjugate:
        mat_imag = -mat_imag
    wave_real, wave_imag = (fields[:, 0], fields[:, 1])
    out_real = jnp.einsum(pattern, mat_real, wave_real, precision=PRECISE) - jnp.einsum(
        pattern, mat_imag, wave_imag, precision=PRECISE
    )
    out_imag = jnp.einsum(pattern, mat_real, wave_imag, precision=PRECISE) + jnp.einsum(
        pattern, mat_imag, wave_real, precision=PRECISE
    )
    return jnp.stack([out_real, out_imag], axis=1)


def apply_left(matrix, fields):
    return complex_apply("ab,nbc->nac", matrix, fields, False)


def apply_right(matrix, fields):
    return complex_apply("cb,nab->nac", matrix, fields, False)


def adjoint_left(matrix, fields):
    return complex_apply("ba,nbc->nac", matrix, fields, True)


def adjoint_right(matrix, fields):
    return complex_apply("cb,nac->nab", matrix, fields, True)


def complex_product(left_term, right_term):
    out_real = left_term[:, 0] * right_term[:, 0] - left_term[:, 1] * right_term[:, 1]
    out_imag = left_term[:, 0] * right_term[:, 1] + left_term[:, 1] * right_term[:, 0]
    return jnp.stack([out_real, out_imag], axis=1)


def conj_product(grads, values):
    out_real = grads[:, 0] * values[:, 0] + grads[:, 1] * values[:, 1]
    out_imag = grads[:, 1] * values[:, 0] - grads[:, 0] * values[:, 1]
    return jnp.stack([out_real, out_imag], axis=1)


def forward_section(incoming, patches, propagator):
    inputs_seen = []
    current = incoming
    for layer_id in range(patches.shape[2]):
        inputs_seen.append(current)
        chi_wave = complex_product(patches[:, :, layer_id], current)
        current = apply_right(propagator, apply_left(propagator, chi_wave))
    return (current, jnp.stack(inputs_seen, axis=0))


def backward_section(grad_out, patches, inputs_seen, propagator):
    patch_grads = []
    current = grad_out
    for layer_id in reversed(range(patches.shape[2])):
        grad_chi = adjoint_left(propagator, adjoint_right(propagator, current))
        patch_grads.append(conj_product(grad_chi, inputs_seen[layer_id]))
        current = conj_product(grad_chi, patches[:, :, layer_id])
    return (current, jnp.stack(patch_grads[::-1], axis=2))


def exit_gradient(exit_wave, measured, fourier):
    far_field = apply_right(fourier, apply_left(fourier, exit_wave))
    misfit = far_field[:, 0] * far_field[:, 0] + far_field[:, 1] * far_field[:, 1] - measured
    grad_far = far_field * misfit[:, None]
    return adjoint_left(fourier, adjoint_right(fourier, grad_far))


def cut_patches(specimen_full, corners, pixels):

    def cut_one(corner):
        return lax.dynamic_slice(
            specimen_full,
            (jnp.int32(0), jnp.int32(0), corner[0], corner[1]),
            (specimen_full.shape[0], specimen_full.shape[1], pixels, pixels),
        )

    return jax.vmap(cut_one)(corners)


def deposit(running, patch_grads, corners):

    def add_one(index_probe, buffer_now):
        corner = corners[index_probe]
        start_at = (jnp.int32(0), jnp.int32(0), corner[0], corner[1])
        region = lax.dynamic_slice(buffer_now, start_at, patch_grads.shape[1:])
        return lax.dynamic_update_slice(buffer_now, region + patch_grads[index_probe], start_at)

    return lax.fori_loop(0, patch_grads.shape[0], add_one, running)


def local(specimen, illumination, positions, scan_index, frames):
    pixels = illumination.shape[-1]
    propagator, fourier = make_tables(pixels)
    specimen_full = lax.all_gather(specimen, "lat", axis=2, tiled=True)
    layers = specimen.shape[1]
    section_id = lax.axis_index("depth")
    sections = lax.axis_size("depth")
    is_last = section_id == sections - 1
    batches, per_device = scan_index.shape
    group_size = batches * per_device // batches
    group_corners = positions[scan_index]
    wave_shape = (group_size, 2, pixels, pixels)
    start_wave = jnp.broadcast_to(illumination, wave_shape)
    tick_count = batches + sections - 1

    def run_forward(incoming, patches):
        return forward_section(incoming, patches, propagator)

    def skip_forward(incoming, patches):
        return (jnp.zeros(wave_shape, jnp.float32), jnp.zeros((layers,) + wave_shape, jnp.float32))

    def forward_tick(tick_id, loop_state):
        arrived, stored, exit_waves = loop_state
        group_id = tick_id - section_id
        active = (group_id >= 0) & (group_id < batches)
        safe_id = jnp.clip(group_id, 0, batches - 1)
        incoming = jnp.where(section_id == 0, start_wave, arrived)
        patches = cut_patches(specimen_full, group_corners[safe_id], pixels)
        leaving, inputs_seen = lax.cond(active, run_forward, skip_forward, incoming, patches)
        stored = lax.dynamic_update_index_in_dim(
            stored, jnp.where(active, inputs_seen, stored[safe_id]), safe_id, 0
        )
        exit_waves = lax.dynamic_update_index_in_dim(
            exit_waves, jnp.where(active, leaving, exit_waves[safe_id]), safe_id, 0
        )
        arrived = from_behind(leaving, "depth", 1)
        return (arrived, stored, exit_waves)

    stored = jnp.zeros((batches, layers) + wave_shape, jnp.float32)
    exit_waves = jnp.zeros((batches,) + wave_shape, jnp.float32)
    arrived = jnp.zeros(wave_shape, jnp.float32)
    arrived, stored, exit_waves = lax.fori_loop(
        0, tick_count, forward_tick, (arrived, stored, exit_waves)
    )

    def exit_grads(exit_all):
        flattened = exit_all.reshape((-1, 2, pixels, pixels))
        return exit_gradient(flattened, frames.reshape((-1, pixels, pixels)), fourier).reshape(
            exit_all.shape
        )

    def no_grads(exit_all):
        return jnp.zeros_like(exit_all)

    grad_exits = lax.cond(is_last, exit_grads, no_grads, exit_waves)
    grad_shape = (group_size, 2, layers, pixels, pixels)

    def run_backward(incoming, patches, inputs_seen):
        return backward_section(incoming, patches, inputs_seen, propagator)

    def skip_backward(incoming, patches, inputs_seen):
        return (jnp.zeros(wave_shape, jnp.float32), jnp.zeros(grad_shape, jnp.float32))

    def backward_tick(tick_id, loop_state):
        arrived, patch_store = loop_state
        group_id = tick_id - (sections - 1 - section_id)
        active = (group_id >= 0) & (group_id < batches)
        safe_id = jnp.clip(group_id, 0, batches - 1)
        incoming = jnp.where(is_last, grad_exits[safe_id], arrived)
        patches = cut_patches(specimen_full, group_corners[safe_id], pixels)
        leaving, patch_grads = lax.cond(
            active, run_backward, skip_backward, incoming, patches, stored[safe_id]
        )
        patch_store = lax.dynamic_update_index_in_dim(
            patch_store, jnp.where(active, patch_grads, patch_store[safe_id]), safe_id, 0
        )
        arrived = from_behind(leaving, "depth", -1)
        return (arrived, patch_store)

    patch_store = jnp.zeros((batches,) + grad_shape, jnp.float32)
    arrived = jnp.zeros(wave_shape, jnp.float32)
    arrived, patch_store = lax.fori_loop(0, tick_count, backward_tick, (arrived, patch_store))
    flat_grads = patch_store.reshape((-1,) + grad_shape[1:])
    flat_corners = group_corners.reshape((-1, 2))
    running = deposit(jnp.zeros(specimen_full.shape, jnp.float32), flat_grads, flat_corners)
    return lax.psum_scatter(running, ("probe", "lat"), scatter_dimension=2, tiled=True)


def solution(mesh):
    return jax.shard_map(
        local,
        mesh=mesh,
        in_specs=(
            P(None, ("groups", "depth"), "lat", None),
            P(),
            P("groups", None),
            P("groups", ("probe", "lat")),
            P("groups", ("probe", "lat"), None, None),
        ),
        out_specs=P(None, ("groups", "depth"), ("probe", "lat"), None),
        check_vma=False,
    )
```

profile of v0, /device:TPU:0, one launch (start us, length us, event | category | flops | bytes accessed | tf_op | source)
XLA Modules:
  0.0 1089.8 jit_solution(10291069416113974077)
XLA Ops:
  6.5 6.1 copy.34
  14.3 33.9 %sine_reduce_fusion = (f32[128,128]{1,0:T(8,128)S(1)}, f32[128,128]{1,0:T(8,128)S(1)}) fusion(f32[128]{0:T(128)S(1)} %multiply_multiply_fusion, f32[128,128]{1,0:T(8,128)S(1)} %subtract_convert_fusion, f32[128]{0:T(128)S(1)} %broadcast_multiply_fusion.2), kind=kLoop, calls=%fused_computation.271 | loop fusion | flops 8355840 | bytes 197632 | tf_op jit(solution)/shard_map/reduce_sum | solution.py:29
  48.3 9.6 copy.37
  61.4 351.0 %while.50 = (s32[]{:T(128)}, f32[1,2,128,128]{3,2,1,0:T(8,128)S(1)}, f32[16,2,1,2,128,128]{4,5,3,2,1,0:T(8,128)}, f32[16,1,2,128,128]{4,3,2,1,0:T(8,128)S(1)}, s...) while((s32[]{:T(128)}, ...), condition=%wide.region_5.6_spmd, body=%wide.region_2.5_spmd.sunk | while | flops 403243040 | bytes 10945034 | solution.py:170
  65.6 7.9 conditional.6
  82.7 7.9 conditional.6
  102.0 7.9 conditional.6
  121.1 7.9 conditional.6
  140.1 7.9 conditional.6
  159.1 7.9 conditional.6
  178.1 7.9 conditional.6
  197.0 7.9 conditional.6
  216.0 7.9 conditional.6
  235.0 7.9 conditional.6
  254.0 7.9 conditional.6
  273.0 7.9 conditional.6
  292.0 7.9 conditional.6
  311.0 7.9 conditional.6
  330.0 7.9 conditional.6
  349.0 7.9 conditional.6
  368.5 12.2 %collective-permute-start = (f32[1,2,128,128]{3,2,1,0:T(8,128)S(1)}, f32[1,2,128,128]{3,2,1,0:T(8,128)S(1)}, u32[]{:S(2)}, u32[]{:S(2)}) collective-permute-start(f32[1,2,128,128]{3,2,1,0:T(8,128)S(1)} %get-tuple-element.1112), channel_id=1, source_target_pairs={{0,4},{4,8},{8,12},{1,5},{5,9},{9,13},{2,6},{6,10},{10,14},{3,7},{... | collective-permute-start | bytes 393224 | tf_op jit(solution)/shard_map/while/body/eval_jaxpr/ppermute | solution.py:15
  398.8 11.1 %collective-permute-start = (f32[1,2,128,128]{3,2,1,0:T(8,128)S(1)}, f32[1,2,128,128]{3,2,1,0:T(8,128)S(1)}, u32[]{:S(2)}, u32[]{:S(2)}) collective-permute-start(f32[1,2,128,128]{3,2,1,0:T(8,128)S(1)} %get-tuple-element.1112), channel_id=1, source_target_pairs={{0,4},{4,8},{8,12},{1,5},{5,9},{9,13},{2,6},{6,10},{10,14},{3,7},{... | collective-permute-start | bytes 393224 | tf_op jit(solution)/shard_map/while/body/eval_jaxpr/ppermute | solution.py:15
  416.5 422.1 %while.51 = (s32[]{:T(128)}, f32[1,2,128,128]{2,3,1,0:T(8,128)S(1)}, f32[16,1,2,2,128,128]{5,4,3,2,0,1:T(8,128)}, s32[]{:T(128)}, s32[16,1,2]{2,1,0:T(1,128)S(1)...) while((s32[]{:T(128)}, ...), condition=%wide.region_11.12_spmd, body=%wide.region_8.11_spmd.sunk | while | flops 403570720 | bytes 11666469 | solution.py:210
  435.7 9.6 collective-permute-done.1
  452.9 55.6 %collective-permute-done.1 = f32[1,2,128,128]{2,3,1,0:T(8,128)S(1)} collective-permute-done((f32[1,2,128,128]{2,3,1,0:T(8,128)S(1)}, f32[1,2,128,128]{2,3,1,0:T(8,128)S(1)}, u32[]{:S(2)}, u32[]{:S(2)}) %collective-permute-start.1) | collective-permute-done | bytes 131104 | tf_op jit(solution)/shard_map/while/body/eval_jaxpr/ppermute | solution.py:15
  512.7 9.5 conditional.7
  533.3 9.5 conditional.7
  553.8 9.5 conditional.7
  574.4 9.5 conditional.7
  595.0 9.5 conditional.7
  615.6 9.5 conditional.7
  636.1 9.5 conditional.7
  656.7 9.5 conditional.7
  677.3 9.5 conditional.7
  697.8 9.5 conditional.7
  718.4 9.5 conditional.7
  739.0 9.5 conditional.7
  759.5 9.5 conditional.7
  780.1 9.5 conditional.7
  792.9 4.5 collective-permute-done.1
  801.6 9.5 conditional.7
  822.2 9.5 conditional.7
  838.6 4.5 broadcast_in_dim.85
  843.1 161.4 %while.52 = (s32[]{:T(128)}, f32[2,2,768,768]{3,2,1,0:T(8,128)}, s32[16,2]{0,1:T(2,128)S(1)}, f32[16,2,2,128,128]{4,3,2,1,0:T(8,128)}, s32[]{:T(128)}, /*index=5*/s32[]{:T(128)}, s32[]{:T(128)}) while((s32[]{:T(128)}, f32[2,2,768,768]{3,2,1,0:T(8,128)}, s32[16,2]{0,1:T(2,128)S(1)}, f32[16,2,2,128,128]{4,3,2,1,0:T(8,128)}, s32[]{:T(128)}, ...), condition=%wide.region_13.14_spmd, body=%wide.region_12.13_spmd.sunk | while | flops 65544 | bytes 1310917 | solution.py:126
  909.5 4.4 dynamic_update_slice.45
  919.6 4.5 dynamic_update_slice.45
  969.7 4.4 dynamic_update_slice.45
  1004.5 78.5 %reduce-scatter.2.cloned.1.call-done = f32[2,2,192,768]{3,2,1,0:T(8,128)} async-done(((f32[2,2,768,768]{3,2,1,0:T(8,128)}), f32[2,2,192,768]{3,2,1,0:T(8,128)}) %reduce-scatter.2.cloned.1.call-update) | async-done | bytes 2359312 | tf_op jit(solution)/shard_map/reduce_scatter | solution.py:214
  (1343 shorter events, 633.6 us)
Async XLA Ops:
  6.5 41.8 %all-gather.2.cloned.1.call-start = ((), (), s32[]{:S(2)}) async-start(), calls=%async_computation.1 | async-start | bytes 14155776 | tf_op jit(solution)/shard_map/all_gather | solution.py:132
  12.6 0.7 copy-start.2
  12.6 0.8 copy-start.3
  12.7 1070.3 %reduce-scatter.2.cloned.1.call-start = ((), (), s32[]{:S(2)}) async-start(), calls=%async_computation.2 | async-start | bytes 11796480 | tf_op jit(solution)/shard_map/reduce_scatter | solution.py:214
  60.5 0.9 copy-start
  73.5 4.9 collective-permute-start
  90.6 7.2 collective-permute-start
  109.9 6.9 collective-permute-start
  128.9 6.9 collective-permute-start
  147.9 6.9 collective-permute-start
  166.9 6.9 collective-permute-start
  185.9 6.9 collective-permute-start
  204.9 6.9 collective-permute-start
  223.9 6.9 collective-permute-start
  242.9 6.9 collective-permute-start
  261.9 6.9 collective-permute-start
  280.9 6.9 collective-permute-start
  299.9 6.9 collective-permute-start
  318.9 6.9 collective-permute-start
  337.9 6.9 collective-permute-start
  356.9 7.3 collective-permute-start
  368.5 14.7 %collective-permute-start = (f32[1,2,128,128]{3,2,1,0:T(8,128)S(1)}, f32[1,2,128,128]{3,2,1,0:T(8,128)S(1)}, u32[]{:S(2)}, u32[]{:S(2)}) collective-permute-start(f32[1,2,128,128]{3,2,1,0:T(8,128)S(1)} %get-tuple-element.1112), channel_id=1, source_target_pairs={{0,4},{4,8},{8,12},{1,5},{5,9},{9,13},{2,6},{6,10},{10,14},{3,7},{... | collective-permute-start | bytes 393224 | tf_op jit(solution)/shard_map/while/body/eval_jaxpr/ppermute | solution.py:15
  387.6 6.9 collective-permute-start
  398.8 13.6 %collective-permute-start = (f32[1,2,128,128]{3,2,1,0:T(8,128)S(1)}, f32[1,2,128,128]{3,2,1,0:T(8,128)S(1)}, u32[]{:S(2)}, u32[]{:S(2)}) collective-permute-start(f32[1,2,128,128]{3,2,1,0:T(8,128)S(1)} %get-tuple-element.1112), channel_id=1, source_target_pairs={{0,4},{4,8},{8,12},{1,5},{5,9},{9,13},{2,6},{6,10},{10,14},{3,7},{... | collective-permute-start | bytes 393224 | tf_op jit(solution)/shard_map/while/body/eval_jaxpr/ppermute | solution.py:15
  420.8 7.3 collective-permute-start.1
  432.4 12.9 %collective-permute-start.1 = (f32[1,2,128,128]{2,3,1,0:T(8,128)S(1)}, f32[1,2,128,128]{2,3,1,0:T(8,128)S(1)}, u32[]{:S(2)}, u32[]{:S(2)}) collective-permute-start(f32[1,2,128,128]{2,3,1,0:T(8,128)S(1)} %get-tuple-element.1127), channel_id=1, source_target_pairs={{4,0},{8,4},{12,8},{5,1},{9,5},{13,9},{6,2},{10,6},{14,10},{7,3},{... | collective-permute-start | bytes 393224 | tf_op jit(solution)/shard_map/while/body/eval_jaxpr/ppermute | solution.py:15
  449.5 59.0 %collective-permute-start.1 = (f32[1,2,128,128]{2,3,1,0:T(8,128)S(1)}, f32[1,2,128,128]{2,3,1,0:T(8,128)S(1)}, u32[]{:S(2)}, u32[]{:S(2)}) collective-permute-start(f32[1,2,128,128]{2,3,1,0:T(8,128)S(1)} %get-tuple-element.1127), channel_id=1, source_target_pairs={{4,0},{8,4},{12,8},{5,1},{9,5},{13,9},{6,2},{10,6},{14,10},{7,3},{... | collective-permute-start | bytes 393224 | tf_op jit(solution)/shard_map/while/body/eval_jaxpr/ppermute | solution.py:15
  522.2 6.9 collective-permute-start.1
  542.8 6.9 collective-permute-start.1
  563.3 6.9 collective-permute-start.1
  583.9 6.9 collective-permute-start.1
  604.5 6.9 collective-permute-start.1
  625.1 6.9 collective-permute-start.1
  645.6 6.9 collective-permute-start.1
  666.2 6.9 collective-permute-start.1
  686.8 6.9 collective-permute-start.1
  707.3 6.9 collective-permute-start.1
  727.9 6.9 collective-permute-start.1
  748.5 6.9 collective-permute-start.1
  769.0 6.9 collective-permute-start.1
  789.6 7.8 collective-permute-start.1
  811.1 6.9 collective-permute-start.1
  831.7 6.9 collective-permute-start.1
Sparse Core Ops, SparseCore 0:
  12.8 24.5 all-gather.1
  1004.6 78.3 reduce-scatter.1
where the time goes:
time: 1110 us; the launch traced here: 1090 us
  local copies, waits for them, and re-layouts  320 us (29%)
  waiting for transfers between devices  215 us (19%)
  loops' own time  206 us (19%)
  matrix products  141 us (13%)
  starting transfers between devices  119 us (11%)
  other arithmetic  76.1 us (7%)
  between operations  13.5 us (1%)
    ppermute x38, waiting for transfers between devices, from_behind(): return lax.ppermute(shard, axis, pairs)  137 us
    ppermute x38, starting transfers between devices, from_behind(): return lax.ppermute(shard, axis, pairs)  119 us
    reduce_scatter x1, waiting for transfers between devices, local(): lax.psum_scatter(running, ('probe', 'lat'), scatter_dimension=2, tiled=True)  78.5 us
    gather x32, local copies, waits for them, and re-layouts, cut_one(): lax.dynamic_slice(specimen_full, (jnp.int32(0), jnp.int32(0), corner[0],...  76.5 us
    another operation x1, loops' own time, local(): lax.fori_loop(0, tick_count, forward_tick, (arrived, stored, exit_waves))  69.8 us
    dynamic_update_slice x16, local copies, waits for them, and re-layouts, add_one(): lax.dynamic_update_slice(buffer_now, region + patch_grads[index_probe], s...  69.4 us
    another operation x1, loops' own time, local(): lax.fori_loop(0, tick_count, backward_tick, (arrived, patch_store))  68.7 us
    another operation x1, loops' own time, deposit(): return lax.fori_loop(0, patch_grads.shape[0], add_one, running)  61.6 us
  transfers between devices with their start and end apart: 40, of which 39 were waited for; matrix products, arithmetic and copies ran while one was open for 10% of the time, Pallas kernels for 0%

commit v1 on v0

v1 whole, which is shorter than its diff:
```python
import functools
import math

import jax
import jax.numpy as jnp
import ml_dtypes
import numpy as np
from jax import lax
from jax.experimental import pallas as pl
from jax.experimental.pallas import tpu as pltpu
from jax.sharding import PartitionSpec as P

FRESNEL = 8.0
LAG = 1
F32 = jnp.float32
BF16 = jnp.bfloat16
HBM = pl.BlockSpec(memory_space=pl.ANY)


def real_blocks(matrix):
    real, imag = matrix.real, matrix.imag
    left = np.block([[real, -imag], [imag, real]])
    right = np.block([[real, imag], [-imag, real]])
    return np.stack([left, right])


@functools.lru_cache(maxsize=None)
def make_tables(pixels):
    index = np.arange(pixels)
    freq = np.where(index < pixels // 2, index, index - pixels) / pixels
    spread = index[:, None] - index[None, :]
    phase = 2.0 * math.pi * freq * spread[:, :, None] - math.pi * FRESNEL * freq * freq
    propagator = np.mean(np.exp(1j * phase), axis=-1)
    turns = index[:, None] * index[None, :] % pixels
    fourier = np.exp(-2j * math.pi * turns / pixels) / math.sqrt(pixels)
    blocks = np.stack([real_blocks(propagator), real_blocks(fourier)]).astype(np.float32)
    high = blocks.astype(ml_dtypes.bfloat16)
    low = (blocks - high.astype(np.float32)).astype(ml_dtypes.bfloat16)
    return np.stack([high, low], axis=2)


def halves(x):
    high = x.astype(BF16)
    return high, (x - high.astype(F32)).astype(BF16)


def dot(a, b):
    return jnp.dot(a, b, preferred_element_type=F32)


def transform(left, right, fields):
    size = fields[0][0].shape[0]
    stacked = jnp.concatenate(
        [
            jnp.concatenate([real for real, _ in fields], axis=1),
            jnp.concatenate([imag for _, imag in fields], axis=1),
        ],
        axis=0,
    )
    high, low = halves(stacked)
    mid = dot(left[0], high) + (dot(left[1], high) + dot(left[0], low))
    rows = jnp.concatenate(
        [
            jnp.concatenate(
                [mid[:size, i * size : (i + 1) * size], mid[size:, i * size : (i + 1) * size]], axis=1
            )
            for i in range(len(fields))
        ],
        axis=0,
    )
    high, low = halves(rows)
    out = dot(high, right[0]) + (dot(high, right[1]) + dot(low, right[0]))
    return [
        (out[i * size : (i + 1) * size, :size], out[i * size : (i + 1) * size, size:])
        for i in range(len(fields))
    ]


def times(a, b):
    return a[0] * b[0] - a[1] * b[1], a[0] * b[1] + a[1] * b[0]


def times_conj(a, b):
    return a[0] * b[0] + a[1] * b[1], a[1] * b[0] - a[0] * b[1]


def cut_kernel(pixels, corners, lat, own, other, out, window, sems):
    half = own.shape[2]
    width = own.shape[3]
    tall = pixels + 8
    step = pl.program_id(0)
    steps = pl.num_programs(0)

    def places(probe):
        row = corners[2 * probe]
        column = corners[2 * probe + 1]
        row0 = jnp.minimum(row // 8 * 8, 2 * half - tall)
        col0 = jnp.minimum(column // pixels * pixels, width - 2 * pixels)
        top = row0 < half
        bottom = row0 + tall > half
        top_from = jnp.minimum(row0, half - tall)
        bottom_from = jnp.clip(row0 - half, 0, half - tall)
        offset = jnp.where(top, row0 - top_from, tall)
        return top, bottom, top_from, bottom_from, offset, row - row0, col0, column - col0

    def copies(probe, slot, act):
        top, bottom, top_from, bottom_from, _, _, col0, _ = places(probe)
        own_top = lat[0] == 0
        col0 = pl.multiple_of(col0, pixels)
        for source, is_top, sem in ((own, own_top, 0), (other, jnp.logical_not(own_top), 1)):
            start = pl.multiple_of(jnp.where(is_top, top_from, bottom_from), 8)
            to = pl.multiple_of(jnp.where(is_top, 0, tall), 8)

            @pl.when(jnp.where(is_top, top, bottom))
            def _(source=source, start=start, to=to, sem=sem):
                act(
                    pltpu.make_async_copy(
                        source.at[:, :, pl.ds(start, tall), pl.ds(col0, 2 * pixels)],
                        window.at[slot, :, :, pl.ds(to, tall), :],
                        sems.at[slot, sem],
                    )
                )

    slot = step % 2

    @pl.when(step == 0)
    def _():
        copies(0, 0, lambda copy: copy.start())

    @pl.when(step + 1 < steps)
    def _():
        copies(step + 1, 1 - slot, lambda copy: copy.start())

    copies(step, slot, lambda copy: copy.wait())
    *_, offset, down, _, shift = places(step)
    offset = pl.multiple_of(offset, 8)
    turn = (pixels - shift) % pixels
    lane = lax.broadcasted_iota(jnp.int32, (tall, pixels), 1)
    for part in range(own.shape[0]):
        for layer in range(own.shape[1]):
            near = window[slot, part, layer, pl.ds(offset, tall), pl.ds(0, pixels)]
            far = window[slot, part, layer, pl.ds(offset, tall), pl.ds(pixels, pixels)]
            near = pltpu.roll(near, turn, 1)
            far = pltpu.roll(far, turn, 1)
            patch = jnp.where(lane < pixels - shift, near, far)
            out[0, layer, part] = pltpu.roll(patch, (tall - down) % tall, 0)[:pixels]


def cut_patches(own, other, corners, lat, pixels):
    count = corners.shape[0]
    parts, layers = own.shape[:2]
    return pl.pallas_call(
        functools.partial(cut_kernel, pixels),
        grid_spec=pltpu.PrefetchScalarGridSpec(
            num_scalar_prefetch=2,
            grid=(count,),
            in_specs=[HBM, HBM],
            out_specs=pl.BlockSpec((1, layers, parts, pixels, pixels), lambda i, *_: (i, 0, 0, 0, 0)),
            scratch_shapes=[
                pltpu.VMEM((2, parts, layers, 2 * (pixels + 8), 2 * pixels), F32),
                pltpu.SemaphoreType.DMA((2, 2)),
            ],
        ),
        out_shape=jax.ShapeDtypeStruct((count, layers, parts, pixels, pixels), F32),
        compiler_params=pltpu.CompilerParams(vmem_limit_bytes=16 << 20),
        cost_estimate=pl.CostEstimate(
            flops=count * layers * parts * pixels * pixels * 4,
            bytes_accessed=count * layers * parts * pixels * pixels * 12,
            transcendentals=0,
        ),
        name="cut_patches",
    )(corners.reshape(-1), lat.reshape(1), own, other)


def forward_kernel(
    scalars, patches, arrived, start_wave, frames, prop, last, unused, leave, seen
):
    _, _, active, first, final = (scalars[i] for i in range(5))
    count, layers = patches.shape[1:3]

    @pl.when(active == 1)
    def _():
        wave = [
            tuple(jnp.where(first == 1, start_wave[part], arrived[i, part]) for part in range(2))
            for i in range(count)
        ]
        for layer in range(layers):
            chi = []
            for i in range(count):
                for part in range(2):
                    seen[0, i, layer, part] = wave[i][part]
                here = patches[0, i, layer, 0], patches[0, i, layer, 1]
                chi.append(times(here, wave[i]))
            table = last if layer == layers - 1 else prop
            wave = transform(
                (table[0, 0, 0], table[0, 0, 1]), (table[0, 1, 0], table[0, 1, 1]), chi
            )
        for i in range(count):
            real, imag = wave[i]
            misfit = real * real + imag * imag - frames[0, i]
            factor = jnp.where(final == 1, misfit, 1.0)
            leave[i, 0] = real * factor
            leave[i, 1] = imag * factor


def backward_kernel(scalars, patches, arrived, own, seen, prop, last, unused, leave, grads):
    _, _, active, _, final = (scalars[i] for i in range(5))
    count, layers = patches.shape[1:3]

    @pl.when(active == 1)
    def _():
        wave = [
            tuple(jnp.where(final == 1, own[i, part], arrived[i, part]) for part in range(2))
            for i in range(count)
        ]
        for layer in reversed(range(layers)):
            table = last if layer == layers - 1 else prop
            chi = transform(
                (table[0, 1, 0], table[0, 1, 1]), (table[0, 0, 0], table[0, 0, 1]), wave
            )
            wave = []
            for i in range(count):
                before = seen[0, i, layer, 0], seen[0, i, layer, 1]
                here = patches[0, i, layer, 0], patches[0, i, layer, 1]
                real, imag = times_conj(chi[i], before)
                grads[0, i, layer, 0] = real
                grads[0, i, layer, 1] = imag
                wave.append(times_conj(chi[i], here))
        for i in range(count):
            leave[i, 0] = wave[i][0]
            leave[i, 1] = wave[i][1]


def section_specs(count, layers, pixels):
    whole = lambda shape: pl.BlockSpec(shape, lambda g, s: (0,) * len(shape))
    at_group = lambda shape: pl.BlockSpec((1,) + shape, lambda g, s: (s[0],) + (0,) * len(shape))
    at_slot = lambda shape: pl.BlockSpec((1,) + shape, lambda g, s: (s[1],) + (0,) * len(shape))
    stack = (count, layers, 2, pixels, pixels)
    wave = (count, 2, pixels, pixels)
    table = (1, 2, 2, 2 * pixels, 2 * pixels)
    prop = pl.BlockSpec(table, lambda g, s: (0, 0, 0, 0, 0))
    last = pl.BlockSpec(table, lambda g, s: (s[4], 0, 0, 0, 0))
    return whole, at_group, at_slot, stack, wave, prop, last


def cost(count, layers, pixels):
    return pl.CostEstimate(
        flops=count * layers * 2 * 3 * 8 * pixels**3,
        bytes_accessed=count * (layers * 4 + 4) * pixels * pixels * 4,
        transcendentals=0,
    )


def run_forward(scalars, patches, arrived, start_wave, frames, tables, store):
    _, count, layers, _, pixels, _ = patches.shape
    whole, at_group, at_slot, stack, wave, prop, last = section_specs(count, layers, pixels)
    return pl.pallas_call(
        forward_kernel,
        grid_spec=pltpu.PrefetchScalarGridSpec(
            num_scalar_prefetch=1,
            grid=(1,),
            in_specs=[
                at_group(stack),
                whole(wave),
                whole((2, pixels, pixels)),
                at_group((count, pixels, pixels)),
                prop,
                last,
                HBM,
            ],
            out_specs=[whole(wave), at_slot(stack)],
        ),
        out_shape=[
            jax.ShapeDtypeStruct(wave, F32),
            jax.ShapeDtypeStruct(store.shape, F32),
        ],
        input_output_aliases={7: 1},
        compiler_params=pltpu.CompilerParams(vmem_limit_bytes=24 << 20),
        cost_estimate=cost(count, layers, pixels),
        name="forward_section",
    )(scalars, patches, arrived, start_wave, frames, tables, tables, store)


def run_backward(scalars, patches, arrived, own, seen, tables, store):
    _, count, layers, _, pixels, _ = patches.shape
    whole, at_group, at_slot, stack, wave, prop, last = section_specs(count, layers, pixels)
    return pl.pallas_call(
        backward_kernel,
        grid_spec=pltpu.PrefetchScalarGridSpec(
            num_scalar_prefetch=1,
            grid=(1,),
            in_specs=[
                at_group(stack),
                whole(wave),
                whole(wave),
                at_group(stack),
                prop,
                last,
                HBM,
            ],
            out_specs=[whole(wave), at_slot(stack)],
        ),
        out_shape=[
            jax.ShapeDtypeStruct(wave, F32),
            jax.ShapeDtypeStruct(store.shape, F32),
        ],
        input_output_aliases={7: 1},
        compiler_params=pltpu.CompilerParams(vmem_limit_bytes=24 << 20),
        cost_estimate=cost(count, layers, pixels),
        name="backward_section",
    )(scalars, patches, arrived, own, seen, tables, tables, store)


def deposit_kernel(pixels, owners, corners, lat, grads, keep, send, total, sems):
    step = pl.program_id(0)
    height, width = total.shape[2:]
    rows = height // (2 * owners)

    @pl.when(step == 0)
    def _():
        total[...] = jnp.zeros(total.shape, F32)

    tall = pixels + 8
    lane = lax.broadcasted_iota(jnp.int32, (tall, pixels), 1)
    row = corners[2 * step]
    column = corners[2 * step + 1]
    row0 = pl.multiple_of(jnp.minimum(row // 8 * 8, height - tall), 8)
    col0 = jnp.minimum(column // pixels * pixels, width - 2 * pixels)
    shift = column - col0
    near_at = pl.multiple_of(col0, pixels)
    far_at = pl.multiple_of(col0 + pixels, pixels)
    blank = jnp.zeros((8, pixels), F32)
    for layer in range(total.shape[1]):
        for part in range(2):
            padded = jnp.concatenate([grads[0, layer, part], blank], axis=0)
            turned = pltpu.roll(pltpu.roll(padded, row - row0, 0), shift % pixels, 1)
            near = jnp.where(lane >= shift, turned, 0.0)
            far = jnp.where(lane >= shift, 0.0, turned)
            total[part, layer, pl.ds(row0, tall), pl.ds(near_at, pixels)] += near
            total[part, layer, pl.ds(row0, tall), pl.ds(far_at, pixels)] += far

    @pl.when(step == pl.num_programs(0) - 1)
    def _():
        copies = []
        for owner in range(owners):
            for kind, target in ((lat[0], keep), (1 - lat[0], send)):
                start = pl.multiple_of((2 * owner + kind) * rows, 8)
                copies.append(
                    pltpu.make_async_copy(
                        total.at[:, :, pl.ds(start, rows), :],
                        target.at[:, :, owner],
                        sems.at[len(copies)],
                    )
                )
        for copy in copies:
            copy.start()
        for copy in copies:
            copy.wait()


def deposit(grads, corners, lat, owners, height, width):
    count = corners.shape[0]
    _, layers, parts, pixels, _ = grads.shape
    half = jax.ShapeDtypeStruct((parts, layers, owners, height // (2 * owners), width), F32)
    return pl.pallas_call(
        functools.partial(deposit_kernel, pixels, owners),
        grid_spec=pltpu.PrefetchScalarGridSpec(
            num_scalar_prefetch=2,
            grid=(count,),
            in_specs=[
                pl.BlockSpec((1, layers, parts, pixels, pixels), lambda i, *_: (i, 0, 0, 0, 0))
            ],
            out_specs=[HBM, HBM],
            scratch_shapes=[
                pltpu.VMEM((parts, layers, height, width), F32),
                pltpu.SemaphoreType.DMA((2 * owners,)),
            ],
        ),
        out_shape=[half, half],
        compiler_params=pltpu.CompilerParams(vmem_limit_bytes=32 << 20),
        cost_estimate=pl.CostEstimate(
            flops=count * layers * parts * pixels * pixels * 8,
            bytes_accessed=grads.size * 4 + parts * layers * height * width * 4,
            transcendentals=0,
        ),
        name="deposit_patches",
    )(corners.reshape(-1), lat.reshape(1), grads)


def swap(shard, axis):
    return lax.ppermute(shard, axis, [(0, 1), (1, 0)])


def local(specimen, illumination, positions, scan_index, frames):
    pixels = illumination.shape[-1]
    parts, layers, half, width = specimen.shape
    tables = jnp.asarray(make_tables(pixels))
    section = lax.axis_index("depth")
    sections = lax.axis_size("depth")
    lat = lax.axis_index("lat")
    owners = lax.axis_size("probe")

    other = swap(specimen, "lat")
    corners = positions[scan_index.reshape(-1)]
    probes = corners.shape[0]
    count = 2 if probes % 2 == 0 else 1
    groups = probes // count
    stack = (count, layers, parts, pixels, pixels)
    wave = (count, parts, pixels, pixels)
    patches = cut_patches(specimen, other, corners, lat, pixels).reshape((groups,) + stack)
    measured = frames.reshape((groups, count, pixels, pixels))

    is_first = (section == 0).astype(jnp.int32)
    is_last = (section == sections - 1).astype(jnp.int32)

    def scalars_of(group):
        active = (group >= 0) & (group < groups)
        at = jnp.clip(group, 0, groups - 1)
        slot = jnp.where(active, group, groups)
        return jnp.stack([at, slot, active.astype(jnp.int32), is_first, is_last]).astype(jnp.int32)

    def pairs_of(tick, by):
        pairs = []
        for source in range(sections):
            delay = source if by > 0 else 2 * (sections - 1) - source
            if 0 <= source + by < sections and 0 <= tick - LAG * delay < groups:
                pairs.append((source, source + by))
        return pairs

    seen = jnp.zeros((groups + 1,) + stack, F32)
    grads = jnp.zeros((groups + 1,) + stack, F32)
    nothing = jnp.zeros(wave, F32)
    down, up = {}, {}
    depth = LAG * (sections - 1)
    for tick in range(groups + 2 * depth):
        leaving = nothing
        if tick < groups + depth:
            scalars = scalars_of(tick - LAG * section)
            leaving, seen = run_forward(
                scalars, patches, down.pop(tick - LAG, nothing), illumination, measured, tables, seen
            )
            pairs = pairs_of(tick, 1)
            if pairs:
                down[tick] = lax.ppermute(leaving, "depth", pairs)
        if tick >= depth:
            scalars = scalars_of(tick - LAG * (2 * (sections - 1) - section))
            rising, grads = run_backward(
                scalars, patches, up.pop(tick - LAG, nothing), leaving, seen, tables, grads
            )
            pairs = pairs_of(tick, -1)
            if pairs:
                up[tick] = lax.ppermute(rising, "depth", pairs)

    flat = grads.reshape((-1,) + stack[1:])
    keep, send = deposit(flat, corners, lat, owners, 2 * half, width)
    halved = keep + swap(send, "lat")
    if owners == 2:
        probe = lax.axis_index("probe")
        mine = lax.dynamic_index_in_dim(halved, probe, 2, keepdims=False)
        theirs = lax.dynamic_index_in_dim(halved, 1 - probe, 2, keepdims=False)
        return mine + swap(theirs, "probe")
    return lax.psum_scatter(halved, "probe", scatter_dimension=2, tiled=False)


def solution(mesh):
    return jax.shard_map(
        local,
        mesh=mesh,
        in_specs=(
            P(None, ("groups", "depth"), "lat", None),
            P(),
            P("groups", None),
            P("groups", ("probe", "lat")),
            P("groups", ("probe", "lat"), None, None),
        ),
        out_specs=P(None, ("groups", "depth"), ("probe", "lat"), None),
        check_vma=False,
    )
```

time: 1110 us -> 382 us (0.34); the launches traced: 1090 us -> 380 us
  loops' own time: 206 us -> 0 us
  local copies, waits for them, and re-layouts: 320 us -> 149 us
  matrix products: 141 us -> 0 us
  waiting for transfers between devices: 215 us -> 110 us
  other arithmetic: 76.1 us -> 9.11 us
  starting transfers between devices: 119 us -> 54.8 us
  Pallas kernels: 0 us -> 56.4 us
  between operations: 13.5 us -> 0.83 us
    another operation x42 -> x0, loops' own time: 206 us -> none  [the longest x1 69.8 us: local(): lax.fori_loop(0, tick_count, forward_tick, (arrived, stored, exit_waves))]
    dot_general x512 -> x0, matrix products: 141 us -> none  [the longest x128 35.5 us: complex_apply(): jnp.einsum(pattern, mat_imag, wave_imag, precision=PRECISE)]
    unnamed x8 -> x149, local copies, waits for them, and re-layouts: 7.5 us -> 144 us
    dynamic_update_slice x92 -> x0, local copies, waits for them, and re-layouts: 102 us -> none  [the longest x16 69.4 us: add_one(): lax.dynamic_update_slice(buffer_now, region + patch_grads[index_probe], s...]
    reduce_scatter x1 -> x0, waiting for transfers between devices: 78.5 us -> none  [local(): lax.psum_scatter(running, ('probe', 'lat'), scatter_dimension=2, tiled=True)]
    gather x33 -> x1, local copies, waits for them, and re-layouts: 77.1 us -> 0.56 us  [local(): corners = positions[scan_index.reshape(-1)]]
    ppermute x38 -> x23, starting transfers between devices: 119 us -> 54.8 us  [the longest x10 36.8 us: local(): down[tick] = lax.ppermute(leaving, 'depth', pairs)]
    pallas_call x0 -> x24, Pallas kernels: none -> 56.4 us  [the longest x11 22.2 us: run_backward(): pl.pallas_call(backward_kernel, grid_spec=pltpu.PrefetchScalarGridSpec(nu...]
  transfers between devices with their start and end apart: 40 -> 23, of which waited for: 39 -> 11; matrix products, arithmetic and copies ran while one was open for 10% -> 1% of each run, Pallas kernels for 0% -> 6%
where the time goes in v1:
time: 382 us; the launch traced here: 380 us
  local copies, waits for them, and re-layouts  149 us (39%)
  waiting for transfers between devices  110 us (29%)
  Pallas kernels  56.4 us (15%)
  starting transfers between devices  54.8 us (14%)
  other arithmetic  9.11 us (2%)
    unnamed x149, local copies, waits for them, and re-layouts  144 us
    ppermute x3, waiting for transfers between devices, swap(): return lax.ppermute(shard, axis, [(0, 1), (1, 0)])  65.7 us
    ppermute x10, starting transfers between devices, local(): down[tick] = lax.ppermute(leaving, 'depth', pairs)  36.8 us
    ppermute x10, waiting for transfers between devices, local(): up[tick] = lax.ppermute(rising, 'depth', pairs)  31.8 us
    pallas_call x11, Pallas kernels, run_backward(): pl.pallas_call(backward_kernel, grid_spec=pltpu.PrefetchScalarGridSpec(nu...  22.2 us
    pallas_call x11, Pallas kernels, run_forward(): pl.pallas_call(forward_kernel, grid_spec=pltpu.PrefetchScalarGridSpec(num...  16.6 us
    ppermute x10, waiting for transfers between devices, local(): down[tick] = lax.ppermute(leaving, 'depth', pairs)  12.6 us
    ppermute x10, starting transfers between devices, local(): up[tick] = lax.ppermute(rising, 'depth', pairs)  11.6 us
  transfers between devices with their start and end apart: 23, of which 11 were waited for; matrix products, arithmetic and copies ran while one was open for 1% of the time, Pallas kernels for 6%

profile of v1, /device:TPU:0, one launch (start us, length us, event | category | flops | bytes accessed | tf_op | source)
XLA Modules:
  0.0 380.3 jit_solution(2352913480005350447)
XLA Ops:
  2.7 5.6 %collective-permute-done.other = f32[2,2,384,768]{3,2,1,0:T(8,128)} collective-permute-done((f32[2,2,384,768]{3,2,1,0:T(8,128)}, f32[2,2,384,768]{3,2,1,0:T(8,128)}, u32[]{:S(2)}, u32[]{:S(2)}) %collective-permute-start) | collective-permute-done | bytes 4718624 | tf_op jit(solution)/shard_map/ppermute | solution.py:391
  8.3 2.3 copy-done.72
  10.7 11.1 %cut_patches.1 = f32[16,2,2,128,128]{4,3,2,1,0:T(8,128)S(1)} custom-call(s32[32]{0:T(128)S(1)} %reshape.18.corners, s32[1]{0:T(128)} %bitcast.1.lat, f32[2,2,384,768]{3,2,1,0:T(8,128)S(1)} %copy-done.72, f32[2,2,384,768]{3,2,1,0:T(8,128)} %collective-permute-done.other), custom_call_target="tpu_custom_call" | custom-call | flops 4194304 | bytes 12582912 | tf_op jit(solution)/shard_map/cut_patches/pallas_call | solution.py:152
  28.9 3.5 collective-permute-start.1
  32.5 4.9 %collective-permute-done.1.arrived = f32[2,2,128,128]{3,2,1,0:T(8,128)S(1)} collective-permute-done((f32[2,2,128,128]{3,2,1,0:T(8,128)S(1)}, f32[2,2,128,128]{3,2,1,0:T(8,128)S(1)}, u32[]{:S(2)}, u32[]{:S(2)}) %collective-permute-start.1) | collective-permute-done | bytes 262176 | tf_op jit(solution)/shard_map/ppermute | solution.py:444
  37.4 2.3 copy-done.1
  46.0 4.4 %collective-permute-start.2 = (f32[2,2,128,128]{3,2,1,0:T(8,128)S(1)}, f32[2,2,128,128]{3,2,1,0:T(8,128)S(1)}, u32[]{:S(2)}, u32[]{:S(2)}) collective-permute-start(f32[2,2,128,128]{3,2,1,0:T(8,128)S(1)} %get-tuple-element.52), channel_id=1, source_target_pairs={{0,4},{4,8},{1,5},{5,9},{2,6},{6,10},{3,7},{7,11},{16,20},{20,24},... | collective-permute-start | bytes 786440 | tf_op jit(solution)/shard_map/ppermute | solution.py:444
  50.5 4.0 %collective-permute-done.2.arrived = f32[2,2,128,128]{3,2,1,0:T(8,128)S(1)} collective-permute-done((f32[2,2,128,128]{3,2,1,0:T(8,128)S(1)}, f32[2,2,128,128]{3,2,1,0:T(8,128)S(1)}, u32[]{:S(2)}, u32[]{:S(2)}) %collective-permute-start.2) | collective-permute-done | bytes 262176 | tf_op jit(solution)/shard_map/ppermute | solution.py:444
  54.5 2.3 copy-done.3
  63.1 4.4 %collective-permute-start.3 = (f32[2,2,128,128]{3,2,1,0:T(8,128)S(1)}, f32[2,2,128,128]{3,2,1,0:T(8,128)S(1)}, u32[]{:S(2)}, u32[]{:S(2)}) collective-permute-start(f32[2,2,128,128]{3,2,1,0:T(8,128)S(1)} %get-tuple-element.54), channel_id=1, source_target_pairs={{0,4},{4,8},{8,12},{1,5},{5,9},{9,13},{2,6},{6,10},{10,14},{3,7},{... | collective-permute-start | bytes 786440 | tf_op jit(solution)/shard_map/ppermute | solution.py:444
  67.7 3.7 collective-permute-done.3.arrived
  71.4 2.3 copy-done.5
  79.9 4.7 %collective-permute-start.5 = (f32[2,2,128,128]{3,2,1,0:T(8,128)S(1)}, f32[2,2,128,128]{3,2,1,0:T(8,128)S(1)}, u32[]{:S(2)}, u32[]{:S(2)}) collective-permute-start(f32[2,2,128,128]{3,2,1,0:T(8,128)S(1)} %get-tuple-element.56.own), channel_id=1, source_target_pairs={{0,4},{4,8},{8,12},{1,5},{5,9},{9,13},{2,6},{6,10},{10,14},{3,7},{... | collective-permute-start | bytes 786440 | tf_op jit(solution)/shard_map/ppermute | solution.py:444
  89.5 2.3 copy-done.8
  98.1 3.3 collective-permute-start.7
  108.2 2.3 copy-done.11
  116.7 2.8 collective-permute-start.9
  126.9 2.3 copy-done.14
  135.5 7.6 %collective-permute-start.11 = (f32[2,2,128,128]{3,2,1,0:T(8,128)S(1)}, f32[2,2,128,128]{3,2,1,0:T(8,128)S(1)}, u32[]{:S(2)}, u32[]{:S(2)}) collective-permute-start(f32[2,2,128,128]{3,2,1,0:T(8,128)S(1)} %get-tuple-element.67.own), channel_id=1, source_target_pairs={{0,4},{4,8},{8,12},{1,5},{5,9},{9,13},{2,6},{6,10},{10,14},{3,7},{... | collective-permute-start | bytes 786440 | tf_op jit(solution)/shard_map/ppermute | solution.py:444
  145.4 2.5 backward_section.14
  151.7 2.3 copy-done.17
  160.2 4.5 %collective-permute-start.13 = (f32[2,2,128,128]{3,2,1,0:T(8,128)S(1)}, f32[2,2,128,128]{3,2,1,0:T(8,128)S(1)}, u32[]{:S(2)}, u32[]{:S(2)}) collective-permute-start(f32[2,2,128,128]{3,2,1,0:T(8,128)S(1)} %get-tuple-element.71.own), channel_id=1, source_target_pairs={{0,4},{4,8},{8,12},{1,5},{5,9},{9,13},{2,6},{6,10},{10,14},{3,7},{... | collective-permute-start | bytes 786440 | tf_op jit(solution)/shard_map/ppermute | solution.py:444
  167.2 2.7 backward_section.15
  173.6 2.3 copy-done.20
  178.7 2.4 copy-done.21
  184.5 2.5 backward_section.16
  190.7 2.3 copy-done.23
  195.8 2.4 copy-done.24
  199.0 3.3 collective-permute-done.14.arrived
  202.3 2.3 copy-done.25
  204.7 2.5 backward_section.17
  210.9 2.3 copy-done.26
  216.0 2.4 copy-done.27
  220.1 2.3 copy-done.28
  227.9 10.9 %collective-permute-done.18.arrived = f32[2,2,128,128]{3,2,1,0:T(8,128)S(1)} collective-permute-done((f32[2,2,128,128]{3,2,1,0:T(8,128)S(1)}, f32[2,2,128,128]{3,2,1,0:T(8,128)S(1)}, u32[]{:S(2)}, u32[]{:S(2)}) %collective-permute-start.18) | collective-permute-done | bytes 262176 | tf_op jit(solution)/shard_map/ppermute | solution.py:452
  238.8 2.3 copy-done.29
  251.1 9.1 %collective-permute-done.19.arrived = f32[2,2,128,128]{3,2,1,0:T(8,128)S(1)} collective-permute-done((f32[2,2,128,128]{3,2,1,0:T(8,128)S(1)}, f32[2,2,128,128]{3,2,1,0:T(8,128)S(1)}, u32[]{:S(2)}, u32[]{:S(2)}) %collective-permute-start.19) | collective-permute-done | bytes 262176 | tf_op jit(solution)/shard_map/ppermute | solution.py:452
  260.2 2.3 copy-done.30
  264.7 2.3 copy-done.64
  272.5 6.9 %collective-permute-done.20.arrived = f32[2,2,128,128]{3,2,1,0:T(8,128)S(1)} collective-permute-done((f32[2,2,128,128]{3,2,1,0:T(8,128)S(1)}, f32[2,2,128,128]{3,2,1,0:T(8,128)S(1)}, u32[]{:S(2)}, u32[]{:S(2)}) %collective-permute-start.20) | collective-permute-done | bytes 262176 | tf_op jit(solution)/shard_map/ppermute | solution.py:452
  279.4 2.3 copy-done.31
  286.2 2.5 backward_section.21
  293.3 6.6 %deposit_patches.1 = (f32[2,2,2,192,768]{4,3,2,1,0:T(8,128)S(1)}, f32[2,2,2,192,768]{4,3,2,1,0:T(8,128)}) custom-call(s32[32]{0:T(128)S(1)} %reshape.18.corners, s32[1]{0:T(128)} %bitcast.1.lat, f32[18,2,2,128,128]{4,3,2,1,0:T(8,128)S(1)} %bitcast.100), custom_call_target="tpu_custom_call" | custom-call | flops 8388608 | bytes 14155776 | tf_op jit(solution)/shard_map/deposit_patches/pallas_call | solution.py:365
  302.1 8.2 %collective-permute-done.21 = f32[2,2,2,192,768]{4,3,2,1,0:T(8,128)} collective-permute-done((f32[2,2,2,192,768]{4,3,2,1,0:T(8,128)}, f32[2,2,2,192,768]{4,3,2,1,0:T(8,128)}, u32[]{:S(2)}, u32[]{:S(2)}) %collective-permute-start.21) | collective-permute-done | bytes 4718624 | tf_op jit(solution)/shard_map/ppermute | solution.py:391
  310.3 4.4 %add.19 = f32[2,2,2,192,768]{4,3,2,1,0:T(8,128)S(1)} add(f32[2,2,2,192,768]{4,3,2,1,0:T(8,128)} %copy-done.71, f32[2,2,2,192,768]{4,3,2,1,0:T(8,128)} %collective-permute-done.21) | non-fusion elementwise | flops 1179648 | bytes 14155776 | tf_op jit(solution)/shard_map/add | solution.py:456
  318.5 5.9 %collective-permute-start.22 = (f32[2,2,192,768]{3,2,1,0:T(8,128)}, f32[2,2,192,768]{3,2,1,0:T(8,128)}, u32[]{:S(2)}, u32[]{:S(2)}) collective-permute-start(f32[2,2,192,768]{3,2,1,0:T(8,128)} %dynamic-slice_bitcast_fusion), channel_id=1, source_target_pairs={{0,2},{2,0},{1,3},{3,1},{4,6},{6,4},{5,7},{7,5},{8,10},{10,8},{9,1... | collective-permute-start | bytes 7077896 | tf_op jit(solution)/shard_map/ppermute | solution.py:391
  324.4 51.9 %collective-permute-done.22 = f32[2,2,192,768]{3,2,1,0:T(8,128)} collective-permute-done((f32[2,2,192,768]{3,2,1,0:T(8,128)}, f32[2,2,192,768]{3,2,1,0:T(8,128)}, u32[]{:S(2)}, u32[]{:S(2)}) %collective-permute-start.22) | collective-permute-done | bytes 2359328 | tf_op jit(solution)/shard_map/ppermute | solution.py:391
  376.3 4.1 %bitcast_add_fusion = f32[2,2,192,768]{3,2,1,0:T(8,128)} fusion(f32[2,2,192,768]{3,2,1,0:T(8,128)} %collective-permute-done.22, f32[2,2,2,192,768]{4,3,2,1,0:T(8,128)} %copy-done.73, s32[]{:T(128)S(6)} %select_n.101), kind=kLoop, calls=%fused_computation.1 | loop fusion | flops 589824 | bytes 7077892 | tf_op jit(solution)/shard_map/add | solution.py:461
  (203 shorter events, 144.1 us)
Async XLA Ops:
  0.0 8.3 %collective-permute-start = (f32[2,2,384,768]{3,2,1,0:T(8,128)}, f32[2,2,384,768]{3,2,1,0:T(8,128)}, u32[]{:S(2)}, u32[]{:S(2)}) collective-permute-start(f32[2,2,384,768]{3,2,1,0:T(8,128)} %own.1), channel_id=1, source_target_pairs={{0,1},{1,0},{2,3},{3,2},{4,5},{5,4},{6,7},{7,6},{8,9},{9,8},{10,11... | collective-permute-start | bytes 14155784 | tf_op jit(solution)/shard_map/ppermute | solution.py:391
  21.8 5.0 %copy-start.32 = (f32[16,2,2,128,128]{4,3,2,1,0:T(8,128)}, f32[16,2,2,128,128]{4,3,2,1,0:T(8,128)S(1)}, u32[]{:S(2)}) copy-start(f32[16,2,2,128,128]{4,3,2,1,0:T(8,128)S(1)} %cut_patches.1) | copy-start | bytes 12582916
  21.8 3.0 copy-start.69
  21.8 3.0 copy-start.70
  28.9 8.5 %collective-permute-start.1 = (f32[2,2,128,128]{3,2,1,0:T(8,128)S(1)}, f32[2,2,128,128]{3,2,1,0:T(8,128)S(1)}, u32[]{:S(2)}, u32[]{:S(2)}) collective-permute-start(f32[2,2,128,128]{3,2,1,0:T(8,128)S(1)} %get-tuple-element.50), channel_id=1, source_target_pairs={{0,4},{1,5},{2,6},{3,7},{16,20},{17,21},{18,22},{19,23}} | collective-permute-start | bytes 786440 | tf_op jit(solution)/shard_map/ppermute | solution.py:444
  46.0 8.5 %collective-permute-start.2 = (f32[2,2,128,128]{3,2,1,0:T(8,128)S(1)}, f32[2,2,128,128]{3,2,1,0:T(8,128)S(1)}, u32[]{:S(2)}, u32[]{:S(2)}) collective-permute-start(f32[2,2,128,128]{3,2,1,0:T(8,128)S(1)} %get-tuple-element.52), channel_id=1, source_target_pairs={{0,4},{4,8},{1,5},{5,9},{2,6},{6,10},{3,7},{7,11},{16,20},{20,24},... | collective-permute-start | bytes 786440 | tf_op jit(solution)/shard_map/ppermute | solution.py:444
  63.1 8.3 %collective-permute-start.3 = (f32[2,2,128,128]{3,2,1,0:T(8,128)S(1)}, f32[2,2,128,128]{3,2,1,0:T(8,128)S(1)}, u32[]{:S(2)}, u32[]{:S(2)}) collective-permute-start(f32[2,2,128,128]{3,2,1,0:T(8,128)S(1)} %get-tuple-element.54), channel_id=1, source_target_pairs={{0,4},{4,8},{8,12},{1,5},{5,9},{9,13},{2,6},{6,10},{10,14},{3,7},{... | collective-permute-start | bytes 786440 | tf_op jit(solution)/shard_map/ppermute | solution.py:444
  79.9 5.2 %copy-start.7 = (f32[9,2,2,2,128,128]{5,4,3,2,1,0:T(8,128)S(1)}, f32[9,2,2,2,128,128]{5,4,3,2,1,0:T(8,128)}, u32[]{:S(2)}) copy-start(f32[9,2,2,2,128,128]{5,4,3,2,1,0:T(8,128)} %copy-done.6) | copy-start | bytes 14155780
  79.9 9.6 %collective-permute-start.5 = (f32[2,2,128,128]{3,2,1,0:T(8,128)S(1)}, f32[2,2,128,128]{3,2,1,0:T(8,128)S(1)}, u32[]{:S(2)}, u32[]{:S(2)}) collective-permute-start(f32[2,2,128,128]{3,2,1,0:T(8,128)S(1)} %get-tuple-element.56.own), channel_id=1, source_target_pairs={{0,4},{4,8},{8,12},{1,5},{5,9},{9,13},{2,6},{6,10},{10,14},{3,7},{... | collective-permute-start | bytes 786440 | tf_op jit(solution)/shard_map/ppermute | solution.py:444
  88.7 12.8 %collective-permute-start.4 = (f32[2,2,128,128]{3,2,1,0:T(8,128)}, f32[2,2,128,128]{3,2,1,0:T(8,128)S(1)}, u32[]{:S(2)}, u32[]{:S(2)}) collective-permute-start(f32[2,2,128,128]{3,2,1,0:T(8,128)} %get-tuple-element.58), channel_id=1, source_target_pairs={{12,8},{13,9},{14,10},{15,11},{28,24},{29,25},{30,26},{31,27}} | collective-permute-start | bytes 786440 | tf_op jit(solution)/shard_map/ppermute | solution.py:452
  89.5 2.3 copy-start.8
  94.1 7.4 %copy-start.48 = (f32[9,2,2,2,128,128]{5,4,3,2,1,0:T(8,128)S(1)}, f32[9,2,2,2,128,128]{5,4,3,2,1,0:T(8,128)}, u32[]{:S(2)}) copy-start(f32[9,2,2,2,128,128]{5,4,3,2,1,0:T(8,128)} %copy-done.47) | copy-start | bytes 14155780
  98.1 10.0 %collective-permute-start.7 = (f32[2,2,128,128]{3,2,1,0:T(8,128)S(1)}, f32[2,2,128,128]{3,2,1,0:T(8,128)S(1)}, u32[]{:S(2)}, u32[]{:S(2)}) collective-permute-start(f32[2,2,128,128]{3,2,1,0:T(8,128)S(1)} %get-tuple-element.59.own), channel_id=1, source_target_pairs={{0,4},{4,8},{8,12},{1,5},{5,9},{9,13},{2,6},{6,10},{10,14},{3,7},{... | collective-permute-start | bytes 786440 | tf_op jit(solution)/shard_map/ppermute | solution.py:444
  101.5 2.3 copy-start.10
  107.3 12.3 %collective-permute-start.6 = (f32[2,2,128,128]{3,2,1,0:T(8,128)}, f32[2,2,128,128]{3,2,1,0:T(8,128)S(1)}, u32[]{:S(2)}, u32[]{:S(2)}) collective-permute-start(f32[2,2,128,128]{3,2,1,0:T(8,128)} %get-tuple-element.62), channel_id=1, source_target_pairs={{8,4},{12,8},{9,5},{13,9},{10,6},{14,10},{11,7},{15,11},{24,20},{2... | collective-permute-start | bytes 786440 | tf_op jit(solution)/shard_map/ppermute | solution.py:452
  108.2 2.3 copy-start.11
  112.7 6.9 %copy-start.50 = (f32[9,2,2,2,128,128]{5,4,3,2,1,0:T(8,128)S(1)}, f32[9,2,2,2,128,128]{5,4,3,2,1,0:T(8,128)}, u32[]{:S(2)}) copy-start(f32[9,2,2,2,128,128]{5,4,3,2,1,0:T(8,128)} %copy-done.49) | copy-start | bytes 14155780
  116.7 10.1 %collective-permute-start.9 = (f32[2,2,128,128]{3,2,1,0:T(8,128)S(1)}, f32[2,2,128,128]{3,2,1,0:T(8,128)S(1)}, u32[]{:S(2)}, u32[]{:S(2)}) collective-permute-start(f32[2,2,128,128]{3,2,1,0:T(8,128)S(1)} %get-tuple-element.63.own), channel_id=1, source_target_pairs={{0,4},{4,8},{8,12},{1,5},{5,9},{9,13},{2,6},{6,10},{10,14},{3,7},{... | collective-permute-start | bytes 786440 | tf_op jit(solution)/shard_map/ppermute | solution.py:444
  119.6 2.3 copy-start.13
  125.4 17.7 %collective-permute-start.8 = (f32[2,2,128,128]{3,2,1,0:T(8,128)}, f32[2,2,128,128]{3,2,1,0:T(8,128)S(1)}, u32[]{:S(2)}, u32[]{:S(2)}) collective-permute-start(f32[2,2,128,128]{3,2,1,0:T(8,128)} %get-tuple-element.66), channel_id=1, source_target_pairs={{4,0},{8,4},{12,8},{5,1},{9,5},{13,9},{6,2},{10,6},{14,10},{7,3},{... | collective-permute-start | bytes 786440 | tf_op jit(solution)/shard_map/ppermute | solution.py:452
  126.9 2.3 copy-start.14
  131.4 11.7 %copy-start.52 = (f32[9,2,2,2,128,128]{5,4,3,2,1,0:T(8,128)S(1)}, f32[9,2,2,2,128,128]{5,4,3,2,1,0:T(8,128)}, u32[]{:S(2)}) copy-start(f32[9,2,2,2,128,128]{5,4,3,2,1,0:T(8,128)} %copy-done.51) | copy-start | bytes 14155780
  135.5 16.2 %collective-permute-start.11 = (f32[2,2,128,128]{3,2,1,0:T(8,128)S(1)}, f32[2,2,128,128]{3,2,1,0:T(8,128)S(1)}, u32[]{:S(2)}, u32[]{:S(2)}) collective-permute-start(f32[2,2,128,128]{3,2,1,0:T(8,128)S(1)} %get-tuple-element.67.own), channel_id=1, source_target_pairs={{0,4},{4,8},{8,12},{1,5},{5,9},{9,13},{2,6},{6,10},{10,14},{3,7},{... | collective-permute-start | bytes 786440 | tf_op jit(solution)/shard_map/ppermute | solution.py:444
  143.1 2.3 copy-start.16
  150.2 14.6 %collective-permute-start.10 = (f32[2,2,128,128]{3,2,1,0:T(8,128)}, f32[2,2,128,128]{3,2,1,0:T(8,128)S(1)}, u32[]{:S(2)}, u32[]{:S(2)}) collective-permute-start(f32[2,2,128,128]{3,2,1,0:T(8,128)} %get-tuple-element.70), channel_id=1, source_target_pairs={{4,0},{8,4},{12,8},{5,1},{9,5},{13,9},{6,2},{10,6},{14,10},{7,3},{... | collective-permute-start | bytes 786440 | tf_op jit(solution)/shard_map/ppermute | solution.py:452
  151.7 2.3 copy-start.17
  156.2 8.6 %copy-start.54 = (f32[9,2,2,2,128,128]{5,4,3,2,1,0:T(8,128)S(1)}, f32[9,2,2,2,128,128]{5,4,3,2,1,0:T(8,128)}, u32[]{:S(2)}) copy-start(f32[9,2,2,2,128,128]{5,4,3,2,1,0:T(8,128)} %copy-done.53) | copy-start | bytes 14155780
  160.2 13.3 %collective-permute-start.13 = (f32[2,2,128,128]{3,2,1,0:T(8,128)S(1)}, f32[2,2,128,128]{3,2,1,0:T(8,128)S(1)}, u32[]{:S(2)}, u32[]{:S(2)}) collective-permute-start(f32[2,2,128,128]{3,2,1,0:T(8,128)S(1)} %get-tuple-element.71.own), channel_id=1, source_target_pairs={{0,4},{4,8},{8,12},{1,5},{5,9},{9,13},{2,6},{6,10},{10,14},{3,7},{... | collective-permute-start | bytes 786440 | tf_op jit(solution)/shard_map/ppermute | solution.py:444
  164.8 2.3 copy-start.19
  172.1 9.8 %collective-permute-start.12 = (f32[2,2,128,128]{3,2,1,0:T(8,128)}, f32[2,2,128,128]{3,2,1,0:T(8,128)S(1)}, u32[]{:S(2)}, u32[]{:S(2)}) collective-permute-start(f32[2,2,128,128]{3,2,1,0:T(8,128)} %get-tuple-element.74), channel_id=1, source_target_pairs={{4,0},{8,4},{12,8},{5,1},{9,5},{13,9},{6,2},{10,6},{14,10},{7,3},{... | collective-permute-start | bytes 786440 | tf_op jit(solution)/shard_map/ppermute | solution.py:452
  173.6 2.3 copy-start.20
  178.1 4.0 %copy-start.56 = (f32[9,2,2,2,128,128]{5,4,3,2,1,0:T(8,128)S(1)}, f32[9,2,2,2,128,128]{5,4,3,2,1,0:T(8,128)}, u32[]{:S(2)}) copy-start(f32[9,2,2,2,128,128]{5,4,3,2,1,0:T(8,128)} %copy-done.55) | copy-start | bytes 14155780
  178.7 2.4 copy-start.21
  181.1 9.7 %collective-permute-start.15 = (f32[2,2,128,128]{3,2,1,0:T(8,128)S(1)}, f32[2,2,128,128]{3,2,1,0:T(8,128)S(1)}, u32[]{:S(2)}, u32[]{:S(2)}) collective-permute-start(f32[2,2,128,128]{3,2,1,0:T(8,128)S(1)} %get-tuple-element.75.own), channel_id=1, source_target_pairs={{4,8},{8,12},{5,9},{9,13},{6,10},{10,14},{7,11},{11,15},{20,24},{2... | collective-permute-start | bytes 786440 | tf_op jit(solution)/shard_map/ppermute | solution.py:444
  189.3 13.1 %collective-permute-start.14 = (f32[2,2,128,128]{3,2,1,0:T(8,128)}, f32[2,2,128,128]{3,2,1,0:T(8,128)S(1)}, u32[]{:S(2)}, u32[]{:S(2)}) collective-permute-start(f32[2,2,128,128]{3,2,1,0:T(8,128)} %get-tuple-element.78), channel_id=1, source_target_pairs={{4,0},{8,4},{12,8},{5,1},{9,5},{13,9},{6,2},{10,6},{14,10},{7,3},{... | collective-permute-start | bytes 786440 | tf_op jit(solution)/shard_map/ppermute | solution.py:452
  190.7 2.3 copy-start.23
  195.3 7.1 %copy-start.58 = (f32[9,2,2,2,128,128]{5,4,3,2,1,0:T(8,128)S(1)}, f32[9,2,2,2,128,128]{5,4,3,2,1,0:T(8,128)}, u32[]{:S(2)}) copy-start(f32[9,2,2,2,128,128]{5,4,3,2,1,0:T(8,128)} %copy-done.57) | copy-start | bytes 14155780
  195.8 2.4 copy-start.24
  198.2 12.7 %collective-permute-start.17 = (f32[2,2,128,128]{3,2,1,0:T(8,128)S(1)}, f32[2,2,128,128]{3,2,1,0:T(8,128)S(1)}, u32[]{:S(2)}, u32[]{:S(2)}) collective-permute-start(f32[2,2,128,128]{3,2,1,0:T(8,128)S(1)} %get-tuple-element.79.own), channel_id=1, source_target_pairs={{8,12},{9,13},{10,14},{11,15},{24,28},{25,29},{26,30},{27,31}} | collective-permute-start | bytes 786440 | tf_op jit(solution)/shard_map/ppermute | solution.py:444
  209.5 10.7 %collective-permute-start.16 = (f32[2,2,128,128]{3,2,1,0:T(8,128)}, f32[2,2,128,128]{3,2,1,0:T(8,128)S(1)}, u32[]{:S(2)}, u32[]{:S(2)}) collective-permute-start(f32[2,2,128,128]{3,2,1,0:T(8,128)} %get-tuple-element.82), channel_id=1, source_target_pairs={{4,0},{8,4},{12,8},{5,1},{9,5},{13,9},{6,2},{10,6},{14,10},{7,3},{... | collective-permute-start | bytes 786440 | tf_op jit(solution)/shard_map/ppermute | solution.py:452
  210.9 2.3 copy-start.26
  215.5 4.7 %copy-start.60 = (f32[9,2,2,2,128,128]{5,4,3,2,1,0:T(8,128)S(1)}, f32[9,2,2,2,128,128]{5,4,3,2,1,0:T(8,128)}, u32[]{:S(2)}) copy-start(f32[9,2,2,2,128,128]{5,4,3,2,1,0:T(8,128)} %copy-done.59) | copy-start | bytes 14155780
  216.0 2.4 copy-start.27
  226.5 12.2 %collective-permute-start.18 = (f32[2,2,128,128]{3,2,1,0:T(8,128)S(1)}, f32[2,2,128,128]{3,2,1,0:T(8,128)S(1)}, u32[]{:S(2)}, u32[]{:S(2)}) collective-permute-start(f32[2,2,128,128]{3,2,1,0:T(8,128)S(1)} %get-tuple-element.86), channel_id=1, source_target_pairs={{4,0},{8,4},{12,8},{5,1},{9,5},{13,9},{6,2},{10,6},{14,10},{7,3},{... | collective-permute-start | bytes 786440 | tf_op jit(solution)/shard_map/ppermute | solution.py:452
  249.7 10.5 %collective-permute-start.19 = (f32[2,2,128,128]{3,2,1,0:T(8,128)S(1)}, f32[2,2,128,128]{3,2,1,0:T(8,128)S(1)}, u32[]{:S(2)}, u32[]{:S(2)}) collective-permute-start(f32[2,2,128,128]{3,2,1,0:T(8,128)S(1)} %get-tuple-element.88), channel_id=1, source_target_pairs={{4,0},{8,4},{5,1},{9,5},{6,2},{10,6},{7,3},{11,7},{20,16},{24,20},... | collective-permute-start | bytes 786440 | tf_op jit(solution)/shard_map/ppermute | solution.py:452
  271.1 8.3 %collective-permute-start.20 = (f32[2,2,128,128]{3,2,1,0:T(8,128)S(1)}, f32[2,2,128,128]{3,2,1,0:T(8,128)S(1)}, u32[]{:S(2)}, u32[]{:S(2)}) collective-permute-start(f32[2,2,128,128]{3,2,1,0:T(8,128)S(1)} %get-tuple-element.90), channel_id=1, source_target_pairs={{4,0},{5,1},{6,2},{7,3},{20,16},{21,17},{22,18},{23,19}} | collective-permute-start | bytes 786440 | tf_op jit(solution)/shard_map/ppermute | solution.py:452
  302.1 8.3 %collective-permute-start.21 = (f32[2,2,2,192,768]{4,3,2,1,0:T(8,128)}, f32[2,2,2,192,768]{4,3,2,1,0:T(8,128)}, u32[]{:S(2)}, u32[]{:S(2)}) collective-permute-start(f32[2,2,2,192,768]{4,3,2,1,0:T(8,128)} %get-tuple-element.94), channel_id=1, source_target_pairs={{0,1},{1,0},{2,3},{3,2},{4,5},{5,4},{6,7},{7,6},{8,9},{9,8},{10,11... | collective-permute-start | bytes 14155784 | tf_op jit(solution)/shard_map/ppermute | solution.py:391
  318.5 57.8 %collective-permute-start.22 = (f32[2,2,192,768]{3,2,1,0:T(8,128)}, f32[2,2,192,768]{3,2,1,0:T(8,128)}, u32[]{:S(2)}, u32[]{:S(2)}) collective-permute-start(f32[2,2,192,768]{3,2,1,0:T(8,128)} %dynamic-slice_bitcast_fusion), channel_id=1, source_target_pairs={{0,2},{2,0},{1,3},{3,1},{4,6},{6,4},{5,7},{7,5},{8,10},{10,8},{9,1... | collective-permute-start | bytes 7077896 | tf_op jit(solution)/shard_map/ppermute | solution.py:391
  (49 other events, 109.5 us)

commit v2 on v1

v2 whole, which is shorter than its diff:
```python
import functools
import math

import jax
import jax.numpy as jnp
import ml_dtypes
import numpy as np
from jax import lax
from jax.experimental import pallas as pl
from jax.experimental.pallas import tpu as pltpu
from jax.sharding import PartitionSpec as P

FRESNEL = 8.0
LAG = 1
SCOPED = 16 << 20
F32 = jnp.float32
BF16 = jnp.bfloat16
HBM = pl.BlockSpec(memory_space=pl.ANY)
VMEM = pl.BlockSpec(memory_space=pltpu.VMEM)
SMEM = pl.BlockSpec(memory_space=pltpu.SMEM)


def in_hbm(x):
    return pltpu.with_memory_space_constraint(x, pltpu.HBM)


def in_vmem(x):
    return pltpu.with_memory_space_constraint(x, pltpu.VMEM)


def real_blocks(matrix):
    real, imag = matrix.real, matrix.imag
    left = np.block([[real, -imag], [imag, real]])
    right = np.block([[real, imag], [-imag, real]])
    return np.stack([left, right])


@functools.lru_cache(maxsize=None)
def make_tables(pixels):
    index = np.arange(pixels)
    freq = np.where(index < pixels // 2, index, index - pixels) / pixels
    spread = index[:, None] - index[None, :]
    phase = 2.0 * math.pi * freq * spread[:, :, None] - math.pi * FRESNEL * freq * freq
    propagator = np.mean(np.exp(1j * phase), axis=-1)
    turns = index[:, None] * index[None, :] % pixels
    fourier = np.exp(-2j * math.pi * turns / pixels) / math.sqrt(pixels)
    blocks = np.stack([real_blocks(propagator), real_blocks(fourier)]).astype(np.float32)
    high = blocks.astype(ml_dtypes.bfloat16)
    low = (blocks - high.astype(np.float32)).astype(ml_dtypes.bfloat16)
    return np.stack([high, low], axis=2)


def halves(x):
    high = x.astype(BF16)
    return high, (x - high.astype(F32)).astype(BF16)


def dot(a, b):
    return jnp.dot(a, b, preferred_element_type=F32)


def transform(left, right, fields):
    size = fields[0][0].shape[0]
    stacked = jnp.concatenate(
        [
            jnp.concatenate([real for real, _ in fields], axis=1),
            jnp.concatenate([imag for _, imag in fields], axis=1),
        ],
        axis=0,
    )
    high, low = halves(stacked)
    mid = dot(left[0], high) + (dot(left[1], high) + dot(left[0], low))
    rows = jnp.concatenate(
        [
            jnp.concatenate(
                [mid[:size, i * size : (i + 1) * size], mid[size:, i * size : (i + 1) * size]], axis=1
            )
            for i in range(len(fields))
        ],
        axis=0,
    )
    high, low = halves(rows)
    out = dot(high, right[0]) + (dot(high, right[1]) + dot(low, right[0]))
    return [
        (out[i * size : (i + 1) * size, :size], out[i * size : (i + 1) * size, size:])
        for i in range(len(fields))
    ]


def times(a, b):
    return a[0] * b[0] - a[1] * b[1], a[0] * b[1] + a[1] * b[0]


def times_conj(a, b):
    return a[0] * b[0] + a[1] * b[1], a[1] * b[0] - a[0] * b[1]


def cut_kernel(pixels, corners, lat, own, other, out, seen, window, sems):
    half = own.shape[2]
    width = own.shape[3]
    tall = pixels + 8
    step = pl.program_id(0)
    steps = pl.num_programs(0)

    def places(probe):
        row = corners[2 * probe]
        column = corners[2 * probe + 1]
        row0 = jnp.minimum(row // 8 * 8, 2 * half - tall)
        col0 = jnp.minimum(column // pixels * pixels, width - 2 * pixels)
        top = row0 < half
        bottom = row0 + tall > half
        top_from = jnp.minimum(row0, half - tall)
        bottom_from = jnp.clip(row0 - half, 0, half - tall)
        offset = jnp.where(top, row0 - top_from, tall)
        return top, bottom, top_from, bottom_from, offset, row - row0, col0, column - col0

    def copies(probe, slot, act):
        top, bottom, top_from, bottom_from, _, _, col0, _ = places(probe)
        own_top = lat[0] == 0
        col0 = pl.multiple_of(col0, pixels)
        for source, is_top, sem in ((own, own_top, 0), (other, jnp.logical_not(own_top), 1)):
            start = pl.multiple_of(jnp.where(is_top, top_from, bottom_from), 8)
            to = pl.multiple_of(jnp.where(is_top, 0, tall), 8)

            @pl.when(jnp.where(is_top, top, bottom))
            def _(source=source, start=start, to=to, sem=sem):
                act(
                    pltpu.make_async_copy(
                        source.at[:, :, pl.ds(start, tall), pl.ds(col0, 2 * pixels)],
                        window.at[slot, :, :, pl.ds(to, tall), :],
                        sems.at[slot, sem],
                    )
                )

    slot = step % 2

    @pl.when(step == 0)
    def _():
        copies(0, 0, lambda copy: copy.start())

    @pl.when(step + 1 < steps)
    def _():
        copies(step + 1, 1 - slot, lambda copy: copy.start())

    copies(step, slot, lambda copy: copy.wait())
    *_, offset, down, _, shift = places(step)
    offset = pl.multiple_of(offset, 8)
    turn = (pixels - shift) % pixels
    lane = lax.broadcasted_iota(jnp.int32, (tall, pixels), 1)
    for part in range(own.shape[0]):
        for layer in range(own.shape[1]):
            near = window[slot, part, layer, pl.ds(offset, tall), pl.ds(0, pixels)]
            far = window[slot, part, layer, pl.ds(offset, tall), pl.ds(pixels, pixels)]
            near = pltpu.roll(near, turn, 1)
            far = pltpu.roll(far, turn, 1)
            patch = jnp.where(lane < pixels - shift, near, far)
            out[step // out.shape[1], step % out.shape[1], layer, part] = pltpu.roll(patch, (tall - down) % tall, 0)[:pixels]


def cut_patches(own, other, corners, lat, pixels, count):
    probes = corners.shape[0]
    parts, layers = own.shape[:2]
    groups = probes // count
    stack = (count, layers, parts, pixels, pixels)
    return pl.pallas_call(
        functools.partial(cut_kernel, pixels),
        grid_spec=pltpu.PrefetchScalarGridSpec(
            num_scalar_prefetch=2,
            grid=(probes,),
            in_specs=[HBM, HBM],
            out_specs=[VMEM, VMEM],
            scratch_shapes=[
                pltpu.VMEM((2, parts, layers, 2 * (pixels + 8), 2 * pixels), F32),
                pltpu.SemaphoreType.DMA((2, 2)),
            ],
        ),
        out_shape=[pltpu.VMEM((groups,) + stack, F32), pltpu.VMEM((groups,) + stack, F32)],
        compiler_params=pltpu.CompilerParams(vmem_limit_bytes=16 << 20),
        cost_estimate=pl.CostEstimate(
            flops=probes * layers * parts * pixels * pixels * 4,
            bytes_accessed=probes * layers * parts * pixels * pixels * 12,
            transcendentals=0,
        ),
        name="cut_patches",
    )(corners.reshape(-1), lat.reshape(1), in_hbm(own), in_hbm(other))


def forward_kernel(scalars, patches, arrived, start_wave, frames, tables, unused, leave, seen):
    group, active, first, final = (scalars[i] for i in range(4))
    count, layers = patches.shape[1:3]

    @pl.when(active == 1)
    def _():
        wave = [
            tuple(jnp.where(first == 1, start_wave[part], arrived[i, part]) for part in range(2))
            for i in range(count)
        ]
        for layer in range(layers):
            chi = []
            for i in range(count):
                for part in range(2):
                    seen[group, i, layer, part] = wave[i][part]
                here = patches[group, i, layer, 0], patches[group, i, layer, 1]
                chi.append(times(here, wave[i]))
            at = final if layer == layers - 1 else 0
            wave = transform((tables[at, 0, 0], tables[at, 0, 1]), (tables[at, 1, 0], tables[at, 1, 1]), chi)
        for i in range(count):
            real, imag = wave[i]
            misfit = real * real + imag * imag - frames[group, i]
            factor = jnp.where(final == 1, misfit, 1.0)
            leave[i, 0] = real * factor
            leave[i, 1] = imag * factor


def backward_kernel(scalars, patches, arrived, own, seen, tables, leave, grads):
    group, active, _, final = (scalars[i] for i in range(4))
    count, layers = patches.shape[1:3]

    @pl.when(active == 1)
    def _():
        wave = [
            tuple(jnp.where(final == 1, own[i, part], arrived[i, part]) for part in range(2))
            for i in range(count)
        ]
        for layer in reversed(range(layers)):
            at = final if layer == layers - 1 else 0
            chi = transform((tables[at, 1, 0], tables[at, 1, 1]), (tables[at, 0, 0], tables[at, 0, 1]), wave)
            wave = []
            for i in range(count):
                before = seen[group, i, layer, 0], seen[group, i, layer, 1]
                here = patches[group, i, layer, 0], patches[group, i, layer, 1]
                real, imag = times_conj(chi[i], before)
                grads[i, layer, 0] = real
                grads[i, layer, 1] = imag
                wave.append(times_conj(chi[i], here))
        for i in range(count):
            leave[i, 0] = wave[i][0]
            leave[i, 1] = wave[i][1]


def cost(count, layers, pixels):
    return pl.CostEstimate(
        flops=count * layers * 2 * 3 * 8 * pixels**3,
        bytes_accessed=count * (layers * 4 + 4) * pixels * pixels * 4,
        transcendentals=0,
    )


def run_forward(scalars, patches, arrived, start_wave, frames, tables, store):
    _, count, layers, _, pixels, _ = patches.shape
    return pl.pallas_call(
        forward_kernel,
        in_specs=[SMEM] + [VMEM] * 6,
        out_specs=[VMEM] * 2,
        out_shape=[pltpu.VMEM(arrived.shape, F32), pltpu.VMEM(store.shape, F32)],
        input_output_aliases={6: 1},
        compiler_params=pltpu.CompilerParams(vmem_limit_bytes=SCOPED),
        cost_estimate=cost(count, layers, pixels),
        name="forward_section",
    )(scalars, *map(in_vmem, (patches, arrived, start_wave, frames, tables, store)))


def run_backward(scalars, patches, arrived, own, seen, tables):
    _, count, layers, _, pixels, _ = patches.shape
    return pl.pallas_call(
        backward_kernel,
        in_specs=[SMEM] + [VMEM] * 5,
        out_specs=[VMEM] * 2,
        out_shape=[pltpu.VMEM(arrived.shape, F32), pltpu.VMEM(patches.shape[1:], F32)],
        compiler_params=pltpu.CompilerParams(vmem_limit_bytes=SCOPED),
        cost_estimate=cost(count, layers, pixels),
        name="backward_section",
    )(scalars, *map(in_vmem, (patches, arrived, own, seen, tables)))


def clear_kernel(total):
    total[...] = jnp.zeros(total.shape, F32)


def blank_total(parts, layers, rows, width, pixels):
    return pl.pallas_call(
        clear_kernel,
        out_specs=VMEM,
        out_shape=pltpu.VMEM((parts, layers, rows + 2 * (pixels + 8), width), F32),
        compiler_params=pltpu.CompilerParams(vmem_limit_bytes=SCOPED),
        name="blank_total",
    )()


def deposit_kernel(height, scalars, corners, sources, unused, total):
    pixels = sources[0].shape[-1]
    tall = pixels + 8
    width = total.shape[3]
    rows = total.shape[2] - 2 * tall
    lane = lax.broadcasted_iota(jnp.int32, (tall, pixels), 1)
    blank = jnp.zeros((8, pixels), F32)
    for which, grads in enumerate(sources):
        group, active = scalars[1 + 2 * which], scalars[2 + 2 * which]
        for i in range(grads.shape[0]):
            row = corners[which, group * grads.shape[0] + i, 0]
            column = corners[which, group * grads.shape[0] + i, 1]
            row0 = jnp.minimum(row // 8 * 8, height - tall)
            col0 = jnp.minimum(column // pixels * pixels, width - 2 * pixels)
            shift = column - col0
            near_at = pl.multiple_of(col0, pixels)
            far_at = pl.multiple_of(col0 + pixels, pixels)
            start = row0 - scalars[0] + tall

            @pl.when((active == 1) & (start > 0) & (start < rows + tall))
            def _(grads=grads, i=i, start=start, down=row - row0, shift=shift, near_at=near_at, far_at=far_at):
                at = pl.ds(pl.multiple_of(start, 8), tall)
                for layer in range(total.shape[1]):
                    for part in range(2):
                        padded = jnp.concatenate([grads[i, layer, part], blank], axis=0)
                        turned = pltpu.roll(pltpu.roll(padded, down, 0), shift % pixels, 1)
                        near = jnp.where(lane >= shift, turned, 0.0)
                        far = jnp.where(lane >= shift, 0.0, turned)
                        total[part, layer, at, pl.ds(near_at, pixels)] += near
                        total[part, layer, at, pl.ds(far_at, pixels)] += far


def deposit(scalars, corners, sources, total, height):
    n = len(sources)

    def body(scalars, corners, *refs):
        deposit_kernel(height, scalars, corners, refs[:n], *refs[n:])

    size = sum(source.size for source in sources)
    return pl.pallas_call(
        body,
        in_specs=[SMEM] * 2 + [VMEM] * (n + 1),
        out_specs=VMEM,
        out_shape=pltpu.VMEM(total.shape, F32),
        input_output_aliases={n + 2: 0},
        compiler_params=pltpu.CompilerParams(vmem_limit_bytes=SCOPED),
        cost_estimate=pl.CostEstimate(flops=size * 8, bytes_accessed=size * 12, transcendentals=0),
        name="deposit_patches",
    )(scalars, corners, *map(in_vmem, (*sources, total)))


def split_kernel(margin, lat, total, keep, send, sems):
    owners, rows = keep.shape[2:4]
    copies = []
    for owner in range(owners):
        for kind, target in ((lat[0], keep), (1 - lat[0], send)):
            start = pl.multiple_of(margin + (2 * owner + kind) * rows, 8)
            copies.append(
                pltpu.make_async_copy(
                    total.at[:, :, pl.ds(start, rows), :], target.at[:, :, owner], sems.at[len(copies)]
                )
            )
    for copy in copies:
        copy.start()
    for copy in copies:
        copy.wait()


def split_rows(total, lat, owners, margin):
    parts, layers, height, width = total.shape
    rows = (height - 2 * margin) // (2 * owners)
    half = jax.ShapeDtypeStruct((parts, layers, owners, rows, width), F32)
    return pl.pallas_call(
        functools.partial(split_kernel, margin),
        in_specs=[SMEM, VMEM],
        out_specs=[HBM, HBM],
        out_shape=[half, half],
        scratch_shapes=[pltpu.SemaphoreType.DMA((2 * owners,))],
        compiler_params=pltpu.CompilerParams(vmem_limit_bytes=SCOPED),
        name="split_rows",
    )(lat.reshape(1), in_vmem(total))


def swap(shard, axis):
    return lax.ppermute(shard, axis, [(0, 1), (1, 0)])


def local(specimen, illumination, positions, scan_index, frames):
    pixels = illumination.shape[-1]
    parts, layers, half, width = specimen.shape
    height = 2 * half
    tables = jnp.asarray(make_tables(pixels))
    section = lax.axis_index("depth")
    sections = lax.axis_size("depth")
    lat = lax.axis_index("lat")
    owners = lax.axis_size("probe")
    paired = owners == 2

    other = swap(specimen, "lat")
    corners = positions[scan_index.reshape(-1)]
    probes = corners.shape[0]
    count = 2 if probes % 2 == 0 else 1
    groups = probes // count
    wave = (count, parts, pixels, pixels)
    patches, seen = cut_patches(specimen, other, corners, lat, pixels, count)
    measured = frames.reshape((groups, count, pixels, pixels))
    if paired:
        both = jnp.stack([corners, swap(corners, "probe")])
        base = lax.axis_index("probe") * (height // 2)
        total = blank_total(parts, layers, height // 2, width, pixels)
    else:
        both = corners[None]
        base = jnp.int32(0)
        total = blank_total(parts, layers, height, width, pixels)

    is_first = (section == 0).astype(jnp.int32)
    is_last = (section == sections - 1).astype(jnp.int32)

    def scalars_of(group):
        active = ((group >= 0) & (group < groups)).astype(jnp.int32)
        return jnp.stack([jnp.clip(group, 0, groups - 1), active, is_first, is_last])

    def pairs_of(tick, by):
        pairs = []
        for source in range(sections):
            delay = source if by > 0 else 2 * (sections - 1) - source
            if 0 <= source + by < sections and 0 <= tick - LAG * delay < groups:
                pairs.append((source, source + by))
        return pairs

    nothing = jnp.zeros(wave, F32)
    down, up, across = {}, {}, None
    depth = LAG * (sections - 1)
    for tick in range(groups + 2 * depth):
        leaving = nothing
        if tick < groups + depth:
            scalars = scalars_of(tick - LAG * section)
            leaving, seen = run_forward(
                scalars, patches, down.pop(tick - LAG, nothing), illumination, measured, tables, seen
            )
            pairs = pairs_of(tick, 1)
            if pairs:
                down[tick] = lax.ppermute(leaving, "depth", pairs)
        if tick >= depth:
            scalars = scalars_of(tick - LAG * (2 * (sections - 1) - section))
            rising, grads = run_backward(
                scalars, patches, up.pop(tick - LAG, nothing), leaving, seen, tables
            )
            pairs = pairs_of(tick, -1)
            if pairs:
                up[tick] = lax.ppermute(rising, "depth", pairs)
            sources = [grads]
            ats = [scalars[:2]]
            if paired:
                if across is not None:
                    sources.append(across[0])
                    ats.append(across[1])
                across = (swap(grads, "probe"), scalars[:2])
            total = deposit(jnp.concatenate([base[None], *ats]), both, sources, total, height)
    if paired:
        scalars = jnp.concatenate([base[None], across[1]])
        total = deposit(scalars, both[1:], [across[0]], total, height)
        keep, send = split_rows(total, lat, 1, pixels + 8)
        return keep[:, :, 0] + swap(send[:, :, 0], "lat")
    keep, send = split_rows(total, lat, owners, pixels + 8)
    return lax.psum_scatter(keep + swap(send, "lat"), "probe", scatter_dimension=2, tiled=False)


def solution(mesh):
    return jax.shard_map(
        local,
        mesh=mesh,
        in_specs=(
            P(None, ("groups", "depth"), "lat", None),
            P(),
            P("groups", None),
            P("groups", ("probe", "lat")),
            P("groups", ("probe", "lat"), None, None),
        ),
        out_specs=P(None, ("groups", "depth"), ("probe", "lat"), None),
        check_vma=False,
    )
```

time: 382 us -> 295 us (0.77)
  local copies, waits for them, and re-layouts: 149 us -> 61.2 us
  waiting for transfers between devices: 110 us -> 94.2 us
  Pallas kernels: 56.4 us -> 67.4 us
  starting transfers between devices: 54.8 us -> 65.1 us
  other arithmetic: 9.11 us -> 4.24 us
    unnamed x149 -> x85, local copies, waits for them, and re-layouts: 144 us -> 59.4 us
    ppermute x3 -> x14, waiting for transfers between devices: 65.7 us -> 48.2 us  [swap(): return lax.ppermute(shard, axis, [(0, 1), (1, 0)])]
    ppermute x10, waiting for transfers between devices: 12.6 us -> 24.1 us  [local(): down[tick] = lax.ppermute(leaving, 'depth', pairs)]
    ppermute x3 -> x14, starting transfers between devices: 6.39 us -> 16.4 us  [swap(): return lax.ppermute(shard, axis, [(0, 1), (1, 0)])]
    ppermute x10, waiting for transfers between devices: 31.8 us -> 21.8 us  [local(): up[tick] = lax.ppermute(rising, 'depth', pairs)]
    pallas_call x23 -> x36, Pallas kernels: 45.4 us -> 55.2 us  [the longest x11 19.9 us: run_backward(): pl.pallas_call(backward_kernel, in_specs=[SMEM] + [VMEM] * 5, out_specs=[...]
    add x2 -> x1, other arithmetic: 8.44 us -> 1.69 us  [local(): return keep[:, :, 0] + swap(send[:, :, 0], 'lat')]
  transfers between devices with their start and end apart: 23 -> 34, of which waited for: 11 -> 22; matrix products, arithmetic and copies ran while one was open for 1% -> 2% of each run, Pallas kernels for 6% -> 16%
where the time goes in v2:
time: 295 us; the launch traced here: 293 us
  waiting for transfers between devices  94.2 us (32%)
  Pallas kernels  67.4 us (23%)
  starting transfers between devices  65.1 us (22%)
  local copies, waits for them, and re-layouts  61.2 us (21%)
  other arithmetic  4.24 us (1%)
    unnamed x85, local copies, waits for them, and re-layouts  59.4 us
    ppermute x14, waiting for transfers between devices, swap(): return lax.ppermute(shard, axis, [(0, 1), (1, 0)])  48.2 us
    ppermute x10, starting transfers between devices, local(): down[tick] = lax.ppermute(leaving, 'depth', pairs)  37 us
    ppermute x10, waiting for transfers between devices, local(): down[tick] = lax.ppermute(leaving, 'depth', pairs)  24.1 us
    ppermute x10, waiting for transfers between devices, local(): up[tick] = lax.ppermute(rising, 'depth', pairs)  21.8 us
    pallas_call x11, Pallas kernels, run_backward(): pl.pallas_call(backward_kernel, in_specs=[SMEM] + [VMEM] * 5, out_specs=[...  19.9 us
    pallas_call x12, Pallas kernels, deposit(): pl.pallas_call(body, in_specs=[SMEM] * 2 + [VMEM] * (n + 1), out_specs=VM...  17.7 us
    pallas_call x11, Pallas kernels, run_forward(): pl.pallas_call(forward_kernel, in_specs=[SMEM] + [VMEM] * 6, out_specs=[V...  16.8 us
  transfers between devices with their start and end apart: 34, of which 22 were waited for; matrix products, arithmetic and copies ran while one was open for 2% of the time, Pallas kernels for 16%

profile of v2, /device:TPU:0, one launch (start us, length us, event | category | flops | bytes accessed | tf_op | source)
XLA Modules:
  0.0 292.9 jit_solution(10835781195725989073)
XLA Ops:
  2.7 5.6 %collective-permute-done.1.other = f32[2,2,384,768]{3,2,1,0:T(8,128)} collective-permute-done((f32[2,2,384,768]{3,2,1,0:T(8,128)}, f32[2,2,384,768]{3,2,1,0:T(8,128)}, u32[]{:S(2)}, u32[]{:S(2)}) %collective-permute-start.1) | collective-permute-done | bytes 4718624 | tf_op jit(solution)/shard_map/ppermute | solution.py:374
  8.3 12.1 %cut_patches.1 = (f32[8,2,2,2,128,128]{5,4,3,2,1,0:T(8,128)S(1)}, f32[8,2,2,2,128,128]{5,4,3,2,1,0:T(8,128)S(1)}) custom-call(s32[32]{0:T(128)S(1)} %reshape.12.corners, s32[1]{0:T(128)} %bitcast.lat, f32[2,2,384,768]{3,2,1,0:T(8,128)} %own.1, f32[2,2,384,768]{3,2,1,0:T(8,128)} %collective-permute-done.1.other), custom_call_target="tpu_custom_call" | custom-call | flops 4194304 | bytes 12582912 | tf_op jit(solution)/shard_map/cut_patches/pallas_call | solution.py:165
  24.5 4.9 %collective-permute-start.2 = (f32[2,2,128,128]{3,2,1,0:T(8,128)S(1)}, f32[2,2,128,128]{3,2,1,0:T(8,128)S(1)}, u32[]{:S(2)}, u32[]{:S(2)}) collective-permute-start(f32[2,2,128,128]{3,2,1,0:T(8,128)S(1)} %get-tuple-element.54), channel_id=1, source_target_pairs={{0,4},{1,5},{2,6},{3,7},{16,20},{17,21},{18,22},{19,23}} | collective-permute-start | bytes 786440 | tf_op jit(solution)/shard_map/ppermute | solution.py:432
  29.5 6.5 %collective-permute-done.2.arrived = f32[2,2,128,128]{3,2,1,0:T(8,128)S(1)} collective-permute-done((f32[2,2,128,128]{3,2,1,0:T(8,128)S(1)}, f32[2,2,128,128]{3,2,1,0:T(8,128)S(1)}, u32[]{:S(2)}, u32[]{:S(2)}) %collective-permute-start.2) | collective-permute-done | bytes 262176 | tf_op jit(solution)/shard_map/ppermute | solution.py:432
  36.0 2.2 copy-done.1
  44.3 4.4 %collective-permute-start.3 = (f32[2,2,128,128]{3,2,1,0:T(8,128)S(1)}, f32[2,2,128,128]{3,2,1,0:T(8,128)S(1)}, u32[]{:S(2)}, u32[]{:S(2)}) collective-permute-start(f32[2,2,128,128]{3,2,1,0:T(8,128)S(1)} %get-tuple-element.56), channel_id=1, source_target_pairs={{0,4},{4,8},{1,5},{5,9},{2,6},{6,10},{3,7},{7,11},{16,20},{20,24},... | collective-permute-start | bytes 786440 | tf_op jit(solution)/shard_map/ppermute | solution.py:432
  48.7 5.6 %collective-permute-done.3.arrived = f32[2,2,128,128]{3,2,1,0:T(8,128)S(1)} collective-permute-done((f32[2,2,128,128]{3,2,1,0:T(8,128)S(1)}, f32[2,2,128,128]{3,2,1,0:T(8,128)S(1)}, u32[]{:S(2)}, u32[]{:S(2)}) %collective-permute-start.3) | collective-permute-done | bytes 262176 | tf_op jit(solution)/shard_map/ppermute | solution.py:432
  54.4 2.2 copy-done.2
  56.6 2.2 copy-done.10
  62.7 4.4 %collective-permute-start.4 = (f32[2,2,128,128]{3,2,1,0:T(8,128)S(1)}, f32[2,2,128,128]{3,2,1,0:T(8,128)S(1)}, u32[]{:S(2)}, u32[]{:S(2)}) collective-permute-start(f32[2,2,128,128]{3,2,1,0:T(8,128)S(1)} %get-tuple-element.58), channel_id=1, source_target_pairs={{0,4},{4,8},{8,12},{1,5},{5,9},{9,13},{2,6},{6,10},{10,14},{3,7},{... | collective-permute-start | bytes 786440 | tf_op jit(solution)/shard_map/ppermute | solution.py:432
  67.3 4.7 %collective-permute-done.4.arrived = f32[2,2,128,128]{3,2,1,0:T(8,128)S(1)} collective-permute-done((f32[2,2,128,128]{3,2,1,0:T(8,128)S(1)}, f32[2,2,128,128]{3,2,1,0:T(8,128)S(1)}, u32[]{:S(2)}, u32[]{:S(2)}) %collective-permute-start.4) | collective-permute-done | bytes 262176 | tf_op jit(solution)/shard_map/ppermute | solution.py:432
  71.9 2.2 copy-done.3
  74.1 2.2 copy-done.12
  78.2 4.4 %collective-permute-start.6 = (f32[2,2,128,128]{3,2,1,0:T(8,128)S(1)}, f32[2,2,128,128]{3,2,1,0:T(8,128)S(1)}, u32[]{:S(2)}, u32[]{:S(2)}) collective-permute-start(f32[2,2,128,128]{3,2,1,0:T(8,128)S(1)} %get-tuple-element.60.own), channel_id=1, source_target_pairs={{0,4},{4,8},{8,12},{1,5},{5,9},{9,13},{2,6},{6,10},{10,14},{3,7},{... | collective-permute-start | bytes 786440 | tf_op jit(solution)/shard_map/ppermute | solution.py:432
  84.0 2.5 collective-permute-done.6.arrived
  88.4 4.4 %collective-permute-start.8 = (f32[2,2,128,128]{3,2,1,0:T(8,128)S(1)}, f32[2,2,128,128]{3,2,1,0:T(8,128)S(1)}, u32[]{:S(2)}, u32[]{:S(2)}) collective-permute-start(f32[2,2,128,128]{3,2,1,0:T(8,128)S(1)} %get-tuple-element.63.own), channel_id=1, source_target_pairs={{0,4},{4,8},{8,12},{1,5},{5,9},{9,13},{2,6},{6,10},{10,14},{3,7},{... | collective-permute-start | bytes 786440 | tf_op jit(solution)/shard_map/ppermute | solution.py:432
  94.2 2.4 collective-permute-done.8.arrived
  98.6 4.4 %collective-permute-start.10 = (f32[2,2,128,128]{3,2,1,0:T(8,128)S(1)}, f32[2,2,128,128]{3,2,1,0:T(8,128)S(1)}, u32[]{:S(2)}, u32[]{:S(2)}) collective-permute-start(f32[2,2,128,128]{3,2,1,0:T(8,128)S(1)} %get-tuple-element.66.own), channel_id=1, source_target_pairs={{0,4},{4,8},{8,12},{1,5},{5,9},{9,13},{2,6},{6,10},{10,14},{3,7},{... | collective-permute-start | bytes 786440 | tf_op jit(solution)/shard_map/ppermute | solution.py:432
  108.7 4.4 %collective-permute-start.12 = (f32[2,2,128,128]{3,2,1,0:T(8,128)S(1)}, f32[2,2,128,128]{3,2,1,0:T(8,128)S(1)}, u32[]{:S(2)}, u32[]{:S(2)}) collective-permute-start(f32[2,2,128,128]{3,2,1,0:T(8,128)S(1)} %get-tuple-element.69.own), channel_id=1, source_target_pairs={{0,4},{4,8},{8,12},{1,5},{5,9},{9,13},{2,6},{6,10},{10,14},{3,7},{... | collective-permute-start | bytes 786440 | tf_op jit(solution)/shard_map/ppermute | solution.py:432
  118.9 4.4 %collective-permute-start.14 = (f32[2,2,128,128]{3,2,1,0:T(8,128)S(1)}, f32[2,2,128,128]{3,2,1,0:T(8,128)S(1)}, u32[]{:S(2)}, u32[]{:S(2)}) collective-permute-start(f32[2,2,128,128]{3,2,1,0:T(8,128)S(1)} %get-tuple-element.72.own), channel_id=1, source_target_pairs={{0,4},{4,8},{8,12},{1,5},{5,9},{9,13},{2,6},{6,10},{10,14},{3,7},{... | collective-permute-start | bytes 786440 | tf_op jit(solution)/shard_map/ppermute | solution.py:432
  123.3 2.6 backward_section.15
  128.8 5.4 %collective-permute-done.13.arrived = f32[2,2,128,128]{3,2,1,0:T(8,128)S(1)} collective-permute-done((f32[2,2,128,128]{3,2,1,0:T(8,128)S(1)}, f32[2,2,128,128]{3,2,1,0:T(8,128)S(1)}, u32[]{:S(2)}, u32[]{:S(2)}) %collective-permute-start.13) | collective-permute-done | bytes 262176 | tf_op jit(solution)/shard_map/ppermute | solution.py:440
  134.2 2.6 backward_section.16
  139.5 6.6 %collective-permute-done.15.arrived = f32[2,2,128,128]{3,2,1,0:T(8,128)S(1)} collective-permute-done((f32[2,2,128,128]{3,2,1,0:T(8,128)S(1)}, f32[2,2,128,128]{3,2,1,0:T(8,128)S(1)}, u32[]{:S(2)}, u32[]{:S(2)}) %collective-permute-start.15) | collective-permute-done | bytes 262176 | tf_op jit(solution)/shard_map/ppermute | solution.py:440
  150.2 3.0 %collective-permute-start.32 = (f32[2,2,2,128,128]{4,3,2,1,0:T(8,128)S(1)}, f32[2,2,2,128,128]{4,3,2,1,0:T(8,128)}, u32[]{:S(2)}, u32[]{:S(2)}) collective-permute-start(f32[2,2,2,128,128]{4,3,2,1,0:T(8,128)S(1)} %get-tuple-element.96.refs_0_), channel_id=1, source_target_pairs={{0,2},{2,0},{1,3},{3,1},{4,6},{6,4},{5,7},{7,5},{8,10},{10,8},{9,1... | collective-permute-start | bytes 1572872 | tf_op jit(solution)/shard_map/ppermute | solution.py:374
  153.8 5.4 %collective-permute-done.17.arrived = f32[2,2,128,128]{3,2,1,0:T(8,128)S(1)} collective-permute-done((f32[2,2,128,128]{3,2,1,0:T(8,128)S(1)}, f32[2,2,128,128]{3,2,1,0:T(8,128)S(1)}, u32[]{:S(2)}, u32[]{:S(2)}) %collective-permute-start.17) | collective-permute-done | bytes 262176 | tf_op jit(solution)/shard_map/ppermute | solution.py:440
  163.3 2.8 collective-permute-start.31
  166.0 4.1 %collective-permute-done.19.arrived = f32[2,2,128,128]{3,2,1,0:T(8,128)S(1)} collective-permute-done((f32[2,2,128,128]{3,2,1,0:T(8,128)S(1)}, f32[2,2,128,128]{3,2,1,0:T(8,128)S(1)}, u32[]{:S(2)}, u32[]{:S(2)}) %collective-permute-start.19) | collective-permute-done | bytes 262176 | tf_op jit(solution)/shard_map/ppermute | solution.py:440
  170.9 2.2 copy-done.4
  173.0 2.2 copy-done.14
  180.1 2.8 collective-permute-start
  187.8 2.8 collective-permute-start.27
  190.6 2.2 copy-done.5
  195.9 2.5 backward_section.20
  200.7 8.4 %collective-permute-done.29.refs_1_ = f32[2,2,2,128,128]{4,3,2,1,0:T(8,128)} collective-permute-done((f32[2,2,2,128,128]{4,3,2,1,0:T(8,128)S(1)}, f32[2,2,2,128,128]{4,3,2,1,0:T(8,128)}, u32[]{:S(2)}, u32[]{:S(2)}) %collective-permute-start.29) | collective-permute-done | bytes 524320 | tf_op jit(solution)/shard_map/ppermute | solution.py:374
  209.3 11.1 %collective-permute-done.28.refs_1_ = f32[2,2,2,128,128]{4,3,2,1,0:T(8,128)} collective-permute-done((f32[2,2,2,128,128]{4,3,2,1,0:T(8,128)}, f32[2,2,2,128,128]{4,3,2,1,0:T(8,128)}, u32[]{:S(2)}, u32[]{:S(2)}) %collective-permute-start.28) | collective-permute-done | bytes 524320 | tf_op jit(solution)/shard_map/ppermute | solution.py:374
  224.6 2.2 copy-done.16
  226.8 3.1 %backward_section.21 = (f32[2,2,128,128]{3,2,1,0:T(8,128)}, f32[2,2,2,128,128]{4,3,2,1,0:T(8,128)}) custom-call(s32[4]{0:T(128)S(1)} %add_add_fusion.scalars, f32[8,2,2,2,128,128]{5,4,3,2,1,0:T(8,128)S(1)} %copy-done.6, f32[2,2,128,128]{3,2,1,0:T(8,128)} %collective-permute-done.21.arrived, f32[2,2,128,128]{3,2,1,0:T(8,128)S(1)} %broadcast_in_dim.5.arrived.own, ...), custom_call_target="tpu_custom_call" | custom-call | flops 402653184 | bytes 1572864 | tf_op jit(solution)/shard_map/backward_section/pallas_call | solution.py:265
  232.4 3.2 %copy-done.17 = f32[2,2,656,768]{3,2,1,0:T(8,128)} copy-done((f32[2,2,656,768]{3,2,1,0:T(8,128)}, f32[2,2,656,768]{3,2,1,0:T(8,128)S(1)}, u32[]{:S(2)}) %copy-start.17) | copy-done | bytes 8060952
  236.9 3.3 %copy-done.18 = f32[2,2,656,768]{3,2,1,0:T(8,128)S(1)} copy-done((f32[2,2,656,768]{3,2,1,0:T(8,128)S(1)}, f32[2,2,656,768]{3,2,1,0:T(8,128)}, u32[]{:S(2)}) %copy-start.18) | copy-done | bytes 8060952
  251.3 2.7 collective-permute-done.25.refs_1_
  255.7 8.1 %collective-permute-done.24.refs_1_ = f32[2,2,2,128,128]{4,3,2,1,0:T(8,128)} collective-permute-done((f32[2,2,2,128,128]{4,3,2,1,0:T(8,128)}, f32[2,2,2,128,128]{4,3,2,1,0:T(8,128)}, u32[]{:S(2)}, u32[]{:S(2)}) %collective-permute-start.24) | collective-permute-done | bytes 524320 | tf_op jit(solution)/shard_map/ppermute | solution.py:374
  265.4 4.0 %collective-permute-done.23.refs_1_ = f32[2,2,2,128,128]{4,3,2,1,0:T(8,128)} collective-permute-done((f32[2,2,2,128,128]{4,3,2,1,0:T(8,128)}, f32[2,2,2,128,128]{4,3,2,1,0:T(8,128)}, u32[]{:S(2)}, u32[]{:S(2)}) %collective-permute-start.23) | collective-permute-done | bytes 524320 | tf_op jit(solution)/shard_map/ppermute | solution.py:374
  271.4 3.2 %copy-done.19 = f32[2,2,656,768]{3,2,1,0:T(8,128)} copy-done((f32[2,2,656,768]{3,2,1,0:T(8,128)}, f32[2,2,656,768]{3,2,1,0:T(8,128)S(1)}, u32[]{:S(2)}) %copy-start.19) | copy-done | bytes 8060952
  275.0 3.3 %copy-done.20 = f32[2,2,656,768]{3,2,1,0:T(8,128)S(1)} copy-done((f32[2,2,656,768]{3,2,1,0:T(8,128)S(1)}, f32[2,2,656,768]{3,2,1,0:T(8,128)}, u32[]{:S(2)}) %copy-start.20) | copy-done | bytes 8060952
  279.7 3.2 %copy-done.21 = f32[2,2,656,768]{3,2,1,0:T(8,128)} copy-done((f32[2,2,656,768]{3,2,1,0:T(8,128)}, f32[2,2,656,768]{3,2,1,0:T(8,128)S(1)}, u32[]{:S(2)}) %copy-start.21) | copy-done | bytes 8060952
  283.0 3.3 %copy-done.22 = f32[2,2,656,768]{3,2,1,0:T(8,128)S(1)} copy-done((f32[2,2,656,768]{3,2,1,0:T(8,128)S(1)}, f32[2,2,656,768]{3,2,1,0:T(8,128)}, u32[]{:S(2)}) %copy-start.22) | copy-done | bytes 8060952
  286.7 4.5 %collective-permute-done.33 = f32[2,2,192,768]{3,2,1,0:T(8,128)S(1)} collective-permute-done((f32[2,2,192,768]{3,2,1,0:T(8,128)S(1)}, f32[2,2,192,768]{3,2,1,0:T(8,128)S(1)}, u32[]{:S(2)}, u32[]{:S(2)}) %collective-permute-start.33) | collective-permute-done | bytes 2359328 | tf_op jit(solution)/shard_map/ppermute | solution.py:374
  (187 shorter events, 95.0 us)
Async XLA Ops:
  0.0 8.3 %collective-permute-start.1 = (f32[2,2,384,768]{3,2,1,0:T(8,128)}, f32[2,2,384,768]{3,2,1,0:T(8,128)}, u32[]{:S(2)}, u32[]{:S(2)}) collective-permute-start(f32[2,2,384,768]{3,2,1,0:T(8,128)} %own.1), channel_id=1, source_target_pairs={{0,1},{1,0},{2,3},{3,2},{4,5},{5,4},{6,7},{7,6},{8,9},{9,8},{10,11... | collective-permute-start | bytes 14155784 | tf_op jit(solution)/shard_map/ppermute | solution.py:374
  8.3 12.2 %copy-start.23 = (bf16[2,2,2,256,256]{4,3,2,1,0:T(8,128)(2,1)S(1)}, bf16[2,2,2,256,256]{4,3,2,1,0:T(8,128)(2,1)}, u32[]{:S(2)}) copy-start(bf16[2,2,2,256,256]{4,3,2,1,0:T(8,128)(2,1)} %constant.48.clone.tables) | copy-start | bytes 3145732
  8.3 12.2 %copy-start.24 = (f32[16,1,128,128]{3,2,1,0:T(8,128)S(1)}, f32[16,1,128,128]{3,2,1,0:T(8,128)}, u32[]{:S(2)}) copy-start(f32[16,1,128,128]{3,2,1,0:T(8,128)} %param.10) | copy-start | bytes 3145732
  8.3 12.2 %copy-start.25 = (f32[2,128,128]{2,1,0:T(8,128)S(1)}, f32[2,128,128]{2,1,0:T(8,128)}, u32[]{:S(2)}) copy-start(f32[2,128,128]{2,1,0:T(8,128)} %start_wave.21) | copy-start | bytes 393220
  24.5 11.4 %collective-permute-start.2 = (f32[2,2,128,128]{3,2,1,0:T(8,128)S(1)}, f32[2,2,128,128]{3,2,1,0:T(8,128)S(1)}, u32[]{:S(2)}, u32[]{:S(2)}) collective-permute-start(f32[2,2,128,128]{3,2,1,0:T(8,128)S(1)} %get-tuple-element.54), channel_id=1, source_target_pairs={{0,4},{1,5},{2,6},{3,7},{16,20},{17,21},{18,22},{19,23}} | collective-permute-start | bytes 786440 | tf_op jit(solution)/shard_map/ppermute | solution.py:432
  44.3 10.1 %collective-permute-start.3 = (f32[2,2,128,128]{3,2,1,0:T(8,128)S(1)}, f32[2,2,128,128]{3,2,1,0:T(8,128)S(1)}, u32[]{:S(2)}, u32[]{:S(2)}) collective-permute-start(f32[2,2,128,128]{3,2,1,0:T(8,128)S(1)} %get-tuple-element.56), channel_id=1, source_target_pairs={{0,4},{4,8},{1,5},{5,9},{2,6},{6,10},{3,7},{7,11},{16,20},{20,24},... | collective-permute-start | bytes 786440 | tf_op jit(solution)/shard_map/ppermute | solution.py:432
  62.7 9.3 %collective-permute-start.4 = (f32[2,2,128,128]{3,2,1,0:T(8,128)S(1)}, f32[2,2,128,128]{3,2,1,0:T(8,128)S(1)}, u32[]{:S(2)}, u32[]{:S(2)}) collective-permute-start(f32[2,2,128,128]{3,2,1,0:T(8,128)S(1)} %get-tuple-element.58), channel_id=1, source_target_pairs={{0,4},{4,8},{8,12},{1,5},{5,9},{9,13},{2,6},{6,10},{10,14},{3,7},{... | collective-permute-start | bytes 786440 | tf_op jit(solution)/shard_map/ppermute | solution.py:432
  78.2 8.4 %collective-permute-start.6 = (f32[2,2,128,128]{3,2,1,0:T(8,128)S(1)}, f32[2,2,128,128]{3,2,1,0:T(8,128)S(1)}, u32[]{:S(2)}, u32[]{:S(2)}) collective-permute-start(f32[2,2,128,128]{3,2,1,0:T(8,128)S(1)} %get-tuple-element.60.own), channel_id=1, source_target_pairs={{0,4},{4,8},{8,12},{1,5},{5,9},{9,13},{2,6},{6,10},{10,14},{3,7},{... | collective-permute-start | bytes 786440 | tf_op jit(solution)/shard_map/ppermute | solution.py:432
  83.1 9.7 %collective-permute-start.5 = (f32[2,2,128,128]{3,2,1,0:T(8,128)S(1)}, f32[2,2,128,128]{3,2,1,0:T(8,128)S(1)}, u32[]{:S(2)}, u32[]{:S(2)}) collective-permute-start(f32[2,2,128,128]{3,2,1,0:T(8,128)S(1)} %get-tuple-element.62), channel_id=1, source_target_pairs={{12,8},{13,9},{14,10},{15,11},{28,24},{29,25},{30,26},{31,27}} | collective-permute-start | bytes 786440 | tf_op jit(solution)/shard_map/ppermute | solution.py:440
  88.4 8.3 %collective-permute-start.8 = (f32[2,2,128,128]{3,2,1,0:T(8,128)S(1)}, f32[2,2,128,128]{3,2,1,0:T(8,128)S(1)}, u32[]{:S(2)}, u32[]{:S(2)}) collective-permute-start(f32[2,2,128,128]{3,2,1,0:T(8,128)S(1)} %get-tuple-element.63.own), channel_id=1, source_target_pairs={{0,4},{4,8},{8,12},{1,5},{5,9},{9,13},{2,6},{6,10},{10,14},{3,7},{... | collective-permute-start | bytes 786440 | tf_op jit(solution)/shard_map/ppermute | solution.py:432
  93.4 9.6 %collective-permute-start.7 = (f32[2,2,128,128]{3,2,1,0:T(8,128)S(1)}, f32[2,2,128,128]{3,2,1,0:T(8,128)S(1)}, u32[]{:S(2)}, u32[]{:S(2)}) collective-permute-start(f32[2,2,128,128]{3,2,1,0:T(8,128)S(1)} %get-tuple-element.65), channel_id=1, source_target_pairs={{8,4},{12,8},{9,5},{13,9},{10,6},{14,10},{11,7},{15,11},{24,20},{2... | collective-permute-start | bytes 786440 | tf_op jit(solution)/shard_map/ppermute | solution.py:440
  98.6 8.3 %collective-permute-start.10 = (f32[2,2,128,128]{3,2,1,0:T(8,128)S(1)}, f32[2,2,128,128]{3,2,1,0:T(8,128)S(1)}, u32[]{:S(2)}, u32[]{:S(2)}) collective-permute-start(f32[2,2,128,128]{3,2,1,0:T(8,128)S(1)} %get-tuple-element.66.own), channel_id=1, source_target_pairs={{0,4},{4,8},{8,12},{1,5},{5,9},{9,13},{2,6},{6,10},{10,14},{3,7},{... | collective-permute-start | bytes 786440 | tf_op jit(solution)/shard_map/ppermute | solution.py:432
  103.5 5.2 %copy-start.26 = (f32[2,2,2,128,128]{4,3,2,1,0:T(8,128)}, f32[2,2,2,128,128]{4,3,2,1,0:T(8,128)S(1)}, u32[]{:S(2)}) copy-start(f32[2,2,2,128,128]{4,3,2,1,0:T(8,128)S(1)} %get-tuple-element.94.refs_0_) | copy-start | bytes 1572868
  103.6 9.6 %collective-permute-start.9 = (f32[2,2,128,128]{3,2,1,0:T(8,128)S(1)}, f32[2,2,128,128]{3,2,1,0:T(8,128)S(1)}, u32[]{:S(2)}, u32[]{:S(2)}) collective-permute-start(f32[2,2,128,128]{3,2,1,0:T(8,128)S(1)} %get-tuple-element.68), channel_id=1, source_target_pairs={{4,0},{8,4},{12,8},{5,1},{9,5},{13,9},{6,2},{10,6},{14,10},{7,3},{... | collective-permute-start | bytes 786440 | tf_op jit(solution)/shard_map/ppermute | solution.py:440
  108.7 8.3 %collective-permute-start.12 = (f32[2,2,128,128]{3,2,1,0:T(8,128)S(1)}, f32[2,2,128,128]{3,2,1,0:T(8,128)S(1)}, u32[]{:S(2)}, u32[]{:S(2)}) collective-permute-start(f32[2,2,128,128]{3,2,1,0:T(8,128)S(1)} %get-tuple-element.69.own), channel_id=1, source_target_pairs={{0,4},{4,8},{8,12},{1,5},{5,9},{9,13},{2,6},{6,10},{10,14},{3,7},{... | collective-permute-start | bytes 786440 | tf_op jit(solution)/shard_map/ppermute | solution.py:432
  115.0 3.9 %copy-start.28 = (f32[2,2,2,128,128]{4,3,2,1,0:T(8,128)}, f32[2,2,2,128,128]{4,3,2,1,0:T(8,128)S(1)}, u32[]{:S(2)}) copy-start(f32[2,2,2,128,128]{4,3,2,1,0:T(8,128)S(1)} %get-tuple-element.93.refs_0_) | copy-start | bytes 1572868
  115.0 8.3 %collective-permute-start.11 = (f32[2,2,128,128]{3,2,1,0:T(8,128)S(1)}, f32[2,2,128,128]{3,2,1,0:T(8,128)S(1)}, u32[]{:S(2)}, u32[]{:S(2)}) collective-permute-start(f32[2,2,128,128]{3,2,1,0:T(8,128)S(1)} %get-tuple-element.71), channel_id=1, source_target_pairs={{4,0},{8,4},{12,8},{5,1},{9,5},{13,9},{6,2},{10,6},{14,10},{7,3},{... | collective-permute-start | bytes 786440 | tf_op jit(solution)/shard_map/ppermute | solution.py:440
  118.9 8.5 %collective-permute-start.14 = (f32[2,2,128,128]{3,2,1,0:T(8,128)S(1)}, f32[2,2,128,128]{3,2,1,0:T(8,128)S(1)}, u32[]{:S(2)}, u32[]{:S(2)}) collective-permute-start(f32[2,2,128,128]{3,2,1,0:T(8,128)S(1)} %get-tuple-element.72.own), channel_id=1, source_target_pairs={{0,4},{4,8},{8,12},{1,5},{5,9},{9,13},{2,6},{6,10},{10,14},{3,7},{... | collective-permute-start | bytes 786440 | tf_op jit(solution)/shard_map/ppermute | solution.py:432
  125.9 8.3 %collective-permute-start.13 = (f32[2,2,128,128]{3,2,1,0:T(8,128)S(1)}, f32[2,2,128,128]{3,2,1,0:T(8,128)S(1)}, u32[]{:S(2)}, u32[]{:S(2)}) collective-permute-start(f32[2,2,128,128]{3,2,1,0:T(8,128)S(1)} %get-tuple-element.74), channel_id=1, source_target_pairs={{4,0},{8,4},{12,8},{5,1},{9,5},{13,9},{6,2},{10,6},{14,10},{7,3},{... | collective-permute-start | bytes 786440 | tf_op jit(solution)/shard_map/ppermute | solution.py:440
  128.1 10.1 %collective-permute-start.16 = (f32[2,2,128,128]{3,2,1,0:T(8,128)S(1)}, f32[2,2,128,128]{3,2,1,0:T(8,128)S(1)}, u32[]{:S(2)}, u32[]{:S(2)}) collective-permute-start(f32[2,2,128,128]{3,2,1,0:T(8,128)S(1)} %get-tuple-element.75.own), channel_id=1, source_target_pairs={{4,8},{8,12},{5,9},{9,13},{6,10},{10,14},{7,11},{11,15},{20,24},{2... | collective-permute-start | bytes 786440 | tf_op jit(solution)/shard_map/ppermute | solution.py:432
  136.8 9.3 %collective-permute-start.15 = (f32[2,2,128,128]{3,2,1,0:T(8,128)S(1)}, f32[2,2,128,128]{3,2,1,0:T(8,128)S(1)}, u32[]{:S(2)}, u32[]{:S(2)}) collective-permute-start(f32[2,2,128,128]{3,2,1,0:T(8,128)S(1)} %get-tuple-element.77), channel_id=1, source_target_pairs={{4,0},{8,4},{12,8},{5,1},{9,5},{13,9},{6,2},{10,6},{14,10},{7,3},{... | collective-permute-start | bytes 786440 | tf_op jit(solution)/shard_map/ppermute | solution.py:440
  138.8 14.4 %collective-permute-start.18 = (f32[2,2,128,128]{3,2,1,0:T(8,128)S(1)}, f32[2,2,128,128]{3,2,1,0:T(8,128)S(1)}, u32[]{:S(2)}, u32[]{:S(2)}) collective-permute-start(f32[2,2,128,128]{3,2,1,0:T(8,128)S(1)} %get-tuple-element.78.own), channel_id=1, source_target_pairs={{8,12},{9,13},{10,14},{11,15},{24,28},{25,29},{26,30},{27,31}} | collective-permute-start | bytes 786440 | tf_op jit(solution)/shard_map/ppermute | solution.py:432
  148.8 10.5 %collective-permute-start.17 = (f32[2,2,128,128]{3,2,1,0:T(8,128)S(1)}, f32[2,2,128,128]{3,2,1,0:T(8,128)S(1)}, u32[]{:S(2)}, u32[]{:S(2)}) collective-permute-start(f32[2,2,128,128]{3,2,1,0:T(8,128)S(1)} %get-tuple-element.80), channel_id=1, source_target_pairs={{4,0},{8,4},{12,8},{5,1},{9,5},{13,9},{6,2},{10,6},{14,10},{7,3},{... | collective-permute-start | bytes 786440 | tf_op jit(solution)/shard_map/ppermute | solution.py:440
  150.2 36.5 %collective-permute-start.32 = (f32[2,2,2,128,128]{4,3,2,1,0:T(8,128)S(1)}, f32[2,2,2,128,128]{4,3,2,1,0:T(8,128)}, u32[]{:S(2)}, u32[]{:S(2)}) collective-permute-start(f32[2,2,2,128,128]{4,3,2,1,0:T(8,128)S(1)} %get-tuple-element.96.refs_0_), channel_id=1, source_target_pairs={{0,2},{2,0},{1,3},{3,1},{4,6},{6,4},{5,7},{7,5},{8,10},{10,8},{9,1... | collective-permute-start | bytes 1572872 | tf_op jit(solution)/shard_map/ppermute | solution.py:374
  153.8 7.3 %copy-start.13 = (f32[8,2,2,2,128,128]{5,4,3,2,1,0:T(8,128)}, f32[8,2,2,2,128,128]{5,4,3,2,1,0:T(8,128)S(1)}, u32[]{:S(2)}) copy-start(f32[8,2,2,2,128,128]{5,4,3,2,1,0:T(8,128)S(1)} %get-tuple-element.82.seen) | copy-start | bytes 12582916
  161.9 8.3 %collective-permute-start.19 = (f32[2,2,128,128]{3,2,1,0:T(8,128)S(1)}, f32[2,2,128,128]{3,2,1,0:T(8,128)S(1)}, u32[]{:S(2)}, u32[]{:S(2)}) collective-permute-start(f32[2,2,128,128]{3,2,1,0:T(8,128)S(1)} %get-tuple-element.83), channel_id=1, source_target_pairs={{4,0},{8,4},{12,8},{5,1},{9,5},{13,9},{6,2},{10,6},{14,10},{7,3},{... | collective-permute-start | bytes 786440 | tf_op jit(solution)/shard_map/ppermute | solution.py:440
  163.3 36.0 %collective-permute-start.31 = (f32[2,2,2,128,128]{4,3,2,1,0:T(8,128)S(1)}, f32[2,2,2,128,128]{4,3,2,1,0:T(8,128)}, u32[]{:S(2)}, u32[]{:S(2)}) collective-permute-start(f32[2,2,2,128,128]{4,3,2,1,0:T(8,128)S(1)} %get-tuple-element.95.refs_0_), channel_id=1, source_target_pairs={{0,2},{2,0},{1,3},{3,1},{4,6},{6,4},{5,7},{7,5},{8,10},{10,8},{9,1... | collective-permute-start | bytes 1572872 | tf_op jit(solution)/shard_map/ppermute | solution.py:374
  176.2 6.7 %copy-start.27 = (f32[2,2,2,128,128]{4,3,2,1,0:T(8,128)S(1)}, f32[2,2,2,128,128]{4,3,2,1,0:T(8,128)}, u32[]{:S(2)}) copy-start(f32[2,2,2,128,128]{4,3,2,1,0:T(8,128)} %copy-done.26) | copy-start | bytes 1572868
  176.2 8.5 %copy-start.29 = (f32[2,2,2,128,128]{4,3,2,1,0:T(8,128)S(1)}, f32[2,2,2,128,128]{4,3,2,1,0:T(8,128)}, u32[]{:S(2)}) copy-start(f32[2,2,2,128,128]{4,3,2,1,0:T(8,128)} %copy-done.28) | copy-start | bytes 1572868
  178.8 8.3 %collective-permute-start.20 = (f32[2,2,128,128]{3,2,1,0:T(8,128)S(1)}, f32[2,2,128,128]{3,2,1,0:T(8,128)S(1)}, u32[]{:S(2)}, u32[]{:S(2)}) collective-permute-start(f32[2,2,128,128]{3,2,1,0:T(8,128)S(1)} %get-tuple-element.84), channel_id=1, source_target_pairs={{4,0},{8,4},{5,1},{9,5},{6,2},{10,6},{7,3},{11,7},{20,16},{24,20},... | collective-permute-start | bytes 786440 | tf_op jit(solution)/shard_map/ppermute | solution.py:440
  180.1 4.6 %collective-permute-start = (s32[16,2]{1,0:T(8,128)S(1)}, s32[16,2]{1,0:T(8,128)S(1)}, u32[]{:S(2)}, u32[]{:S(2)}) collective-permute-start(s32[16,2]{1,0:T(8,128)S(1)} %gather_fusion), channel_id=1, source_target_pairs={{0,2},{2,0},{1,3},{3,1},{4,6},{6,4},{5,7},{7,5},{8,10},{10,8},{9,1... | collective-permute-start | bytes 392 | tf_op jit(solution)/shard_map/ppermute | solution.py:374
  182.9 17.8 %collective-permute-start.30 = (f32[2,2,2,128,128]{4,3,2,1,0:T(8,128)S(1)}, f32[2,2,2,128,128]{4,3,2,1,0:T(8,128)}, u32[]{:S(2)}, u32[]{:S(2)}) collective-permute-start(f32[2,2,2,128,128]{4,3,2,1,0:T(8,128)S(1)} %copy-done.27), channel_id=1, source_target_pairs={{0,2},{2,0},{1,3},{3,1},{4,6},{6,4},{5,7},{7,5},{8,10},{10,8},{9,1... | collective-permute-start | bytes 1572872 | tf_op jit(solution)/shard_map/ppermute | solution.py:374
  184.7 24.4 %collective-permute-start.29 = (f32[2,2,2,128,128]{4,3,2,1,0:T(8,128)S(1)}, f32[2,2,2,128,128]{4,3,2,1,0:T(8,128)}, u32[]{:S(2)}, u32[]{:S(2)}) collective-permute-start(f32[2,2,2,128,128]{4,3,2,1,0:T(8,128)S(1)} %copy-done.29), channel_id=1, source_target_pairs={{0,2},{2,0},{1,3},{3,1},{4,6},{6,4},{5,7},{7,5},{8,10},{10,8},{9,1... | collective-permute-start | bytes 1572872 | tf_op jit(solution)/shard_map/ppermute | solution.py:374
  186.7 33.6 %collective-permute-start.28 = (f32[2,2,2,128,128]{4,3,2,1,0:T(8,128)}, f32[2,2,2,128,128]{4,3,2,1,0:T(8,128)}, u32[]{:S(2)}, u32[]{:S(2)}) collective-permute-start(f32[2,2,2,128,128]{4,3,2,1,0:T(8,128)} %get-tuple-element.92.refs_0_), channel_id=1, source_target_pairs={{0,2},{2,0},{1,3},{3,1},{4,6},{6,4},{5,7},{7,5},{8,10},{10,8},{9,1... | collective-permute-start | bytes 1572872 | tf_op jit(solution)/shard_map/ppermute | solution.py:374
  187.8 43.8 %collective-permute-start.27 = (f32[2,2,2,128,128]{4,3,2,1,0:T(8,128)}, f32[2,2,2,128,128]{4,3,2,1,0:T(8,128)}, u32[]{:S(2)}, u32[]{:S(2)}) collective-permute-start(f32[2,2,2,128,128]{4,3,2,1,0:T(8,128)} %get-tuple-element.91.refs_0_), channel_id=1, source_target_pairs={{0,2},{2,0},{1,3},{3,1},{4,6},{6,4},{5,7},{7,5},{8,10},{10,8},{9,1... | collective-permute-start | bytes 1572872 | tf_op jit(solution)/shard_map/ppermute | solution.py:374
  199.3 21.2 %collective-permute-start.21 = (f32[2,2,128,128]{3,2,1,0:T(8,128)}, f32[2,2,128,128]{3,2,1,0:T(8,128)}, u32[]{:S(2)}, u32[]{:S(2)}) collective-permute-start(f32[2,2,128,128]{3,2,1,0:T(8,128)} %get-tuple-element.85), channel_id=1, source_target_pairs={{4,0},{5,1},{6,2},{7,3},{20,16},{21,17},{22,18},{23,19}} | collective-permute-start | bytes 786440 | tf_op jit(solution)/shard_map/ppermute | solution.py:440
  200.7 49.1 %collective-permute-start.26 = (f32[2,2,2,128,128]{4,3,2,1,0:T(8,128)}, f32[2,2,2,128,128]{4,3,2,1,0:T(8,128)}, u32[]{:S(2)}, u32[]{:S(2)}) collective-permute-start(f32[2,2,2,128,128]{4,3,2,1,0:T(8,128)} %copy-done.30), channel_id=1, source_target_pairs={{0,2},{2,0},{1,3},{3,1},{4,6},{6,4},{5,7},{7,5},{8,10},{10,8},{9,1... | collective-permute-start | bytes 1572872 | tf_op jit(solution)/shard_map/ppermute | solution.py:374
  209.1 44.9 %collective-permute-start.25 = (f32[2,2,2,128,128]{4,3,2,1,0:T(8,128)}, f32[2,2,2,128,128]{4,3,2,1,0:T(8,128)}, u32[]{:S(2)}, u32[]{:S(2)}) collective-permute-start(f32[2,2,2,128,128]{4,3,2,1,0:T(8,128)} %copy-done.32), channel_id=1, source_target_pairs={{0,2},{2,0},{1,3},{3,1},{4,6},{6,4},{5,7},{7,5},{8,10},{10,8},{9,1... | collective-permute-start | bytes 1572872 | tf_op jit(solution)/shard_map/ppermute | solution.py:374
  220.4 43.4 %collective-permute-start.24 = (f32[2,2,2,128,128]{4,3,2,1,0:T(8,128)}, f32[2,2,2,128,128]{4,3,2,1,0:T(8,128)}, u32[]{:S(2)}, u32[]{:S(2)}) collective-permute-start(f32[2,2,2,128,128]{4,3,2,1,0:T(8,128)} %copy-done.34), channel_id=1, source_target_pairs={{0,2},{2,0},{1,3},{3,1},{4,6},{6,4},{5,7},{7,5},{8,10},{10,8},{9,1... | collective-permute-start | bytes 1572872 | tf_op jit(solution)/shard_map/ppermute | solution.py:374
  220.5 48.9 %collective-permute-start.23 = (f32[2,2,2,128,128]{4,3,2,1,0:T(8,128)}, f32[2,2,2,128,128]{4,3,2,1,0:T(8,128)}, u32[]{:S(2)}, u32[]{:S(2)}) collective-permute-start(f32[2,2,2,128,128]{4,3,2,1,0:T(8,128)} %copy-done.36), channel_id=1, source_target_pairs={{0,2},{2,0},{1,3},{3,1},{4,6},{6,4},{5,7},{7,5},{8,10},{10,8},{9,1... | collective-permute-start | bytes 1572872 | tf_op jit(solution)/shard_map/ppermute | solution.py:374
  231.6 43.4 %collective-permute-start.22 = (f32[2,2,2,128,128]{4,3,2,1,0:T(8,128)}, f32[2,2,2,128,128]{4,3,2,1,0:T(8,128)}, u32[]{:S(2)}, u32[]{:S(2)}) collective-permute-start(f32[2,2,2,128,128]{4,3,2,1,0:T(8,128)} %get-tuple-element.86.refs_0_), channel_id=1, source_target_pairs={{0,2},{2,0},{1,3},{3,1},{4,6},{6,4},{5,7},{7,5},{8,10},{10,8},{9,1... | collective-permute-start | bytes 1572872 | tf_op jit(solution)/shard_map/ppermute | solution.py:374
  232.4 3.2 %copy-start.17 = (f32[2,2,656,768]{3,2,1,0:T(8,128)}, f32[2,2,656,768]{3,2,1,0:T(8,128)S(1)}, u32[]{:S(2)}) copy-start(f32[2,2,656,768]{3,2,1,0:T(8,128)S(1)} %blank_total.1.refs_1_) | copy-start | bytes 24182788
  236.9 3.3 %copy-start.18 = (f32[2,2,656,768]{3,2,1,0:T(8,128)S(1)}, f32[2,2,656,768]{3,2,1,0:T(8,128)}, u32[]{:S(2)}) copy-start(f32[2,2,656,768]{3,2,1,0:T(8,128)} %copy-done.17) | copy-start | bytes 24182788
  249.8 4.3 %copy-start.35 = (f32[2,2,2,128,128]{4,3,2,1,0:T(8,128)S(1)}, f32[2,2,2,128,128]{4,3,2,1,0:T(8,128)}, u32[]{:S(2)}) copy-start(f32[2,2,2,128,128]{4,3,2,1,0:T(8,128)} %copy-done.34) | copy-start | bytes 1572868
  251.3 12.5 %copy-start.37 = (f32[2,2,2,128,128]{4,3,2,1,0:T(8,128)S(1)}, f32[2,2,2,128,128]{4,3,2,1,0:T(8,128)}, u32[]{:S(2)}) copy-start(f32[2,2,2,128,128]{4,3,2,1,0:T(8,128)} %copy-done.36) | copy-start | bytes 1572868
  275.0 3.3 %copy-start.20 = (f32[2,2,656,768]{3,2,1,0:T(8,128)S(1)}, f32[2,2,656,768]{3,2,1,0:T(8,128)}, u32[]{:S(2)}) copy-start(f32[2,2,656,768]{3,2,1,0:T(8,128)} %copy-done.19) | copy-start | bytes 24182788
  283.0 3.3 %copy-start.22 = (f32[2,2,656,768]{3,2,1,0:T(8,128)S(1)}, f32[2,2,656,768]{3,2,1,0:T(8,128)}, u32[]{:S(2)}) copy-start(f32[2,2,656,768]{3,2,1,0:T(8,128)} %copy-done.21) | copy-start | bytes 24182788
  286.6 4.6 %collective-permute-start.33 = (f32[2,2,192,768]{3,2,1,0:T(8,128)S(1)}, f32[2,2,192,768]{3,2,1,0:T(8,128)S(1)}, u32[]{:S(2)}, u32[]{:S(2)}) collective-permute-start(f32[2,2,192,768]{3,2,1,0:T(8,128)S(1)} %bitcast.67), channel_id=1, source_target_pairs={{0,1},{1,0},{2,3},{3,2},{4,5},{5,4},{6,7},{7,6},{8,9},{9,8},{10,11... | collective-permute-start | bytes 7077896 | tf_op jit(solution)/shard_map/ppermute | solution.py:374
  (28 other events, 50.9 us)

commit v3 on v2

--- a/solution.py
+++ b/solution.py
@@ -12,7 +12,7 @@
 
 FRESNEL = 8.0
 LAG = 1
-SCOPED = 16 << 20
+SCOPED = 4 << 20
 F32 = jnp.float32
 BF16 = jnp.bfloat16
 HBM = pl.BlockSpec(memory_space=pl.ANY)
@@ -95,14 +95,15 @@
     return a[0] * b[0] + a[1] * b[1], a[1] * b[0] - a[0] * b[1]
 
 
-def cut_kernel(pixels, corners, lat, own, other, out, seen, window, sems):
+def cut_kernel(pixels, begin, corners, lat, own, other, unused, out, window, sems):
     half = own.shape[2]
     width = own.shape[3]
     tall = pixels + 8
     step = pl.program_id(0)
     steps = pl.num_programs(0)
 
-    def places(probe):
+    def places(step):
+        probe = begin + step
         row = corners[2 * probe]
         column = corners[2 * probe + 1]
         row0 = jnp.minimum(row // 8 * 8, 2 * half - tall)
@@ -114,8 +115,8 @@
         offset = jnp.where(top, row0 - top_from, tall)
         return top, bottom, top_from, bottom_from, offset, row - row0, col0, column - col0
 
-    def copies(probe, slot, act):
-        top, bottom, top_from, bottom_from, _, _, col0, _ = places(probe)
+    def copies(step, slot, act):
+        top, bottom, top_from, bottom_from, _, _, col0, _ = places(step)
         own_top = lat[0] == 0
         col0 = pl.multiple_of(col0, pixels)
         for source, is_top, sem in ((own, own_top, 0), (other, jnp.logical_not(own_top), 1)):
@@ -146,6 +147,7 @@
     *_, offset, down, _, shift = places(step)
     offset = pl.multiple_of(offset, 8)
     turn = (pixels - shift) % pixels
+    probe = begin + step
     lane = lax.broadcasted_iota(jnp.int32, (tall, pixels), 1)
     for part in range(own.shape[0]):
         for layer in range(own.shape[1]):
@@ -154,35 +156,44 @@
             near = pltpu.roll(near, turn, 1)
             far = pltpu.roll(far, turn, 1)
             patch = jnp.where(lane < pixels - shift, near, far)
-            out[step // out.shape[1], step % out.shape[1], layer, part] = pltpu.roll(patch, (tall - down) % tall, 0)[:pixels]
-
-
-def cut_patches(own, other, corners, lat, pixels, count):
-    probes = corners.shape[0]
-    parts, layers = own.shape[:2]
-    groups = probes // count
-    stack = (count, layers, parts, pixels, pixels)
-    return pl.pallas_call(
-        functools.partial(cut_kernel, pixels),
+            out[probe // out.shape[1], probe % out.shape[1], layer, part] = pltpu.roll(patch, (tall - down) % tall, 0)[:pixels]
+
+
+def cut_patches(own, other, corners, lat, patches, begin, end):
+    _, _, layers, parts, pixels, _ = patches.shape
+    size = (end - begin) * layers * parts * pixels * pixels
+    return pl.pallas_call(
+        functools.partial(cut_kernel, pixels, begin),
         grid_spec=pltpu.PrefetchScalarGridSpec(
             num_scalar_prefetch=2,
-            grid=(probes,),
-            in_specs=[HBM, HBM],
-            out_specs=[VMEM, VMEM],
+            grid=(end - begin,),
+            in_specs=[HBM, HBM, VMEM],
+            out_specs=VMEM,
             scratch_shapes=[
                 pltpu.VMEM((2, parts, layers, 2 * (pixels + 8), 2 * pixels), F32),
                 pltpu.SemaphoreType.DMA((2, 2)),
             ],
         ),
-        out_shape=[pltpu.VMEM((groups,) + stack, F32), pltpu.VMEM((groups,) + stack, F32)],
-        compiler_params=pltpu.CompilerParams(vmem_limit_bytes=16 << 20),
-        cost_estimate=pl.CostEstimate(
-            flops=probes * layers * parts * pixels * pixels * 4,
-            bytes_accessed=probes * layers * parts * pixels * pixels * 12,
-            transcendentals=0,
-        ),
+        out_shape=pltpu.VMEM(patches.shape, F32),
+        input_output_aliases={4: 0},
+        compiler_params=pltpu.CompilerParams(vmem_limit_bytes=8 << 20),
+        cost_estimate=pl.CostEstimate(flops=size * 4, bytes_accessed=size * 12, transcendentals=0),
         name="cut_patches",
-    )(corners.reshape(-1), lat.reshape(1), in_hbm(own), in_hbm(other))
+    )(corners.reshape(-1), lat.reshape(1), in_hbm(own), in_hbm(other), in_vmem(patches))
+
+
+def rooms_kernel(patches, seen, total):
+    total[...] = jnp.zeros(total.shape, F32)
+
+
+def make_rooms(stack, total):
+    return pl.pallas_call(
+        rooms_kernel,
+        out_specs=[VMEM] * 3,
+        out_shape=[pltpu.VMEM(stack, F32), pltpu.VMEM(stack, F32), pltpu.VMEM(total, F32)],
+        compiler_params=pltpu.CompilerParams(vmem_limit_bytes=SCOPED),
+        name="make_rooms",
+    )()
 
 
 def forward_kernel(scalars, patches, arrived, start_wave, frames, tables, unused, leave, seen):
@@ -273,20 +284,6 @@
     )(scalars, *map(in_vmem, (patches, arrived, own, seen, tables)))
 
 
-def clear_kernel(total):
-    total[...] = jnp.zeros(total.shape, F32)
-
-
-def blank_total(parts, layers, rows, width, pixels):
-    return pl.pallas_call(
-        clear_kernel,
-        out_specs=VMEM,
-        out_shape=pltpu.VMEM((parts, layers, rows + 2 * (pixels + 8), width), F32),
-        compiler_params=pltpu.CompilerParams(vmem_limit_bytes=SCOPED),
-        name="blank_total",
-    )()
-
-
 def deposit_kernel(height, scalars, corners, sources, unused, total):
     pixels = sources[0].shape[-1]
     tall = pixels + 8
@@ -391,16 +388,18 @@
     count = 2 if probes % 2 == 0 else 1
     groups = probes // count
     wave = (count, parts, pixels, pixels)
-    patches, seen = cut_patches(specimen, other, corners, lat, pixels, count)
     measured = frames.reshape((groups, count, pixels, pixels))
     if paired:
         both = jnp.stack([corners, swap(corners, "probe")])
         base = lax.axis_index("probe") * (height // 2)
-        total = blank_total(parts, layers, height // 2, width, pixels)
     else:
         both = corners[None]
         base = jnp.int32(0)
-        total = blank_total(parts, layers, height, width, pixels)
+    rows = height // 2 if paired else height
+    patches, seen, total = make_rooms(
+        (groups, count, layers, parts, pixels, pixels), (parts, layers, rows + 2 * (pixels + 8), width)
+    )
+    patches = cut_patches(specimen, other, corners, lat, patches, 0, count)
 
     is_first = (section == 0).astype(jnp.int32)
     is_last = (section == sections - 1).astype(jnp.int32)
@@ -430,6 +429,8 @@
             pairs = pairs_of(tick, 1)
             if pairs:
                 down[tick] = lax.ppermute(leaving, "depth", pairs)
+            if tick == 0:
+                patches = cut_patches(specimen, other, corners, lat, patches, count, probes)
         if tick >= depth:
             scalars = scalars_of(tick - LAG * (2 * (sections - 1) - section))
             rising, grads = run_backward(
@@ -446,6 +447,10 @@
                     ats.append(across[1])
                 across = (swap(grads, "probe"), scalars[:2])
             total = deposit(jnp.concatenate([base[None], *ats]), both, sources, total, height)
+            if tick in down:
+                total, down[tick] = lax.optimization_barrier((total, down[tick]))
+            elif tick in up:
+                total, up[tick] = lax.optimization_barrier((total, up[tick]))
     if paired:
         scalars = jnp.concatenate([base[None], across[1]])
         total = deposit(scalars, both[1:], [across[0]], total, height)

time: 295 us -> 269 us (0.912)
  waiting for transfers between devices: 94.2 us -> 28.4 us
  local copies, waits for them, and re-layouts: 61.2 us -> 90.9 us
  Pallas kernels: 67.4 us -> 77.3 us
  starting transfers between devices: 65.1 us -> 60.5 us
  other arithmetic: 4.24 us -> 8.27 us
    ppermute x14, waiting for transfers between devices: 48.2 us -> 8.44 us  [swap(): return lax.ppermute(shard, axis, [(0, 1), (1, 0)])]
    unnamed x85 -> x153, local copies, waits for them, and re-layouts: 59.4 us -> 82.6 us
    ppermute x10, waiting for transfers between devices: 24.1 us -> 7.34 us  [local(): down[tick] = lax.ppermute(leaving, 'depth', pairs)]
    ppermute x10, waiting for transfers between devices: 21.8 us -> 12.6 us  [local(): up[tick] = lax.ppermute(rising, 'depth', pairs)]
    pallas_call x11, Pallas kernels: 19.9 us -> 24.9 us  [run_backward(): pl.pallas_call(backward_kernel, in_specs=[SMEM] + [VMEM] * 5, out_specs=[...]
    ppermute x14, starting transfers between devices: 16.4 us -> 12 us  [swap(): return lax.ppermute(shard, axis, [(0, 1), (1, 0)])]
    pallas_call x11, Pallas kernels: 16.8 us -> 20.7 us  [run_forward(): pl.pallas_call(forward_kernel, in_specs=[SMEM] + [VMEM] * 6, out_specs=[V...]
    concatenate x10, local copies, waits for them, and re-layouts: 0.84 us -> 4.14 us  [local(): jnp.concatenate([base[None], *ats])]
  transfers between devices with their start and end apart: 34 -> 34, of which waited for: 22 -> 9; matrix products, arithmetic and copies ran while one was open for 2% -> 6% of each run, Pallas kernels for 16% -> 26%
where the time goes in v3:
time: 269 us; the launch traced here: 266 us
  local copies, waits for them, and re-layouts  90.9 us (34%)
  Pallas kernels  77.3 us (29%)
  starting transfers between devices  60.5 us (22%)
  waiting for transfers between devices  28.4 us (11%)
  other arithmetic  8.27 us (3%)
    unnamed x153, local copies, waits for them, and re-layouts  82.6 us
    ppermute x10, starting transfers between devices, local(): down[tick] = lax.ppermute(leaving, 'depth', pairs)  36 us
    pallas_call x11, Pallas kernels, run_backward(): pl.pallas_call(backward_kernel, in_specs=[SMEM] + [VMEM] * 5, out_specs=[...  24.9 us
    pallas_call x11, Pallas kernels, run_forward(): pl.pallas_call(forward_kernel, in_specs=[SMEM] + [VMEM] * 6, out_specs=[V...  20.7 us
    pallas_call x12, Pallas kernels, deposit(): pl.pallas_call(body, in_specs=[SMEM] * 2 + [VMEM] * (n + 1), out_specs=VM...  16.8 us
    pallas_call x2, Pallas kernels, cut_patches(): pl.pallas_call(functools.partial(cut_kernel, pixels, begin), grid_spec=pl...  14 us
    ppermute x10, waiting for transfers between devices, local(): up[tick] = lax.ppermute(rising, 'depth', pairs)  12.6 us
    ppermute x10, starting transfers between devices, local(): up[tick] = lax.ppermute(rising, 'depth', pairs)  12.5 us
  transfers between devices with their start and end apart: 34, of which 9 were waited for; matrix products, arithmetic and copies ran while one was open for 6% of the time, Pallas kernels for 26%

profile of v3, /device:TPU:0, one launch (start us, length us, event | category | flops | bytes accessed | tf_op | source)
XLA Modules:
  0.0 266.3 jit_solution(976972401066964821)
XLA Ops:
  5.0 3.2 %copy-done.36 = f32[2,2,656,768]{3,2,1,0:T(8,128)} copy-done((f32[2,2,656,768]{3,2,1,0:T(8,128)}, f32[2,2,656,768]{3,2,1,0:T(8,128)S(1)}, u32[]{:S(2)}) %copy-start.36) | copy-done | bytes 8060952
  12.3 2.2 copy-done.1
  14.4 2.5 cut_patches.2.unused.patches
  19.1 2.2 copy-done.3
  25.1 3.2 %collective-permute-start.2 = (f32[2,2,128,128]{3,2,1,0:T(8,128)S(1)}, f32[2,2,128,128]{3,2,1,0:T(8,128)S(1)}, u32[]{:S(2)}, u32[]{:S(2)}) collective-permute-start(f32[2,2,128,128]{3,2,1,0:T(8,128)S(1)} %get-tuple-element.75), channel_id=1, source_target_pairs={{0,4},{1,5},{2,6},{3,7},{16,20},{17,21},{18,22},{19,23}} | collective-permute-start | bytes 786440 | tf_op jit(solution)/shard_map/ppermute | solution.py:431
  28.3 2.2 copy-done.4
  30.5 11.5 %cut_patches.3.patches = f32[8,2,2,2,128,128]{5,4,3,2,1,0:T(8,128)S(1)} custom-call(s32[32]{0:T(128)S(1)} %reshape.14.corners, s32[1]{0:T(128)} %bitcast.lat, f32[2,2,384,768]{3,2,1,0:T(8,128)} %own.3, f32[2,2,384,768]{3,2,1,0:T(8,128)} %collective-permute-done.1.other, f32[8,2,2,2,128,128]{5,4,3,2,1,0:T(8,128)S(1)} %copy-done.4), custom_call_target="tpu_custom_call", output_to_operand_aliasing={{}: (4, {})} | custom-call | flops 3670016 | bytes 11010048 | tf_op jit(solution)/shard_map/cut_patches/pallas_call | solution.py:165
  44.1 2.2 copy-done.6
  51.5 5.9 %collective-permute-done.3.arrived = f32[2,2,128,128]{3,2,1,0:T(8,128)S(1)} collective-permute-done((f32[2,2,128,128]{3,2,1,0:T(8,128)S(1)}, f32[2,2,128,128]{3,2,1,0:T(8,128)S(1)}, u32[]{:S(2)}, u32[]{:S(2)}) %collective-permute-start.3) | collective-permute-done | bytes 262176 | tf_op jit(solution)/shard_map/ppermute | solution.py:431
  57.4 2.2 copy-done.7
  59.6 2.2 copy-done.21
  65.6 4.4 %collective-permute-start.4 = (f32[2,2,128,128]{3,2,1,0:T(8,128)S(1)}, f32[2,2,128,128]{3,2,1,0:T(8,128)S(1)}, u32[]{:S(2)}, u32[]{:S(2)}) collective-permute-start(f32[2,2,128,128]{3,2,1,0:T(8,128)S(1)} %get-tuple-element.79), channel_id=1, source_target_pairs={{0,4},{4,8},{8,12},{1,5},{5,9},{9,13},{2,6},{6,10},{10,14},{3,7},{... | collective-permute-start | bytes 786440 | tf_op jit(solution)/shard_map/ppermute | solution.py:431
  75.1 2.2 copy-done.8
  77.3 2.2 copy-done.23
  81.4 4.4 %collective-permute-start.6 = (f32[2,2,128,128]{3,2,1,0:T(8,128)S(1)}, f32[2,2,128,128]{3,2,1,0:T(8,128)S(1)}, u32[]{:S(2)}, u32[]{:S(2)}) collective-permute-start(f32[2,2,128,128]{3,2,1,0:T(8,128)S(1)} %get-tuple-element.81.own), channel_id=1, source_target_pairs={{0,4},{4,8},{8,12},{1,5},{5,9},{9,13},{2,6},{6,10},{10,14},{3,7},{... | collective-permute-start | bytes 786440 | tf_op jit(solution)/shard_map/ppermute | solution.py:431
  87.1 2.1 collective-permute-start.8
  94.0 3.3 %copy-done.37 = f32[2,2,656,768]{3,2,1,0:T(8,128)S(1)} copy-done((f32[2,2,656,768]{3,2,1,0:T(8,128)S(1)}, f32[2,2,656,768]{3,2,1,0:T(8,128)}, u32[]{:S(2)}) %copy-start.37) | copy-done | bytes 8060952
  98.8 2.3 copy-done.9
  101.0 3.2 %copy-done.25 = f32[8,2,2,2,128,128]{5,4,3,2,1,0:T(8,128)S(1)} copy-done((f32[8,2,2,2,128,128]{5,4,3,2,1,0:T(8,128)S(1)}, f32[8,2,2,2,128,128]{5,4,3,2,1,0:T(8,128)}, u32[]{:S(2)}) %copy-start.25) | copy-done | bytes 4194328
  106.2 2.2 collective-permute-start.9
  113.0 3.2 %forward_section.16 = (f32[2,2,128,128]{3,2,1,0:T(8,128)}, f32[8,2,2,2,128,128]{5,4,3,2,1,0:T(8,128)S(1)}) custom-call(s32[4]{0:T(128)S(1)} %get-tuple-element.147.scalars, f32[8,2,2,2,128,128]{5,4,3,2,1,0:T(8,128)S(1)} %copy-done.9, f32[2,2,128,128]{3,2,1,0:T(8,128)S(1)} %collective-permute-done.9.arrived, ...), custom_call_target="tpu_custom_call", output_to_operand_aliasing={{1}: (6, {})} | custom-call | flops 402653184 | bytes 1572864 | tf_op jit(solution)/shard_map/forward_section/pallas_call | solution.py:262
  116.3 4.4 %collective-permute-start.12 = (f32[2,2,128,128]{3,2,1,0:T(8,128)}, f32[2,2,128,128]{3,2,1,0:T(8,128)}, u32[]{:S(2)}, u32[]{:S(2)}) collective-permute-start(f32[2,2,128,128]{3,2,1,0:T(8,128)} %get-tuple-element.93.own), channel_id=1, source_target_pairs={{0,4},{4,8},{8,12},{1,5},{5,9},{9,13},{2,6},{6,10},{10,14},{3,7},{... | collective-permute-start | bytes 786440 | tf_op jit(solution)/shard_map/ppermute | solution.py:431
  125.3 3.4 %copy-done.41 = f32[2,2,656,768]{3,2,1,0:T(8,128)S(1)} copy-done((f32[2,2,656,768]{3,2,1,0:T(8,128)S(1)}, f32[2,2,656,768]{3,2,1,0:T(8,128)}, u32[]{:S(2)}) %copy-start.41) | copy-done | bytes 8060952
  131.4 2.7 %forward_section.17 = (f32[2,2,128,128]{3,2,1,0:T(8,128)S(1)}, f32[8,2,2,2,128,128]{5,4,3,2,1,0:T(8,128)S(1)}) custom-call(s32[4]{0:T(128)S(1)} %copy-done.70, f32[8,2,2,2,128,128]{5,4,3,2,1,0:T(8,128)S(1)} %copy-done.10, f32[2,2,128,128]{3,2,1,0:T(8,128)} %collective-permute-done.12.arrived, ...), custom_call_target="tpu_custom_call", output_to_operand_aliasing={{1}: (6, {})} | custom-call | flops 402653184 | bytes 1572864 | tf_op jit(solution)/shard_map/forward_section/pallas_call | solution.py:262
  134.6 8.2 %collective-permute-start.15 = (f32[2,2,128,128]{3,2,1,0:T(8,128)S(1)}, f32[2,2,128,128]{3,2,1,0:T(8,128)S(1)}, u32[]{:S(2)}, u32[]{:S(2)}) collective-permute-start(f32[2,2,128,128]{3,2,1,0:T(8,128)S(1)} %get-tuple-element.99.own), channel_id=1, source_target_pairs={{0,4},{4,8},{8,12},{1,5},{5,9},{9,13},{2,6},{6,10},{10,14},{3,7},{... | collective-permute-start | bytes 786440 | tf_op jit(solution)/shard_map/ppermute | solution.py:431
  142.9 2.4 backward_section.14
  149.0 3.2 %forward_section.18 = (f32[2,2,128,128]{3,2,1,0:T(8,128)}, f32[8,2,2,2,128,128]{5,4,3,2,1,0:T(8,128)S(1)}) custom-call(s32[4]{0:T(128)S(1)} %get-tuple-element.149.scalars, f32[8,2,2,2,128,128]{5,4,3,2,1,0:T(8,128)S(1)} %copy-done.10, f32[2,2,128,128]{3,2,1,0:T(8,128)S(1)} %collective-permute-done.15.arrived, ...), custom_call_target="tpu_custom_call", output_to_operand_aliasing={{1}: (6, {})} | custom-call | flops 402653184 | bytes 1572864 | tf_op jit(solution)/shard_map/forward_section/pallas_call | solution.py:262
  152.2 6.7 %collective-permute-start.18 = (f32[2,2,128,128]{3,2,1,0:T(8,128)}, f32[2,2,128,128]{3,2,1,0:T(8,128)}, u32[]{:S(2)}, u32[]{:S(2)}) collective-permute-start(f32[2,2,128,128]{3,2,1,0:T(8,128)} %get-tuple-element.105.own), channel_id=1, source_target_pairs={{0,4},{4,8},{8,12},{1,5},{5,9},{9,13},{2,6},{6,10},{10,14},{3,7},{... | collective-permute-start | bytes 786440 | tf_op jit(solution)/shard_map/ppermute | solution.py:431
  159.0 3.0 %backward_section.15 = (f32[2,2,128,128]{3,2,1,0:T(8,128)}, f32[2,2,2,128,128]{4,3,2,1,0:T(8,128)S(1)}) custom-call(s32[4]{0:T(128)S(1)} %add_add_fusion.6.scalars, f32[8,2,2,2,128,128]{5,4,3,2,1,0:T(8,128)S(1)} %copy-done.10, f32[2,2,128,128]{3,2,1,0:T(8,128)S(1)} %collective-permute-done.13.arrived, f32[2,2,128,128]{3,2,1,0:T(8,128)} %get-tuple-element.105.own, ...), custom_call_target="tpu_custom_call" | custom-call | flops 402653184 | bytes 1572864 | tf_op jit(solution)/shard_map/backward_section/pallas_call | solution.py:276
  165.7 3.4 %copy-done.45 = f32[2,2,656,768]{3,2,1,0:T(8,128)S(1)} copy-done((f32[2,2,656,768]{3,2,1,0:T(8,128)S(1)}, f32[2,2,656,768]{3,2,1,0:T(8,128)}, u32[]{:S(2)}) %copy-start.45) | copy-done | bytes 8060952
  176.4 2.4 backward_section.16
  183.7 2.7 %copy-done.48 = f32[2,2,656,768]{3,2,1,0:T(8,128)} copy-done((f32[2,2,656,768]{3,2,1,0:T(8,128)}, f32[2,2,656,768]{3,2,1,0:T(8,128)S(1)}, u32[]{:S(2)}) %copy-start.48) | copy-done | bytes 8060952
  187.1 3.9 %collective-permute-done.19.arrived = f32[2,2,128,128]{3,2,1,0:T(8,128)S(1)} collective-permute-done((f32[2,2,128,128]{3,2,1,0:T(8,128)S(1)}, f32[2,2,128,128]{3,2,1,0:T(8,128)S(1)}, u32[]{:S(2)}, u32[]{:S(2)}) %collective-permute-start.19) | collective-permute-done | bytes 262176 | tf_op jit(solution)/shard_map/ppermute | solution.py:441
  191.0 2.7 %backward_section.17 = (f32[2,2,128,128]{3,2,1,0:T(8,128)}, f32[2,2,2,128,128]{4,3,2,1,0:T(8,128)}) custom-call(s32[4]{0:T(128)S(1)} %add_add_fusion.4.scalars, f32[8,2,2,2,128,128]{5,4,3,2,1,0:T(8,128)S(1)} %copy-done.11, f32[2,2,128,128]{3,2,1,0:T(8,128)S(1)} %collective-permute-done.19.arrived, f32[2,2,128,128]{3,2,1,0:T(8,128)S(1)} %get-tuple-element.117.own, ...), custom_call_target="tpu_custom_call" | custom-call | flops 402653184 | bytes 1572864 | tf_op jit(solution)/shard_map/backward_section/pallas_call | solution.py:276
  196.1 3.4 %copy-done.49 = f32[2,2,656,768]{3,2,1,0:T(8,128)S(1)} copy-done((f32[2,2,656,768]{3,2,1,0:T(8,128)S(1)}, f32[2,2,656,768]{3,2,1,0:T(8,128)}, u32[]{:S(2)}) %copy-start.49) | copy-done | bytes 8060952
  203.5 2.6 copy-done.50
  206.2 2.4 backward_section.18
  211.4 3.4 %copy-done.51 = f32[2,2,656,768]{3,2,1,0:T(8,128)S(1)} copy-done((f32[2,2,656,768]{3,2,1,0:T(8,128)S(1)}, f32[2,2,656,768]{3,2,1,0:T(8,128)}, u32[]{:S(2)}) %copy-start.51) | copy-done | bytes 8060952
  214.9 2.6 deposit_patches.19.refs_2_
  218.9 2.5 backward_section.19
  223.6 3.4 %copy-done.53 = f32[2,2,656,768]{3,2,1,0:T(8,128)S(1)} copy-done((f32[2,2,656,768]{3,2,1,0:T(8,128)S(1)}, f32[2,2,656,768]{3,2,1,0:T(8,128)}, u32[]{:S(2)}) %copy-start.53) | copy-done | bytes 8060952
  228.5 5.4 %collective-permute-done.28.arrived = f32[2,2,128,128]{3,2,1,0:T(8,128)} collective-permute-done((f32[2,2,128,128]{3,2,1,0:T(8,128)}, f32[2,2,128,128]{3,2,1,0:T(8,128)}, u32[]{:S(2)}, u32[]{:S(2)}) %collective-permute-start.28) | collective-permute-done | bytes 262176 | tf_op jit(solution)/shard_map/ppermute | solution.py:441
  233.9 3.0 %backward_section.20 = (f32[2,2,128,128]{3,2,1,0:T(8,128)}, f32[2,2,2,128,128]{4,3,2,1,0:T(8,128)S(1)}) custom-call(s32[4]{0:T(128)S(1)} %get-tuple-element.142.scalars, f32[8,2,2,2,128,128]{5,4,3,2,1,0:T(8,128)S(1)} %copy-done.14, f32[2,2,128,128]{3,2,1,0:T(8,128)} %collective-permute-done.28.arrived, f32[2,2,128,128]{3,2,1,0:T(8,128)S(1)} %broadcast_in_dim.5.arrived.own, ...), custom_call_target="tpu_custom_call" | custom-call | flops 402653184 | bytes 1572864 | tf_op jit(solution)/shard_map/backward_section/pallas_call | solution.py:276
  238.9 3.6 %copy-done.55 = f32[2,2,656,768]{3,2,1,0:T(8,128)S(1)} copy-done((f32[2,2,656,768]{3,2,1,0:T(8,128)S(1)}, f32[2,2,656,768]{3,2,1,0:T(8,128)}, u32[]{:S(2)}) %copy-start.55) | copy-done | bytes 8060952
  245.5 3.2 %backward_section.21 = (f32[2,2,128,128]{3,2,1,0:T(8,128)}, f32[2,2,2,128,128]{4,3,2,1,0:T(8,128)S(1)}) custom-call(s32[4]{0:T(128)S(1)} %get-tuple-element.141.scalars, f32[8,2,2,2,128,128]{5,4,3,2,1,0:T(8,128)S(1)} %copy-done.15, f32[2,2,128,128]{3,2,1,0:T(8,128)} %collective-permute-done.30.arrived, f32[2,2,128,128]{3,2,1,0:T(8,128)S(1)} %broadcast_in_dim.5.arrived.own, ...), custom_call_target="tpu_custom_call" | custom-call | flops 402653184 | bytes 1572864 | tf_op jit(solution)/shard_map/backward_section/pallas_call | solution.py:276
  251.8 3.3 %copy-done.57 = f32[2,2,656,768]{3,2,1,0:T(8,128)S(1)} copy-done((f32[2,2,656,768]{3,2,1,0:T(8,128)S(1)}, f32[2,2,656,768]{3,2,1,0:T(8,128)}, u32[]{:S(2)}) %copy-start.57) | copy-done | bytes 8060952
  256.2 2.5 collective-permute-done.31.refs_0_
  260.0 4.5 %collective-permute-done.33 = f32[2,2,192,768]{3,2,1,0:T(8,128)S(1)} collective-permute-done((f32[2,2,192,768]{3,2,1,0:T(8,128)S(1)}, f32[2,2,192,768]{3,2,1,0:T(8,128)S(1)}, u32[]{:S(2)}, u32[]{:S(2)}) %collective-permute-start.33) | collective-permute-done | bytes 2359328 | tf_op jit(solution)/shard_map/ppermute | solution.py:371
  (250 shorter events, 101.3 us)
Async XLA Ops:
  0.0 12.2 %collective-permute-start.1 = (f32[2,2,384,768]{3,2,1,0:T(8,128)}, f32[2,2,384,768]{3,2,1,0:T(8,128)}, u32[]{:S(2)}, u32[]{:S(2)}) collective-permute-start(f32[2,2,384,768]{3,2,1,0:T(8,128)} %own.3), channel_id=1, source_target_pairs={{0,1},{1,0},{2,3},{3,2},{4,5},{5,4},{6,7},{7,6},{8,9},{9,8},{10,11... | collective-permute-start | bytes 14155784 | tf_op jit(solution)/shard_map/ppermute | solution.py:371
  25.1 19.0 %collective-permute-start.2 = (f32[2,2,128,128]{3,2,1,0:T(8,128)S(1)}, f32[2,2,128,128]{3,2,1,0:T(8,128)S(1)}, u32[]{:S(2)}, u32[]{:S(2)}) collective-permute-start(f32[2,2,128,128]{3,2,1,0:T(8,128)S(1)} %get-tuple-element.75), channel_id=1, source_target_pairs={{0,4},{1,5},{2,6},{3,7},{16,20},{17,21},{18,22},{19,23}} | collective-permute-start | bytes 786440 | tf_op jit(solution)/shard_map/ppermute | solution.py:431
  30.5 13.6 %copy-start.19 = (f32[8,2,2,2,128,128]{5,4,3,2,1,0:T(8,128)S(1)}, f32[8,2,2,2,128,128]{5,4,3,2,1,0:T(8,128)}, u32[]{:S(2)}) copy-start(f32[8,2,2,2,128,128]{5,4,3,2,1,0:T(8,128)} %copy-done.18) | copy-start | bytes 12582916
  50.1 7.3 %collective-permute-start.3 = (f32[2,2,128,128]{3,2,1,0:T(8,128)S(1)}, f32[2,2,128,128]{3,2,1,0:T(8,128)S(1)}, u32[]{:S(2)}, u32[]{:S(2)}) collective-permute-start(f32[2,2,128,128]{3,2,1,0:T(8,128)S(1)} %get-tuple-element.77), channel_id=1, source_target_pairs={{0,4},{4,8},{1,5},{5,9},{2,6},{6,10},{3,7},{7,11},{16,20},{20,24},... | collective-permute-start | bytes 786440 | tf_op jit(solution)/shard_map/ppermute | solution.py:431
  65.6 9.6 %collective-permute-start.4 = (f32[2,2,128,128]{3,2,1,0:T(8,128)S(1)}, f32[2,2,128,128]{3,2,1,0:T(8,128)S(1)}, u32[]{:S(2)}, u32[]{:S(2)}) collective-permute-start(f32[2,2,128,128]{3,2,1,0:T(8,128)S(1)} %get-tuple-element.79), channel_id=1, source_target_pairs={{0,4},{4,8},{8,12},{1,5},{5,9},{9,13},{2,6},{6,10},{10,14},{3,7},{... | collective-permute-start | bytes 786440 | tf_op jit(solution)/shard_map/ppermute | solution.py:431
  70.0 20.5 %collective-permute-start = (s32[16,2]{1,0:T(8,128)}, s32[16,2]{1,0:T(8,128)S(1)}, u32[]{:S(2)}, u32[]{:S(2)}) collective-permute-start(s32[16,2]{1,0:T(8,128)} %gather_fusion), channel_id=1, source_target_pairs={{0,2},{2,0},{1,3},{3,1},{4,6},{6,4},{5,7},{7,5},{8,10},{10,8},{9,1... | collective-permute-start | bytes 392 | tf_op jit(solution)/shard_map/ppermute | solution.py:371
  81.4 17.4 %collective-permute-start.6 = (f32[2,2,128,128]{3,2,1,0:T(8,128)S(1)}, f32[2,2,128,128]{3,2,1,0:T(8,128)S(1)}, u32[]{:S(2)}, u32[]{:S(2)}) collective-permute-start(f32[2,2,128,128]{3,2,1,0:T(8,128)S(1)} %get-tuple-element.81.own), channel_id=1, source_target_pairs={{0,4},{4,8},{8,12},{1,5},{5,9},{9,13},{2,6},{6,10},{10,14},{3,7},{... | collective-permute-start | bytes 786440 | tf_op jit(solution)/shard_map/ppermute | solution.py:431
  87.1 24.2 %collective-permute-start.8 = (f32[2,2,2,128,128]{4,3,2,1,0:T(8,128)S(1)}, f32[2,2,2,128,128]{4,3,2,1,0:T(8,128)}, u32[]{:S(2)}, u32[]{:S(2)}) collective-permute-start(f32[2,2,2,128,128]{4,3,2,1,0:T(8,128)S(1)} %get-tuple-element.84.refs_0_), channel_id=1, source_target_pairs={{0,2},{2,0},{1,3},{3,1},{4,6},{6,4},{5,7},{7,5},{8,10},{10,8},{9,1... | collective-permute-start | bytes 1572872 | tf_op jit(solution)/shard_map/ppermute | solution.py:371
  90.6 17.9 %collective-permute-start.5 = (f32[2,2,128,128]{3,2,1,0:T(8,128)}, f32[2,2,128,128]{3,2,1,0:T(8,128)}, u32[]{:S(2)}, u32[]{:S(2)}) collective-permute-start(f32[2,2,128,128]{3,2,1,0:T(8,128)} %copy-done.73), channel_id=1, source_target_pairs={{12,8},{13,9},{14,10},{15,11},{28,24},{29,25},{30,26},{31,27}} | collective-permute-start | bytes 786440 | tf_op jit(solution)/shard_map/ppermute | solution.py:441
  98.8 7.4 %copy-start.38 = (f32[2,2,656,768]{3,2,1,0:T(8,128)}, f32[2,2,656,768]{3,2,1,0:T(8,128)S(1)}, u32[]{:S(2)}) copy-start(f32[2,2,656,768]{3,2,1,0:T(8,128)S(1)} %deposit_patches.12.refs_2_) | copy-start | bytes 24182788
  106.2 6.9 %collective-permute-start.9 = (f32[2,2,128,128]{3,2,1,0:T(8,128)S(1)}, f32[2,2,128,128]{3,2,1,0:T(8,128)S(1)}, u32[]{:S(2)}, u32[]{:S(2)}) collective-permute-start(f32[2,2,128,128]{3,2,1,0:T(8,128)S(1)} %get-tuple-element.87.own), channel_id=1, source_target_pairs={{0,4},{4,8},{8,12},{1,5},{5,9},{9,13},{2,6},{6,10},{10,14},{3,7},{... | collective-permute-start | bytes 786440 | tf_op jit(solution)/shard_map/ppermute | solution.py:431
  109.6 11.2 %collective-permute-start.7 = (f32[2,2,128,128]{3,2,1,0:T(8,128)S(1)}, f32[2,2,128,128]{3,2,1,0:T(8,128)S(1)}, u32[]{:S(2)}, u32[]{:S(2)}) collective-permute-start(f32[2,2,128,128]{3,2,1,0:T(8,128)S(1)} %get-tuple-element.89), channel_id=1, source_target_pairs={{8,4},{12,8},{9,5},{13,9},{10,6},{14,10},{11,7},{15,11},{24,20},{2... | collective-permute-start | bytes 786440 | tf_op jit(solution)/shard_map/ppermute | solution.py:441
  110.4 14.9 %collective-permute-start.11 = (f32[2,2,2,128,128]{4,3,2,1,0:T(8,128)S(1)}, f32[2,2,2,128,128]{4,3,2,1,0:T(8,128)}, u32[]{:S(2)}, u32[]{:S(2)}) collective-permute-start(f32[2,2,2,128,128]{4,3,2,1,0:T(8,128)S(1)} %get-tuple-element.90.refs_0_), channel_id=1, source_target_pairs={{0,2},{2,0},{1,3},{3,1},{4,6},{6,4},{5,7},{7,5},{8,10},{10,8},{9,1... | collective-permute-start | bytes 1572872 | tf_op jit(solution)/shard_map/ppermute | solution.py:371
  116.3 15.1 %collective-permute-start.12 = (f32[2,2,128,128]{3,2,1,0:T(8,128)}, f32[2,2,128,128]{3,2,1,0:T(8,128)}, u32[]{:S(2)}, u32[]{:S(2)}) collective-permute-start(f32[2,2,128,128]{3,2,1,0:T(8,128)} %get-tuple-element.93.own), channel_id=1, source_target_pairs={{0,4},{4,8},{8,12},{1,5},{5,9},{9,13},{2,6},{6,10},{10,14},{3,7},{... | collective-permute-start | bytes 786440 | tf_op jit(solution)/shard_map/ppermute | solution.py:431
  122.5 25.3 %collective-permute-start.14 = (f32[2,2,2,128,128]{4,3,2,1,0:T(8,128)S(1)}, f32[2,2,2,128,128]{4,3,2,1,0:T(8,128)}, u32[]{:S(2)}, u32[]{:S(2)}) collective-permute-start(f32[2,2,2,128,128]{4,3,2,1,0:T(8,128)S(1)} %get-tuple-element.96.refs_0_), channel_id=1, source_target_pairs={{0,2},{2,0},{1,3},{3,1},{4,6},{6,4},{5,7},{7,5},{8,10},{10,8},{9,1... | collective-permute-start | bytes 1572872 | tf_op jit(solution)/shard_map/ppermute | solution.py:371
  122.8 20.1 %collective-permute-start.10 = (f32[2,2,128,128]{3,2,1,0:T(8,128)}, f32[2,2,128,128]{3,2,1,0:T(8,128)}, u32[]{:S(2)}, u32[]{:S(2)}) collective-permute-start(f32[2,2,128,128]{3,2,1,0:T(8,128)} %get-tuple-element.95), channel_id=1, source_target_pairs={{4,0},{8,4},{12,8},{5,1},{9,5},{13,9},{6,2},{10,6},{14,10},{7,3},{... | collective-permute-start | bytes 786440 | tf_op jit(solution)/shard_map/ppermute | solution.py:441
  134.6 14.3 %collective-permute-start.15 = (f32[2,2,128,128]{3,2,1,0:T(8,128)S(1)}, f32[2,2,128,128]{3,2,1,0:T(8,128)S(1)}, u32[]{:S(2)}, u32[]{:S(2)}) collective-permute-start(f32[2,2,128,128]{3,2,1,0:T(8,128)S(1)} %get-tuple-element.99.own), channel_id=1, source_target_pairs={{0,4},{4,8},{8,12},{1,5},{5,9},{9,13},{2,6},{6,10},{10,14},{3,7},{... | collective-permute-start | bytes 786440 | tf_op jit(solution)/shard_map/ppermute | solution.py:431
  145.3 13.7 %collective-permute-start.13 = (f32[2,2,128,128]{3,2,1,0:T(8,128)S(1)}, f32[2,2,128,128]{3,2,1,0:T(8,128)S(1)}, u32[]{:S(2)}, u32[]{:S(2)}) collective-permute-start(f32[2,2,128,128]{3,2,1,0:T(8,128)S(1)} %get-tuple-element.101), channel_id=1, source_target_pairs={{4,0},{8,4},{12,8},{5,1},{9,5},{13,9},{6,2},{10,6},{14,10},{7,3},{... | collective-permute-start | bytes 786440 | tf_op jit(solution)/shard_map/ppermute | solution.py:441
  146.6 19.1 %collective-permute-start.17 = (f32[2,2,2,128,128]{4,3,2,1,0:T(8,128)S(1)}, f32[2,2,2,128,128]{4,3,2,1,0:T(8,128)}, u32[]{:S(2)}, u32[]{:S(2)}) collective-permute-start(f32[2,2,2,128,128]{4,3,2,1,0:T(8,128)S(1)} %get-tuple-element.102.refs_0_), channel_id=1, source_target_pairs={{0,2},{2,0},{1,3},{3,1},{4,6},{6,4},{5,7},{7,5},{8,10},{10,8},{9,1... | collective-permute-start | bytes 1572872 | tf_op jit(solution)/shard_map/ppermute | solution.py:371
  152.2 9.7 %copy-start.28 = (f32[8,2,2,2,128,128]{5,4,3,2,1,0:T(8,128)}, f32[8,2,2,2,128,128]{5,4,3,2,1,0:T(8,128)S(1)}, u32[]{:S(2)}) copy-start(f32[8,2,2,2,128,128]{5,4,3,2,1,0:T(8,128)S(1)} %get-tuple-element.106.seen.unused) | copy-start | bytes 12582916
  152.2 20.2 %collective-permute-start.18 = (f32[2,2,128,128]{3,2,1,0:T(8,128)}, f32[2,2,128,128]{3,2,1,0:T(8,128)}, u32[]{:S(2)}, u32[]{:S(2)}) collective-permute-start(f32[2,2,128,128]{3,2,1,0:T(8,128)} %get-tuple-element.105.own), channel_id=1, source_target_pairs={{0,4},{4,8},{8,12},{1,5},{5,9},{9,13},{2,6},{6,10},{10,14},{3,7},{... | collective-permute-start | bytes 786440 | tf_op jit(solution)/shard_map/ppermute | solution.py:431
  162.0 19.3 %collective-permute-start.20 = (f32[2,2,2,128,128]{4,3,2,1,0:T(8,128)S(1)}, f32[2,2,2,128,128]{4,3,2,1,0:T(8,128)}, u32[]{:S(2)}, u32[]{:S(2)}) collective-permute-start(f32[2,2,2,128,128]{4,3,2,1,0:T(8,128)S(1)} %get-tuple-element.108.refs_0_), channel_id=1, source_target_pairs={{0,2},{2,0},{1,3},{3,1},{4,6},{6,4},{5,7},{7,5},{8,10},{10,8},{9,1... | collective-permute-start | bytes 1572872 | tf_op jit(solution)/shard_map/ppermute | solution.py:371
  163.2 13.2 %collective-permute-start.16 = (f32[2,2,128,128]{3,2,1,0:T(8,128)}, f32[2,2,128,128]{3,2,1,0:T(8,128)}, u32[]{:S(2)}, u32[]{:S(2)}) collective-permute-start(f32[2,2,128,128]{3,2,1,0:T(8,128)} %get-tuple-element.107), channel_id=1, source_target_pairs={{4,0},{8,4},{12,8},{5,1},{9,5},{13,9},{6,2},{10,6},{14,10},{7,3},{... | collective-permute-start | bytes 786440 | tf_op jit(solution)/shard_map/ppermute | solution.py:441
  165.7 6.7 %copy-start.29 = (f32[8,2,2,2,128,128]{5,4,3,2,1,0:T(8,128)S(1)}, f32[8,2,2,2,128,128]{5,4,3,2,1,0:T(8,128)}, u32[]{:S(2)}) copy-start(f32[8,2,2,2,128,128]{5,4,3,2,1,0:T(8,128)} %copy-done.28) | copy-start | bytes 12582916
  175.7 7.4 %collective-permute-start.21 = (f32[2,2,128,128]{3,2,1,0:T(8,128)S(1)}, f32[2,2,128,128]{3,2,1,0:T(8,128)S(1)}, u32[]{:S(2)}, u32[]{:S(2)}) collective-permute-start(f32[2,2,128,128]{3,2,1,0:T(8,128)S(1)} %get-tuple-element.111.own), channel_id=1, source_target_pairs={{4,8},{8,12},{5,9},{9,13},{6,10},{10,14},{7,11},{11,15},{20,24},{2... | collective-permute-start | bytes 786440 | tf_op jit(solution)/shard_map/ppermute | solution.py:431
  178.9 12.2 %collective-permute-start.19 = (f32[2,2,128,128]{3,2,1,0:T(8,128)S(1)}, f32[2,2,128,128]{3,2,1,0:T(8,128)S(1)}, u32[]{:S(2)}, u32[]{:S(2)}) collective-permute-start(f32[2,2,128,128]{3,2,1,0:T(8,128)S(1)} %get-tuple-element.113), channel_id=1, source_target_pairs={{4,0},{8,4},{12,8},{5,1},{9,5},{13,9},{6,2},{10,6},{14,10},{7,3},{... | collective-permute-start | bytes 786440 | tf_op jit(solution)/shard_map/ppermute | solution.py:441
  180.2 16.0 %collective-permute-start.23 = (f32[2,2,2,128,128]{4,3,2,1,0:T(8,128)S(1)}, f32[2,2,2,128,128]{4,3,2,1,0:T(8,128)}, u32[]{:S(2)}, u32[]{:S(2)}) collective-permute-start(f32[2,2,2,128,128]{4,3,2,1,0:T(8,128)S(1)} %get-tuple-element.114.refs_0_), channel_id=1, source_target_pairs={{0,2},{2,0},{1,3},{3,1},{4,6},{6,4},{5,7},{7,5},{8,10},{10,8},{9,1... | collective-permute-start | bytes 1572872 | tf_op jit(solution)/shard_map/ppermute | solution.py:371
  186.3 7.4 %copy-start.30 = (f32[8,2,2,2,128,128]{5,4,3,2,1,0:T(8,128)}, f32[8,2,2,2,128,128]{5,4,3,2,1,0:T(8,128)S(1)}, u32[]{:S(2)}) copy-start(f32[8,2,2,2,128,128]{5,4,3,2,1,0:T(8,128)S(1)} %get-tuple-element.118.seen.unused) | copy-start | bytes 12582916
  186.3 16.6 %collective-permute-start.24 = (f32[2,2,128,128]{3,2,1,0:T(8,128)S(1)}, f32[2,2,128,128]{3,2,1,0:T(8,128)S(1)}, u32[]{:S(2)}, u32[]{:S(2)}) collective-permute-start(f32[2,2,128,128]{3,2,1,0:T(8,128)S(1)} %get-tuple-element.117.own), channel_id=1, source_target_pairs={{8,12},{9,13},{10,14},{11,15},{24,28},{25,29},{26,30},{27,31}} | collective-permute-start | bytes 786440 | tf_op jit(solution)/shard_map/ppermute | solution.py:431
  193.7 12.4 %collective-permute-start.22 = (f32[2,2,128,128]{3,2,1,0:T(8,128)}, f32[2,2,128,128]{3,2,1,0:T(8,128)}, u32[]{:S(2)}, u32[]{:S(2)}) collective-permute-start(f32[2,2,128,128]{3,2,1,0:T(8,128)} %get-tuple-element.119), channel_id=1, source_target_pairs={{4,0},{8,4},{12,8},{5,1},{9,5},{13,9},{6,2},{10,6},{14,10},{7,3},{... | collective-permute-start | bytes 786440 | tf_op jit(solution)/shard_map/ppermute | solution.py:441
  195.0 16.4 %collective-permute-start.25 = (f32[2,2,2,128,128]{4,3,2,1,0:T(8,128)}, f32[2,2,2,128,128]{4,3,2,1,0:T(8,128)}, u32[]{:S(2)}, u32[]{:S(2)}) collective-permute-start(f32[2,2,2,128,128]{4,3,2,1,0:T(8,128)} %get-tuple-element.120.refs_0_), channel_id=1, source_target_pairs={{0,2},{2,0},{1,3},{3,1},{4,6},{6,4},{5,7},{7,5},{8,10},{10,8},{9,1... | collective-permute-start | bytes 1572872 | tf_op jit(solution)/shard_map/ppermute | solution.py:371
  196.1 6.8 %copy-start.12 = (f32[8,2,2,2,128,128]{5,4,3,2,1,0:T(8,128)S(1)}, f32[8,2,2,2,128,128]{5,4,3,2,1,0:T(8,128)}, u32[]{:S(2)}) copy-start(f32[8,2,2,2,128,128]{5,4,3,2,1,0:T(8,128)} %copy-done.5) | copy-start | bytes 12582916
  196.1 6.8 %copy-start.31 = (f32[8,2,2,2,128,128]{5,4,3,2,1,0:T(8,128)S(1)}, f32[8,2,2,2,128,128]{5,4,3,2,1,0:T(8,128)}, u32[]{:S(2)}) copy-start(f32[8,2,2,2,128,128]{5,4,3,2,1,0:T(8,128)} %copy-done.30) | copy-start | bytes 12582916
  208.6 10.2 %collective-permute-start.26 = (f32[2,2,128,128]{3,2,1,0:T(8,128)S(1)}, f32[2,2,128,128]{3,2,1,0:T(8,128)S(1)}, u32[]{:S(2)}, u32[]{:S(2)}) collective-permute-start(f32[2,2,128,128]{3,2,1,0:T(8,128)S(1)} %get-tuple-element.127), channel_id=1, source_target_pairs={{4,0},{8,4},{12,8},{5,1},{9,5},{13,9},{6,2},{10,6},{14,10},{7,3},{... | collective-permute-start | bytes 786440 | tf_op jit(solution)/shard_map/ppermute | solution.py:441
  209.9 13.7 %collective-permute-start.27 = (f32[2,2,2,128,128]{4,3,2,1,0:T(8,128)S(1)}, f32[2,2,2,128,128]{4,3,2,1,0:T(8,128)S(1)}, u32[]{:S(2)}, u32[]{:S(2)}) collective-permute-start(f32[2,2,2,128,128]{4,3,2,1,0:T(8,128)S(1)} %get-tuple-element.125.refs_0_), channel_id=1, source_target_pairs={{0,2},{2,0},{1,3},{3,1},{4,6},{6,4},{5,7},{7,5},{8,10},{10,8},{9,1... | collective-permute-start | bytes 1572872 | tf_op jit(solution)/shard_map/ppermute | solution.py:371
  211.4 7.4 %copy-start.13 = (f32[8,2,2,2,128,128]{5,4,3,2,1,0:T(8,128)S(1)}, f32[8,2,2,2,128,128]{5,4,3,2,1,0:T(8,128)}, u32[]{:S(2)}) copy-start(f32[8,2,2,2,128,128]{5,4,3,2,1,0:T(8,128)} %copy-done.5) | copy-start | bytes 12582916
  211.4 7.4 %copy-start.33 = (f32[8,2,2,2,128,128]{5,4,3,2,1,0:T(8,128)S(1)}, f32[8,2,2,2,128,128]{5,4,3,2,1,0:T(8,128)}, u32[]{:S(2)}) copy-start(f32[8,2,2,2,128,128]{5,4,3,2,1,0:T(8,128)} %copy-done.32) | copy-start | bytes 12582916
  221.4 12.5 %collective-permute-start.28 = (f32[2,2,128,128]{3,2,1,0:T(8,128)}, f32[2,2,128,128]{3,2,1,0:T(8,128)}, u32[]{:S(2)}, u32[]{:S(2)}) collective-permute-start(f32[2,2,128,128]{3,2,1,0:T(8,128)} %get-tuple-element.131), channel_id=1, source_target_pairs={{4,0},{8,4},{5,1},{9,5},{6,2},{10,6},{7,3},{11,7},{20,16},{24,20},... | collective-permute-start | bytes 786440 | tf_op jit(solution)/shard_map/ppermute | solution.py:441
  222.7 16.2 %collective-permute-start.29 = (f32[2,2,2,128,128]{4,3,2,1,0:T(8,128)S(1)}, f32[2,2,2,128,128]{4,3,2,1,0:T(8,128)S(1)}, u32[]{:S(2)}, u32[]{:S(2)}) collective-permute-start(f32[2,2,2,128,128]{4,3,2,1,0:T(8,128)S(1)} %get-tuple-element.129.refs_0_), channel_id=1, source_target_pairs={{0,2},{2,0},{1,3},{3,1},{4,6},{6,4},{5,7},{7,5},{8,10},{10,8},{9,1... | collective-permute-start | bytes 1572872 | tf_op jit(solution)/shard_map/ppermute | solution.py:371
  223.6 10.3 %copy-start.14 = (f32[8,2,2,2,128,128]{5,4,3,2,1,0:T(8,128)S(1)}, f32[8,2,2,2,128,128]{5,4,3,2,1,0:T(8,128)}, u32[]{:S(2)}) copy-start(f32[8,2,2,2,128,128]{5,4,3,2,1,0:T(8,128)} %copy-done.5) | copy-start | bytes 12582916
  223.6 10.3 %copy-start.34 = (f32[8,2,2,2,128,128]{5,4,3,2,1,0:T(8,128)S(1)}, f32[8,2,2,2,128,128]{5,4,3,2,1,0:T(8,128)}, u32[]{:S(2)}) copy-start(f32[8,2,2,2,128,128]{5,4,3,2,1,0:T(8,128)} %copy-done.32) | copy-start | bytes 12582916
  228.5 8.4 %copy-start.54 = (f32[2,2,656,768]{3,2,1,0:T(8,128)}, f32[2,2,656,768]{3,2,1,0:T(8,128)S(1)}, u32[]{:S(2)}) copy-start(f32[2,2,656,768]{3,2,1,0:T(8,128)S(1)} %deposit_patches.20.refs_2_) | copy-start | bytes 24182788
  236.9 8.7 %collective-permute-start.30 = (f32[2,2,128,128]{3,2,1,0:T(8,128)}, f32[2,2,128,128]{3,2,1,0:T(8,128)}, u32[]{:S(2)}, u32[]{:S(2)}) collective-permute-start(f32[2,2,128,128]{3,2,1,0:T(8,128)} %get-tuple-element.135), channel_id=1, source_target_pairs={{4,0},{5,1},{6,2},{7,3},{20,16},{21,17},{22,18},{23,19}} | collective-permute-start | bytes 786440 | tf_op jit(solution)/shard_map/ppermute | solution.py:441
  238.2 7.3 %copy-start.15 = (f32[8,2,2,2,128,128]{5,4,3,2,1,0:T(8,128)S(1)}, f32[8,2,2,2,128,128]{5,4,3,2,1,0:T(8,128)}, u32[]{:S(2)}) copy-start(f32[8,2,2,2,128,128]{5,4,3,2,1,0:T(8,128)} %copy-done.5) | copy-start | bytes 12582916
  238.3 7.3 %copy-start.35 = (f32[8,2,2,2,128,128]{5,4,3,2,1,0:T(8,128)S(1)}, f32[8,2,2,2,128,128]{5,4,3,2,1,0:T(8,128)}, u32[]{:S(2)}) copy-start(f32[8,2,2,2,128,128]{5,4,3,2,1,0:T(8,128)} %copy-done.32) | copy-start | bytes 12582916
  238.3 13.5 %collective-permute-start.32 = (f32[2,2,2,128,128]{4,3,2,1,0:T(8,128)S(1)}, f32[2,2,2,128,128]{4,3,2,1,0:T(8,128)S(1)}, u32[]{:S(2)}, u32[]{:S(2)}) collective-permute-start(f32[2,2,2,128,128]{4,3,2,1,0:T(8,128)S(1)} %get-tuple-element.133.refs_0_), channel_id=1, source_target_pairs={{0,2},{2,0},{1,3},{3,1},{4,6},{6,4},{5,7},{7,5},{8,10},{10,8},{9,1... | collective-permute-start | bytes 1572872 | tf_op jit(solution)/shard_map/ppermute | solution.py:371
  248.7 10.0 %collective-permute-start.31 = (f32[2,2,2,128,128]{4,3,2,1,0:T(8,128)S(1)}, f32[2,2,2,128,128]{4,3,2,1,0:T(8,128)S(1)}, u32[]{:S(2)}, u32[]{:S(2)}) collective-permute-start(f32[2,2,2,128,128]{4,3,2,1,0:T(8,128)S(1)} %get-tuple-element.137.refs_0_), channel_id=1, source_target_pairs={{0,2},{2,0},{1,3},{3,1},{4,6},{6,4},{5,7},{7,5},{8,10},{10,8},{9,1... | collective-permute-start | bytes 1572872 | tf_op jit(solution)/shard_map/ppermute | solution.py:371
  259.9 4.6 %collective-permute-start.33 = (f32[2,2,192,768]{3,2,1,0:T(8,128)S(1)}, f32[2,2,192,768]{3,2,1,0:T(8,128)S(1)}, u32[]{:S(2)}, u32[]{:S(2)}) collective-permute-start(f32[2,2,192,768]{3,2,1,0:T(8,128)S(1)} %bitcast.67), channel_id=1, source_target_pairs={{0,1},{1,0},{2,3},{3,2},{4,5},{5,4},{6,7},{7,6},{8,9},{9,8},{10,11... | collective-permute-start | bytes 7077896 | tf_op jit(solution)/shard_map/ppermute | solution.py:371
  (62 other events, 204.5 us)

commit v4 on v0

v4 whole, which is shorter than its diff:
```python
import functools
import math

import jax
import jax.numpy as jnp
import ml_dtypes
import numpy as np
from jax import lax
from jax.experimental import pallas as pl
from jax.experimental.pallas import tpu as pltpu
from jax.sharding import PartitionSpec as P

FRESNEL = 8.0
CROSSING = 2
F32 = jnp.float32
BF16 = jnp.bfloat16
HBM = pl.BlockSpec(memory_space=pl.ANY)
VMEM = pl.BlockSpec(memory_space=pltpu.VMEM)
SMEM = pl.BlockSpec(memory_space=pltpu.SMEM)


def in_hbm(x):
    return pltpu.with_memory_space_constraint(x, pltpu.HBM)


def in_vmem(x):
    return pltpu.with_memory_space_constraint(x, pltpu.VMEM)


def real_blocks(matrix):
    real, imag = matrix.real, matrix.imag
    left = np.block([[real, -imag], [imag, real]])
    right = np.block([[real, imag], [-imag, real]])
    return np.stack([left, right])


@functools.lru_cache(maxsize=None)
def make_tables(pixels):
    index = np.arange(pixels)
    freq = np.where(index < pixels // 2, index, index - pixels) / pixels
    spread = index[:, None] - index[None, :]
    phase = 2.0 * math.pi * freq * spread[:, :, None] - math.pi * FRESNEL * freq * freq
    propagator = np.mean(np.exp(1j * phase), axis=-1)
    turns = index[:, None] * index[None, :] % pixels
    fourier = np.exp(-2j * math.pi * turns / pixels) / math.sqrt(pixels)
    blocks = np.stack([real_blocks(propagator), real_blocks(fourier)]).astype(np.float32)
    high = blocks.astype(ml_dtypes.bfloat16)
    low = (blocks - high.astype(np.float32)).astype(ml_dtypes.bfloat16)
    return np.stack([high, low], axis=2)


def halves(x):
    high = x.astype(BF16)
    return high, (x - high.astype(F32)).astype(BF16)


def dot(a, b):
    return jnp.dot(a, b, preferred_element_type=F32)


def transform(left, right, fields):
    size = fields[0][0].shape[0]
    stacked = jnp.concatenate(
        [
            jnp.concatenate([real for real, _ in fields], axis=1),
            jnp.concatenate([imag for _, imag in fields], axis=1),
        ],
        axis=0,
    )
    high, low = halves(stacked)
    mid = dot(left[0], high) + (dot(left[1], high) + dot(left[0], low))
    rows = jnp.concatenate(
        [
            jnp.concatenate(
                [mid[:size, i * size : (i + 1) * size], mid[size:, i * size : (i + 1) * size]], axis=1
            )
            for i in range(len(fields))
        ],
        axis=0,
    )
    high, low = halves(rows)
    out = dot(high, right[0]) + (dot(high, right[1]) + dot(low, right[0]))
    return [
        (out[i * size : (i + 1) * size, :size], out[i * size : (i + 1) * size, size:])
        for i in range(len(fields))
    ]


def times(a, b):
    return a[0] * b[0] - a[1] * b[1], a[0] * b[1] + a[1] * b[0]


def times_conj(a, b):
    return a[0] * b[0] + a[1] * b[1], a[1] * b[0] - a[0] * b[1]


class Layout:
    def __init__(self, probes, count, layers, pixels, rows, width):
        self.probes, self.count, self.layers, self.pixels = probes, count, layers, pixels
        self.groups = probes // count
        self.tall = pixels + 8
        self.rows, self.width = rows, width
        self.blocks = width // pixels
        self.deep = rows + 2 * self.tall
        stack = probes * layers * 2 * pixels
        self.seen_from = stack
        self.frames_from = 2 * stack
        self.total_from = self.frames_from + probes * pixels
        self.shape = (self.total_from + 2 * layers * self.blocks * self.deep, pixels)

    def stacked(self, group, i, layer, part):
        probe = group * self.count + i
        return ((probe * self.layers + layer) * 2 + part) * self.pixels

    def tile(self, start):
        return pl.ds(pl.multiple_of(start, 8), self.pixels)

    def patch(self, group, i, layer, part):
        return self.tile(self.stacked(group, i, layer, part))

    def seen(self, group, i, layer, part):
        return self.tile(self.seen_from + self.stacked(group, i, layer, part))

    def frame(self, group, i):
        return self.tile(self.frames_from + (group * self.count + i) * self.pixels)

    def total(self, part, layer, block, row):
        block = (part * self.layers + layer) * self.blocks + block
        return self.total_from + block * self.deep + row

    def window(self, corners, probe):
        row, column = corners[2 * probe], corners[2 * probe + 1]
        row0 = jnp.minimum(row // 8 * 8, self.height - self.tall)
        block = jnp.minimum(column // self.pixels, self.blocks - 2)
        return row0, row - row0, block, column - block * self.pixels


def call(lay, body, state, before, outs, scratch=(), grid=(), prefetch=(), limit=4, flops=0, moved=0, name=None):
    spaces = {"hbm": (HBM, in_hbm), "vmem": (VMEM, in_vmem), "smem": (SMEM, lambda x: x)}
    specs = [spaces[kind][0] for kind, _ in before]
    operands = [spaces[kind][1](x) for kind, x in before]
    at = len(prefetch) + len(before)

    def kernel(*refs):
        body(*refs[:at], *refs[at + 1 :])

    return pl.pallas_call(
        kernel,
        grid_spec=pltpu.PrefetchScalarGridSpec(
            num_scalar_prefetch=len(prefetch),
            grid=grid,
            in_specs=[*specs, VMEM],
            out_specs=[VMEM] * (1 + len(outs)),
            scratch_shapes=list(scratch),
        ),
        out_shape=[pltpu.VMEM(shape, F32) for shape in (lay.shape, *outs)],
        input_output_aliases={at: 0},
        compiler_params=pltpu.CompilerParams(vmem_limit_bytes=limit << 20),
        cost_estimate=pl.CostEstimate(flops=flops, bytes_accessed=moved, transcendentals=0),
        name=name,
    )(*prefetch, *operands, in_vmem(state))


def make_state(lay, frames):
    start = lay.total_from

    def body(frames, state, sem):
        copy = pltpu.make_async_copy(
            frames, state.at[pl.ds(lay.frames_from, lay.probes * lay.pixels), :], sem
        )
        copy.start()
        state[pl.ds(start, lay.shape[0] - start), :] = jnp.zeros((lay.shape[0] - start, lay.pixels), F32)
        copy.wait()

    return pl.pallas_call(
        body,
        in_specs=[HBM],
        out_specs=VMEM,
        out_shape=pltpu.VMEM(lay.shape, F32),
        scratch_shapes=[pltpu.SemaphoreType.DMA(())],
        compiler_params=pltpu.CompilerParams(vmem_limit_bytes=4 << 20),
        name="make_state",
    )(in_hbm(frames.reshape((-1, lay.pixels))))


def cut_patches(lay, info, own, other, state, begin, end):
    half = own.shape[2]
    tall, pixels = lay.tall, lay.pixels

    def body(info, own, other, state, window, sems):
        step = pl.program_id(0)
        steps = pl.num_programs(0)

        def copies(step, slot, act):
            row0, _, block, _ = lay.window(info.at[pl.ds(3, 2 * lay.probes)], begin + step)
            own_top = info[1] == 0
            for source, is_top, sem in ((own, own_top, 0), (other, jnp.logical_not(own_top), 1)):
                start = jnp.clip(row0 - jnp.where(is_top, 0, half), 0, half - tall)
                to = jnp.where(is_top, 0, tall)

                @pl.when(jnp.where(is_top, row0 < half, row0 + tall > half))
                def _(source=source, start=start, to=to, sem=sem):
                    act(
                        pltpu.make_async_copy(
                            source.at[
                                :,
                                :,
                                pl.ds(pl.multiple_of(start, 8), tall),
                                pl.ds(pl.multiple_of(block * pixels, pixels), 2 * pixels),
                            ],
                            window.at[slot, :, :, pl.ds(pl.multiple_of(to, 8), tall), :],
                            sems.at[slot, sem],
                        )
                    )

        slot = step % 2

        @pl.when(step == 0)
        def _():
            copies(0, 0, lambda copy: copy.start())

        @pl.when(step + 1 < steps)
        def _():
            copies(step + 1, 1 - slot, lambda copy: copy.start())

        copies(step, slot, lambda copy: copy.wait())
        row0, down, _, shift = lay.window(info.at[pl.ds(3, 2 * lay.probes)], begin + step)
        offset = jnp.where(row0 < half, jnp.maximum(row0 - (half - tall), 0), tall)
        offset = pl.multiple_of(offset, 8)
        turn = (pixels - shift) % pixels
        lane = lax.broadcasted_iota(jnp.int32, (tall, pixels), 1)
        for part in range(2):
            for layer in range(lay.layers):
                near = window[slot, part, layer, pl.ds(offset, tall), pl.ds(0, pixels)]
                far = window[slot, part, layer, pl.ds(offset, tall), pl.ds(pixels, pixels)]
                near = pltpu.roll(near, turn, 1)
                far = pltpu.roll(far, turn, 1)
                patch = jnp.where(lane < pixels - shift, near, far)
                patch = pltpu.roll(patch, (tall - down) % tall, 0)[:pixels]
                state[lay.patch(0, begin + step, layer, part), :] = patch

    size = (end - begin) * lay.layers * 2 * pixels * pixels
    return call(
        lay,
        body,
        state,
        [("hbm", own), ("hbm", other)],
        [],
        scratch=[
            pltpu.VMEM((2, 2, lay.layers, 2 * tall, 2 * pixels), F32),
            pltpu.SemaphoreType.DMA((2, 2)),
        ],
        grid=(end - begin,),
        prefetch=(info,),
        limit=8,
        flops=size * 4,
        moved=size * 12,
        name="cut_patches",
    )[0]


def section_cost(lay):
    size = lay.count * lay.pixels**2
    return dict(flops=lay.layers * 2 * 3 * 8 * size * lay.pixels, moved=(lay.layers * 2 + 4) * 8 * size)


def pair(ref, at):
    return ref[at(0), :], ref[at(1), :]


def run_forward(lay, tick, sections, info, tables, state, arrived, start_wave):
    def body(info, tables, *refs):
        arrived_ref = refs[0] if arrived is not None else None
        start_ref = refs[-3] if start_wave is not None else None
        state, leave = refs[-2:]
        section = info[0]
        group = tick - section
        final = (section == sections - 1).astype(jnp.int32)

        @pl.when((group >= 0) & (group < lay.groups))
        def _():
            wave = []
            for i in range(lay.count):
                if arrived is None:
                    wave.append((start_ref[0], start_ref[1]))
                elif start_wave is None:
                    wave.append((arrived_ref[i, 0], arrived_ref[i, 1]))
                else:
                    wave.append(
                        tuple(jnp.where(section == 0, start_ref[p], arrived_ref[i, p]) for p in range(2))
                    )
            for layer in range(lay.layers):
                chi = []
                for i in range(lay.count):
                    for part in range(2):
                        state[lay.seen(group, i, layer, part), :] = wave[i][part]
                    chi.append(times(pair(state, functools.partial(lay.patch, group, i, layer)), wave[i]))
                at = final if layer == lay.layers - 1 else 0
                wave = transform((tables[at, 0, 0], tables[at, 0, 1]), (tables[at, 1, 0], tables[at, 1, 1]), chi)
            for i in range(lay.count):
                real, imag = wave[i]
                misfit = real * real + imag * imag - state[lay.frame(group, i), :]
                factor = jnp.where(final == 1, misfit, 1.0)
                leave[i, 0] = real * factor
                leave[i, 1] = imag * factor

    waves = [("vmem", x) for x in (arrived, start_wave) if x is not None]
    return call(
        lay,
        body,
        state,
        [("smem", info), ("vmem", tables), *waves],
        [(lay.count, 2, lay.pixels, lay.pixels)],
        name="forward_section",
        **section_cost(lay),
    )


def run_backward(lay, tick, sections, info, tables, state, arrived, own):
    def body(info, tables, *refs):
        arrived_ref = refs[0] if arrived is not None else None
        own_ref = refs[-4] if own is not None else None
        state, leave, grads = refs[-3:]
        section = info[0]
        group = tick - (2 * (sections - 1) - section)
        final = (section == sections - 1).astype(jnp.int32)

        @pl.when((group >= 0) & (group < lay.groups))
        def _():
            wave = []
            for i in range(lay.count):
                if arrived is None:
                    wave.append((own_ref[i, 0], own_ref[i, 1]))
                elif own is None:
                    wave.append((arrived_ref[i, 0], arrived_ref[i, 1]))
                else:
                    wave.append(
                        tuple(jnp.where(final == 1, own_ref[i, p], arrived_ref[i, p]) for p in range(2))
                    )
            for layer in reversed(range(lay.layers)):
                at = final if layer == lay.layers - 1 else 0
                chi = transform((tables[at, 1, 0], tables[at, 1, 1]), (tables[at, 0, 0], tables[at, 0, 1]), wave)
                wave = []
                for i in range(lay.count):
                    real, imag = times_conj(chi[i], pair(state, functools.partial(lay.seen, group, i, layer)))
                    grads[i, layer, 0] = real
                    grads[i, layer, 1] = imag
                    wave.append(times_conj(chi[i], pair(state, functools.partial(lay.patch, group, i, layer))))
            for i in range(lay.count):
                leave[i, 0] = wave[i][0]
                leave[i, 1] = wave[i][1]

    waves = [("vmem", x) for x in (arrived, own) if x is not None]
    return call(
        lay,
        body,
        state,
        [("smem", info), ("vmem", tables), *waves],
        [
            (lay.count, 2, lay.pixels, lay.pixels),
            (lay.count, lay.layers, 2, lay.pixels, lay.pixels),
        ],
        name="backward_section",
        **section_cost(lay),
    )


def deposit(lay, sections, info, sources, state):
    n = len(sources)
    pixels, tall = lay.pixels, lay.tall

    def body(info, *refs):
        state = refs[2 * n]
        lane = lax.broadcasted_iota(jnp.int32, (tall, pixels), 1)
        blank = jnp.zeros((8, pixels), F32)
        for which, (tick, _, _) in enumerate(sources):
            corners, grads = refs[which], refs[n + which]
            group = tick - (2 * (sections - 1) - info[0])
            active = (group >= 0) & (group < lay.groups)
            for i in range(lay.count):
                probe = jnp.clip(group, 0, lay.groups - 1) * lay.count + i
                row0, down, block, shift = lay.window(corners, probe)
                start = row0 - info[2] + tall

                @pl.when(active & (start > 0) & (start < lay.rows + tall))
                def _(grads=grads, i=i, start=start, down=down, block=block, shift=shift):
                    for layer in range(lay.layers):
                        for part in range(2):
                            padded = jnp.concatenate([grads[i, layer, part], blank], axis=0)
                            turned = pltpu.roll(pltpu.roll(padded, down, 0), shift % pixels, 1)
                            near = pl.ds(pl.multiple_of(lay.total(part, layer, block, start), 8), tall)
                            far = pl.ds(pl.multiple_of(lay.total(part, layer, block + 1, start), 8), tall)
                            state[near, :] += jnp.where(lane >= shift, turned, 0.0)
                            state[far, :] += jnp.where(lane >= shift, 0.0, turned)

    size = sum(grads.size for *_, grads in sources)
    return call(
        lay,
        body,
        state,
        [("smem", info)]
        + [("smem", corners) for _, corners, _ in sources]
        + [("vmem", grads) for *_, grads in sources],
        [],
        flops=size * 8,
        moved=size * 12,
        name="deposit_patches",
    )[0]


def split_rows(lay, info, state, owners):
    rows = lay.rows // (2 * owners)

    def body(info, state, keep, send, sems):
        copies = []
        for owner in range(owners):
            for kind, target in ((info[1], keep), (1 - info[1], send)):
                for part in range(2):
                    for layer in range(lay.layers):
                        for block in range(lay.blocks):
                            start = lay.total(part, layer, block, lay.tall + (2 * owner + kind) * rows)
                            copies.append(
                                pltpu.make_async_copy(
                                    state.at[pl.ds(pl.multiple_of(start, 8), rows), :],
                                    target.at[part, layer, owner, :, pl.ds(block * lay.pixels, lay.pixels)],
                                    sems.at[len(copies)],
                                )
                            )
        for copy in copies:
            copy.start()
        for copy in copies:
            copy.wait()

    half = (2, lay.layers, owners, rows, lay.width)
    return pl.pallas_call(
        body,
        in_specs=[SMEM, VMEM],
        out_specs=[VMEM, VMEM],
        out_shape=[pltpu.VMEM(half, F32), pltpu.VMEM(half, F32)],
        scratch_shapes=[pltpu.SemaphoreType.DMA((4 * owners * lay.layers * lay.blocks,))],
        compiler_params=pltpu.CompilerParams(vmem_limit_bytes=4 << 20),
        name="split_rows",
    )(info, in_vmem(state))


def swap(shard, axis):
    return lax.ppermute(shard, axis, [(0, 1), (1, 0)])


def local(specimen, illumination, positions, scan_index, frames):
    pixels = illumination.shape[-1]
    _, layers, half, width = specimen.shape
    height = 2 * half
    tables = jnp.asarray(make_tables(pixels))
    section = lax.axis_index("depth")
    sections = lax.axis_size("depth")
    owners = lax.axis_size("probe")
    paired = owners == 2

    other = swap(specimen, "lat")
    corners = positions[scan_index.reshape(-1)].reshape(-1)
    probes = corners.shape[0] // 2
    count = 2 if probes % 2 == 0 else 1
    base = lax.axis_index("probe") * half if paired else 0
    lay = Layout(probes, count, layers, pixels, half if paired else height, width)
    lay.height = height
    info = jnp.concatenate([jnp.stack([section, lax.axis_index("lat"), jnp.int32(base)]), corners])
    partner = swap(corners, "probe") if paired else corners
    state = make_state(lay, frames)
    state = cut_patches(lay, info, specimen, other, state, 0, count)

    def busy(tick, source, by):
        delay = source if by > 0 else 2 * (sections - 1) - source
        return 0 <= tick - delay < lay.groups

    def pass_on(wave, tick, by):
        pairs = [
            (source, source + by)
            for source in range(sections)
            if 0 <= source + by < sections and busy(tick, source, by)
        ]
        return lax.ppermute(wave, "depth", pairs) if pairs else None

    def cross(grads, tick):
        pairs = [
            (2 * source + side, 2 * source + 1 - side)
            for source in range(sections)
            for side in range(2)
            if busy(tick, source, -1)
        ]
        return lax.ppermute(grads, ("depth", "probe"), pairs)

    down = up = None
    crossing = []
    last_tick = lay.groups + 2 * (sections - 1) - 1
    for tick in range(last_tick + 1):
        own = None
        if tick < lay.groups + sections - 1:
            start_wave = illumination if tick < lay.groups else None
            state, own = run_forward(lay, tick, sections, info, tables, state, down, start_wave)
            down = pass_on(own, tick, 1)
            if tick == 0:
                state = cut_patches(lay, info, specimen, other, state, count, probes)
        if tick >= sections - 1:
            state, rising, grads = run_backward(lay, tick, sections, info, tables, state, up, own)
            up = pass_on(rising, tick, -1)
            sources = [(tick, corners, grads)]
            if paired:
                crossing.append((tick, partner, cross(grads, tick)))
                if len(crossing) > CROSSING:
                    sources.append(crossing.pop(0))
            state = deposit(lay, sections, info, sources, state)
    for source in crossing:
        state = deposit(lay, sections, info, [source], state)
    if paired:
        keep, send = split_rows(lay, info, state, 1)
        return keep[:, :, 0] + swap(send[:, :, 0], "lat")
    keep, send = split_rows(lay, info, state, owners)
    return lax.psum_scatter(keep + swap(send, "lat"), "probe", scatter_dimension=2, tiled=False)


def solution(mesh):
    return jax.shard_map(
        local,
        mesh=mesh,
        in_specs=(
            P(None, ("groups", "depth"), "lat", None),
            P(),
            P("groups", None),
            P("groups", ("probe", "lat")),
            P("groups", ("probe", "lat"), None, None),
        ),
        out_specs=P(None, ("groups", "depth"), ("probe", "lat"), None),
        check_vma=False,
    )
```

time: 1110 us -> 250 us (0.23); the launches traced: 1090 us -> 249 us
  local copies, waits for them, and re-layouts: 320 us -> 49.6 us
  loops' own time: 206 us -> 0 us
  waiting for transfers between devices: 215 us -> 66.5 us
  matrix products: 141 us -> 0 us
  other arithmetic: 76.1 us -> 2.46 us
  Pallas kernels: 0 us -> 61.1 us
  starting transfers between devices: 119 us -> 68.3 us
  between operations: 13.5 us -> 0.69 us
    another operation x42 -> x0, loops' own time: 206 us -> none  [the longest x1 69.8 us: local(): lax.fori_loop(0, tick_count, forward_tick, (arrived, stored, exit_waves))]
    dot_general x512 -> x0, matrix products: 141 us -> none  [the longest x128 35.5 us: complex_apply(): jnp.einsum(pattern, mat_imag, wave_imag, precision=PRECISE)]
    dynamic_update_slice x92 -> x0, local copies, waits for them, and re-layouts: 102 us -> none  [the longest x16 69.4 us: add_one(): lax.dynamic_update_slice(buffer_now, region + patch_grads[index_probe], s...]
    reduce_scatter x1 -> x0, waiting for transfers between devices: 78.5 us -> none  [local(): lax.psum_scatter(running, ('probe', 'lat'), scatter_dimension=2, tiled=True)]
    gather x33 -> x1, local copies, waits for them, and re-layouts: 77.1 us -> 0.56 us  [local(): corners = positions[scan_index.reshape(-1)].reshape(-1)]
    ppermute x38 -> x34, waiting for transfers between devices: 137 us -> 66.5 us  [the longest x20 39.5 us: pass_on(): return lax.ppermute(wave, 'depth', pairs) if pairs else None]
    pallas_call x0 -> x39, Pallas kernels: none -> 61.1 us  [the longest x37 58.4 us: call(): pl.pallas_call(kernel, grid_spec=pltpu.PrefetchScalarGridSpec(num_scalar_...]
    ppermute x38 -> x34, starting transfers between devices: 119 us -> 68.3 us  [the longest x20 48.7 us: pass_on(): return lax.ppermute(wave, 'depth', pairs) if pairs else None]
  transfers between devices with their start and end apart: 40 -> 34, of which waited for: 39 -> 16; matrix products, arithmetic and copies ran while one was open for 10% -> 1% of each run, Pallas kernels for 0% -> 20%
where the time goes in v4:
time: 250 us; the launch traced here: 249 us
  starting transfers between devices  68.3 us (27%)
  waiting for transfers between devices  66.5 us (27%)
  Pallas kernels  61.1 us (24%)
  local copies, waits for them, and re-layouts  49.6 us (20%)
    pallas_call x37, Pallas kernels, call(): pl.pallas_call(kernel, grid_spec=pltpu.PrefetchScalarGridSpec(num_scalar_...  58.4 us
    unnamed x21, local copies, waits for them, and re-layouts  48.9 us
    ppermute x20, starting transfers between devices, pass_on(): return lax.ppermute(wave, 'depth', pairs) if pairs else None  48.7 us
    ppermute x20, waiting for transfers between devices, pass_on(): return lax.ppermute(wave, 'depth', pairs) if pairs else None  39.5 us
    ppermute x11, waiting for transfers between devices, cross(): return lax.ppermute(grads, ('depth', 'probe'), pairs)  20.2 us
    ppermute x11, starting transfers between devices, cross(): return lax.ppermute(grads, ('depth', 'probe'), pairs)  17.7 us
    ppermute x3, waiting for transfers between devices, swap(): return lax.ppermute(shard, axis, [(0, 1), (1, 0)])  6.78 us
  transfers between devices with their start and end apart: 34, of which 16 were waited for; matrix products, arithmetic and copies ran while one was open for 1% of the time, Pallas kernels for 20%

profile of v4, /device:TPU:0, one launch (start us, length us, event | category | flops | bytes accessed | tf_op | source)
XLA Modules:
  0.0 248.5 jit_solution(14426663571597565216)
XLA Ops:
  3.9 6.0 %copy-done = f32[34176,128]{1,0:T(8,128)} copy-done((f32[34176,128]{1,0:T(8,128)}, f32[34176,128]{1,0:T(8,128)S(1)}, u32[]{:S(2)}) %copy-start) | copy-done | bytes 17498136
  10.0 6.0 %copy-done.1 = f32[34176,128]{1,0:T(8,128)S(1)} copy-done((f32[34176,128]{1,0:T(8,128)S(1)}, f32[34176,128]{1,0:T(8,128)}, u32[]{:S(2)}) %copy-start.1) | copy-done | bytes 17498136
  16.0 2.2 cut_patches.2.refs_3_
  18.2 6.0 %copy-done.2 = f32[34176,128]{1,0:T(8,128)} copy-done((f32[34176,128]{1,0:T(8,128)}, f32[34176,128]{1,0:T(8,128)S(1)}, u32[]{:S(2)}) %copy-start.2) | copy-done | bytes 17498136
  24.2 6.0 %copy-done.3 = f32[34176,128]{1,0:T(8,128)S(1)} copy-done((f32[34176,128]{1,0:T(8,128)S(1)}, f32[34176,128]{1,0:T(8,128)}, u32[]{:S(2)}) %copy-start.3) | copy-done | bytes 17498136
  30.2 1.9 forward_section.11
  32.1 6.0 %copy-done.4 = f32[34176,128]{1,0:T(8,128)} copy-done((f32[34176,128]{1,0:T(8,128)}, f32[34176,128]{1,0:T(8,128)S(1)}, u32[]{:S(2)}) %copy-start.4) | copy-done | bytes 17498136
  38.1 3.2 %collective-permute-start.2 = (f32[2,2,128,128]{3,2,1,0:T(8,128)S(1)}, f32[2,2,128,128]{3,2,1,0:T(8,128)S(1)}, u32[]{:S(2)}, u32[]{:S(2)}) collective-permute-start(f32[2,2,128,128]{3,2,1,0:T(8,128)S(1)} %get-tuple-element.61), channel_id=1, source_target_pairs={{0,4},{1,5},{2,6},{3,7},{16,20},{17,21},{18,22},{19,23}} | collective-permute-start | bytes 786440 | tf_op jit(solution)/shard_map/ppermute | solution.py:482
  41.3 6.0 %copy-done.5 = f32[34176,128]{1,0:T(8,128)S(1)} copy-done((f32[34176,128]{1,0:T(8,128)S(1)}, f32[34176,128]{1,0:T(8,128)}, u32[]{:S(2)}) %copy-start.5) | copy-done | bytes 17498136
  47.3 10.7 %cut_patches.3.refs_4_ = f32[34176,128]{1,0:T(8,128)S(1)} custom-call(s32[35]{0:T(128)S(1)} %pad_add_fusion.refs_0_.info, f32[2,2,384,768]{3,2,1,0:T(8,128)} %refs_1_.25, f32[2,2,384,768]{3,2,1,0:T(8,128)} %collective-permute-done.1.refs_2_, f32[34176,128]{1,0:T(8,128)S(1)} %copy-done.5), custom_call_target="tpu_custom_call", output_to_operand_aliasing={{}: (3, {})} | custom-call | flops 3670016 | bytes 11010048 | tf_op jit(solution)/shard_map/cut_patches/pallas_call | solution.py:147
  58.0 6.0 %copy-done.6 = f32[34176,128]{1,0:T(8,128)} copy-done((f32[34176,128]{1,0:T(8,128)}, f32[34176,128]{1,0:T(8,128)S(1)}, u32[]{:S(2)}) %copy-start.6) | copy-done | bytes 17498136
  64.0 6.0 %copy-done.7 = f32[34176,128]{1,0:T(8,128)S(1)} copy-done((f32[34176,128]{1,0:T(8,128)S(1)}, f32[34176,128]{1,0:T(8,128)}, u32[]{:S(2)}) %copy-start.7) | copy-done | bytes 17498136
  70.0 1.9 forward_section.12
  73.2 6.5 %collective-permute-done.3.refs_2_ = f32[2,2,128,128]{3,2,1,0:T(8,128)S(1)} collective-permute-done((f32[2,2,128,128]{3,2,1,0:T(8,128)S(1)}, f32[2,2,128,128]{3,2,1,0:T(8,128)S(1)}, u32[]{:S(2)}, u32[]{:S(2)}) %collective-permute-start.3) | collective-permute-done | bytes 262176 | tf_op jit(solution)/shard_map/ppermute | solution.py:482
  79.7 1.9 forward_section.13
  81.6 4.4 %collective-permute-start.4 = (f32[2,2,128,128]{3,2,1,0:T(8,128)S(1)}, f32[2,2,128,128]{3,2,1,0:T(8,128)S(1)}, u32[]{:S(2)}, u32[]{:S(2)}) collective-permute-start(f32[2,2,128,128]{3,2,1,0:T(8,128)S(1)} %get-tuple-element.65), channel_id=1, source_target_pairs={{0,4},{4,8},{8,12},{1,5},{5,9},{9,13},{2,6},{6,10},{10,14},{3,7},{... | collective-permute-start | bytes 786440 | tf_op jit(solution)/shard_map/ppermute | solution.py:482
  86.0 5.7 %collective-permute-done.4.refs_2_ = f32[2,2,128,128]{3,2,1,0:T(8,128)S(1)} collective-permute-done((f32[2,2,128,128]{3,2,1,0:T(8,128)S(1)}, f32[2,2,128,128]{3,2,1,0:T(8,128)S(1)}, u32[]{:S(2)}, u32[]{:S(2)}) %collective-permute-start.4) | collective-permute-done | bytes 262176 | tf_op jit(solution)/shard_map/ppermute | solution.py:482
  91.7 1.9 forward_section.14
  93.6 4.4 %collective-permute-start.6 = (f32[2,2,128,128]{3,2,1,0:T(8,128)S(1)}, f32[2,2,128,128]{3,2,1,0:T(8,128)S(1)}, u32[]{:S(2)}, u32[]{:S(2)}) collective-permute-start(f32[2,2,128,128]{3,2,1,0:T(8,128)S(1)} %get-tuple-element.67.refs_2_), channel_id=1, source_target_pairs={{0,4},{4,8},{8,12},{1,5},{5,9},{9,13},{2,6},{6,10},{10,14},{3,7},{... | collective-permute-start | bytes 786440 | tf_op jit(solution)/shard_map/ppermute | solution.py:482
  100.5 2.2 collective-permute-done.6.refs_2_
  102.8 1.9 forward_section.15
  104.7 4.4 %collective-permute-start.8 = (f32[2,2,128,128]{3,2,1,0:T(8,128)S(1)}, f32[2,2,128,128]{3,2,1,0:T(8,128)S(1)}, u32[]{:S(2)}, u32[]{:S(2)}) collective-permute-start(f32[2,2,128,128]{3,2,1,0:T(8,128)S(1)} %get-tuple-element.72.refs_3_), channel_id=1, source_target_pairs={{0,4},{4,8},{8,12},{1,5},{5,9},{9,13},{2,6},{6,10},{10,14},{3,7},{... | collective-permute-start | bytes 786440 | tf_op jit(solution)/shard_map/ppermute | solution.py:482
  112.9 1.9 forward_section.16
  114.8 4.4 %collective-permute-start.10 = (f32[2,2,128,128]{3,2,1,0:T(8,128)S(1)}, f32[2,2,128,128]{3,2,1,0:T(8,128)S(1)}, u32[]{:S(2)}, u32[]{:S(2)}) collective-permute-start(f32[2,2,128,128]{3,2,1,0:T(8,128)S(1)} %get-tuple-element.77.refs_3_), channel_id=1, source_target_pairs={{0,4},{4,8},{8,12},{1,5},{5,9},{9,13},{2,6},{6,10},{10,14},{3,7},{... | collective-permute-start | bytes 786440 | tf_op jit(solution)/shard_map/ppermute | solution.py:482
  122.5 2.3 collective-permute-done.refs_2_.refs_1_
  126.1 1.9 forward_section.17
  128.0 8.9 %collective-permute-start.13 = (f32[2,2,128,128]{3,2,1,0:T(8,128)S(1)}, f32[2,2,128,128]{3,2,1,0:T(8,128)S(1)}, u32[]{:S(2)}, u32[]{:S(2)}) collective-permute-start(f32[2,2,128,128]{3,2,1,0:T(8,128)S(1)} %get-tuple-element.82.refs_3_), channel_id=1, source_target_pairs={{0,4},{4,8},{8,12},{1,5},{5,9},{9,13},{2,6},{6,10},{10,14},{3,7},{... | collective-permute-start | bytes 786440 | tf_op jit(solution)/shard_map/ppermute | solution.py:482
  136.9 2.0 backward_section.14
  141.8 1.9 forward_section.18
  143.7 4.7 %collective-permute-start.16 = (f32[2,2,128,128]{3,2,1,0:T(8,128)S(1)}, f32[2,2,128,128]{3,2,1,0:T(8,128)S(1)}, u32[]{:S(2)}, u32[]{:S(2)}) collective-permute-start(f32[2,2,128,128]{3,2,1,0:T(8,128)S(1)} %get-tuple-element.87.refs_3_), channel_id=1, source_target_pairs={{0,4},{4,8},{8,12},{1,5},{5,9},{9,13},{2,6},{6,10},{10,14},{3,7},{... | collective-permute-start | bytes 786440 | tf_op jit(solution)/shard_map/ppermute | solution.py:482
  148.5 1.8 backward_section.15
  154.9 4.5 %collective-permute-done.15.refs_2_ = f32[2,2,128,128]{3,2,1,0:T(8,128)S(1)} collective-permute-done((f32[2,2,128,128]{3,2,1,0:T(8,128)S(1)}, f32[2,2,128,128]{3,2,1,0:T(8,128)S(1)}, u32[]{:S(2)}, u32[]{:S(2)}) %collective-permute-start.15) | collective-permute-done | bytes 262176 | tf_op jit(solution)/shard_map/ppermute | solution.py:482
  159.4 1.8 backward_section.16
  164.9 6.4 %collective-permute-done.18.refs_2_ = f32[2,2,128,128]{3,2,1,0:T(8,128)S(1)} collective-permute-done((f32[2,2,128,128]{3,2,1,0:T(8,128)S(1)}, f32[2,2,128,128]{3,2,1,0:T(8,128)S(1)}, u32[]{:S(2)}, u32[]{:S(2)}) %collective-permute-start.18) | collective-permute-done | bytes 262176 | tf_op jit(solution)/shard_map/ppermute | solution.py:482
  171.3 1.8 backward_section.17
  176.8 4.6 %collective-permute-done.21.refs_2_ = f32[2,2,128,128]{3,2,1,0:T(8,128)S(1)} collective-permute-done((f32[2,2,128,128]{3,2,1,0:T(8,128)S(1)}, f32[2,2,128,128]{3,2,1,0:T(8,128)S(1)}, u32[]{:S(2)}, u32[]{:S(2)}) %collective-permute-start.21) | collective-permute-done | bytes 262176 | tf_op jit(solution)/shard_map/ppermute | solution.py:482
  185.2 2.4 collective-permute-done.25.refs_4_
  188.5 3.9 %collective-permute-done.24.refs_2_ = f32[2,2,128,128]{3,2,1,0:T(8,128)S(1)} collective-permute-done((f32[2,2,128,128]{3,2,1,0:T(8,128)S(1)}, f32[2,2,128,128]{3,2,1,0:T(8,128)S(1)}, u32[]{:S(2)}, u32[]{:S(2)}) %collective-permute-start.24) | collective-permute-done | bytes 262176 | tf_op jit(solution)/shard_map/ppermute | solution.py:482
  197.2 2.2 collective-permute-done.27.refs_4_
  200.6 4.4 %collective-permute-done.26.refs_2_ = f32[2,2,128,128]{3,2,1,0:T(8,128)S(1)} collective-permute-done((f32[2,2,128,128]{3,2,1,0:T(8,128)S(1)}, f32[2,2,128,128]{3,2,1,0:T(8,128)S(1)}, u32[]{:S(2)}, u32[]{:S(2)}) %collective-permute-start.26) | collective-permute-done | bytes 262176 | tf_op jit(solution)/shard_map/ppermute | solution.py:482
  208.1 4.6 %collective-permute-start.32 = (f32[2,2,2,128,128]{4,3,2,1,0:T(8,128)S(1)}, f32[2,2,2,128,128]{4,3,2,1,0:T(8,128)S(1)}, u32[]{:S(2)}, u32[]{:S(2)}) collective-permute-start(f32[2,2,2,128,128]{4,3,2,1,0:T(8,128)S(1)} %get-tuple-element.108.refs_3_), channel_id=1, source_target_pairs={{0,2},{2,0},{4,6},{6,4},{8,10},{10,8},{1,3},{3,1},{5,7},{7,5},{9,1... | collective-permute-start | bytes 1572872 | tf_op jit(solution)/shard_map/ppermute | solution.py:491
  212.8 1.9 collective-permute-start.31
  215.8 2.5 %backward_section.21 = (f32[34176,128]{1,0:T(8,128)S(1)}, f32[2,2,128,128]{3,2,1,0:T(8,128)}, f32[2,2,2,128,128]{4,3,2,1,0:T(8,128)S(1)}) custom-call(s32[35]{0:T(128)S(1)} %pad_add_fusion.refs_0_.info, bf16[2,2,2,256,256]{4,3,2,1,0:T(8,128)(2,1)S(1)} %copy-done.8, ...), custom_call_target="tpu_custom_call", output_to_operand_aliasing={{0}: (3, {})} | custom-call | flops 402653184 | bytes 2097152 | tf_op jit(solution)/shard_map/backward_section/pallas_call | solution.py:147
  218.4 3.9 %collective-permute-start.30 = (f32[2,2,2,128,128]{4,3,2,1,0:T(8,128)S(1)}, f32[2,2,2,128,128]{4,3,2,1,0:T(8,128)S(1)}, u32[]{:S(2)}, u32[]{:S(2)}) collective-permute-start(f32[2,2,2,128,128]{4,3,2,1,0:T(8,128)S(1)} %get-tuple-element.113.refs_3_), channel_id=1, source_target_pairs={{0,2},{2,0},{1,3},{3,1},{16,18},{18,16},{17,19},{19,17}} | collective-permute-start | bytes 1572872 | tf_op jit(solution)/shard_map/ppermute | solution.py:491
  222.3 3.3 %collective-permute-done.32.refs_4_ = f32[2,2,2,128,128]{4,3,2,1,0:T(8,128)S(1)} collective-permute-done((f32[2,2,2,128,128]{4,3,2,1,0:T(8,128)S(1)}, f32[2,2,2,128,128]{4,3,2,1,0:T(8,128)S(1)}, u32[]{:S(2)}, u32[]{:S(2)}) %collective-permute-start.32) | collective-permute-done | bytes 524320 | tf_op jit(solution)/shard_map/ppermute | solution.py:491
  226.7 7.5 %collective-permute-done.31.refs_2_ = f32[2,2,2,128,128]{4,3,2,1,0:T(8,128)S(1)} collective-permute-done((f32[2,2,2,128,128]{4,3,2,1,0:T(8,128)S(1)}, f32[2,2,2,128,128]{4,3,2,1,0:T(8,128)S(1)}, u32[]{:S(2)}, u32[]{:S(2)}) %collective-permute-start.31) | collective-permute-done | bytes 524320 | tf_op jit(solution)/shard_map/ppermute | solution.py:491
  235.1 4.7 %collective-permute-done.30.refs_2_ = f32[2,2,2,128,128]{4,3,2,1,0:T(8,128)S(1)} collective-permute-done((f32[2,2,2,128,128]{4,3,2,1,0:T(8,128)S(1)}, f32[2,2,2,128,128]{4,3,2,1,0:T(8,128)S(1)}, u32[]{:S(2)}, u32[]{:S(2)}) %collective-permute-start.30) | collective-permute-done | bytes 524320 | tf_op jit(solution)/shard_map/ppermute | solution.py:491
  242.3 4.5 %collective-permute-done.33 = f32[2,2,192,768]{3,2,1,0:T(8,128)S(1)} collective-permute-done((f32[2,2,192,768]{3,2,1,0:T(8,128)S(1)}, f32[2,2,192,768]{3,2,1,0:T(8,128)S(1)}, u32[]{:S(2)}, u32[]{:S(2)}) %collective-permute-start.33) | collective-permute-done | bytes 2359328 | tf_op jit(solution)/shard_map/ppermute | solution.py:447
  (86 shorter events, 51.9 us)
Async XLA Ops:
  0.0 10.0 %collective-permute-start.1 = (f32[2,2,384,768]{3,2,1,0:T(8,128)}, f32[2,2,384,768]{3,2,1,0:T(8,128)}, u32[]{:S(2)}, u32[]{:S(2)}) collective-permute-start(f32[2,2,384,768]{3,2,1,0:T(8,128)} %refs_1_.25), channel_id=1, source_target_pairs={{0,1},{1,0},{2,3},{3,2},{4,5},{5,4},{6,7},{7,6},{8,9},{9,8},{10,11... | collective-permute-start | bytes 14155784 | tf_op jit(solution)/shard_map/ppermute | solution.py:447
  3.9 6.1 %copy-start = (f32[34176,128]{1,0:T(8,128)}, f32[34176,128]{1,0:T(8,128)S(1)}, u32[]{:S(2)}) copy-start(f32[34176,128]{1,0:T(8,128)S(1)} %make_state.1.refs_3_) | copy-start | bytes 52494340
  10.0 6.0 %copy-start.1 = (f32[34176,128]{1,0:T(8,128)S(1)}, f32[34176,128]{1,0:T(8,128)}, u32[]{:S(2)}) copy-start(f32[34176,128]{1,0:T(8,128)} %copy-done) | copy-start | bytes 52494340
  16.0 8.3 %copy-start.8 = (bf16[2,2,2,256,256]{4,3,2,1,0:T(8,128)(2,1)S(1)}, bf16[2,2,2,256,256]{4,3,2,1,0:T(8,128)(2,1)}, u32[]{:S(2)}) copy-start(bf16[2,2,2,256,256]{4,3,2,1,0:T(8,128)(2,1)} %constant.19.clone.refs_1_) | copy-start | bytes 3145732
  16.0 8.3 %copy-start.9 = (f32[2,128,128]{2,1,0:T(8,128)S(1)}, f32[2,128,128]{2,1,0:T(8,128)}, u32[]{:S(2)}) copy-start(f32[2,128,128]{2,1,0:T(8,128)} %refs_3_.13) | copy-start | bytes 393220
  18.2 6.1 %copy-start.2 = (f32[34176,128]{1,0:T(8,128)}, f32[34176,128]{1,0:T(8,128)S(1)}, u32[]{:S(2)}) copy-start(f32[34176,128]{1,0:T(8,128)S(1)} %cut_patches.2.refs_3_) | copy-start | bytes 52494340
  24.2 6.0 %copy-start.3 = (f32[34176,128]{1,0:T(8,128)S(1)}, f32[34176,128]{1,0:T(8,128)}, u32[]{:S(2)}) copy-start(f32[34176,128]{1,0:T(8,128)} %copy-done.2) | copy-start | bytes 52494340
  32.1 6.1 %copy-start.4 = (f32[34176,128]{1,0:T(8,128)}, f32[34176,128]{1,0:T(8,128)S(1)}, u32[]{:S(2)}) copy-start(f32[34176,128]{1,0:T(8,128)S(1)} %get-tuple-element.62.refs_3_) | copy-start | bytes 52494340
  38.1 25.9 %collective-permute-start.2 = (f32[2,2,128,128]{3,2,1,0:T(8,128)S(1)}, f32[2,2,128,128]{3,2,1,0:T(8,128)S(1)}, u32[]{:S(2)}, u32[]{:S(2)}) collective-permute-start(f32[2,2,128,128]{3,2,1,0:T(8,128)S(1)} %get-tuple-element.61), channel_id=1, source_target_pairs={{0,4},{1,5},{2,6},{3,7},{16,20},{17,21},{18,22},{19,23}} | collective-permute-start | bytes 786440 | tf_op jit(solution)/shard_map/ppermute | solution.py:482
  41.3 6.0 %copy-start.5 = (f32[34176,128]{1,0:T(8,128)S(1)}, f32[34176,128]{1,0:T(8,128)}, u32[]{:S(2)}) copy-start(f32[34176,128]{1,0:T(8,128)} %copy-done.4) | copy-start | bytes 52494340
  58.0 6.1 %copy-start.6 = (f32[34176,128]{1,0:T(8,128)}, f32[34176,128]{1,0:T(8,128)S(1)}, u32[]{:S(2)}) copy-start(f32[34176,128]{1,0:T(8,128)S(1)} %cut_patches.3.refs_4_) | copy-start | bytes 52494340
  64.0 6.0 %copy-start.7 = (f32[34176,128]{1,0:T(8,128)S(1)}, f32[34176,128]{1,0:T(8,128)}, u32[]{:S(2)}) copy-start(f32[34176,128]{1,0:T(8,128)} %copy-done.6) | copy-start | bytes 52494340
  71.9 7.8 %collective-permute-start.3 = (f32[2,2,128,128]{3,2,1,0:T(8,128)S(1)}, f32[2,2,128,128]{3,2,1,0:T(8,128)S(1)}, u32[]{:S(2)}, u32[]{:S(2)}) collective-permute-start(f32[2,2,128,128]{3,2,1,0:T(8,128)S(1)} %get-tuple-element.63), channel_id=1, source_target_pairs={{0,4},{4,8},{1,5},{5,9},{2,6},{6,10},{3,7},{7,11},{16,20},{20,24},... | collective-permute-start | bytes 786440 | tf_op jit(solution)/shard_map/ppermute | solution.py:482
  81.6 10.1 %collective-permute-start.4 = (f32[2,2,128,128]{3,2,1,0:T(8,128)S(1)}, f32[2,2,128,128]{3,2,1,0:T(8,128)S(1)}, u32[]{:S(2)}, u32[]{:S(2)}) collective-permute-start(f32[2,2,128,128]{3,2,1,0:T(8,128)S(1)} %get-tuple-element.65), channel_id=1, source_target_pairs={{0,4},{4,8},{8,12},{1,5},{5,9},{9,13},{2,6},{6,10},{10,14},{3,7},{... | collective-permute-start | bytes 786440 | tf_op jit(solution)/shard_map/ppermute | solution.py:482
  93.6 9.2 %collective-permute-start.6 = (f32[2,2,128,128]{3,2,1,0:T(8,128)S(1)}, f32[2,2,128,128]{3,2,1,0:T(8,128)S(1)}, u32[]{:S(2)}, u32[]{:S(2)}) collective-permute-start(f32[2,2,128,128]{3,2,1,0:T(8,128)S(1)} %get-tuple-element.67.refs_2_), channel_id=1, source_target_pairs={{0,4},{4,8},{8,12},{1,5},{5,9},{9,13},{2,6},{6,10},{10,14},{3,7},{... | collective-permute-start | bytes 786440 | tf_op jit(solution)/shard_map/ppermute | solution.py:482
  98.5 10.5 %collective-permute-start.5 = (f32[2,2,128,128]{3,2,1,0:T(8,128)S(1)}, f32[2,2,128,128]{3,2,1,0:T(8,128)S(1)}, u32[]{:S(2)}, u32[]{:S(2)}) collective-permute-start(f32[2,2,128,128]{3,2,1,0:T(8,128)S(1)} %get-tuple-element.69), channel_id=1, source_target_pairs={{12,8},{13,9},{14,10},{15,11},{28,24},{29,25},{30,26},{31,27}} | collective-permute-start | bytes 786440 | tf_op jit(solution)/shard_map/ppermute | solution.py:482
  99.2 26.2 %collective-permute-start.11 = (f32[2,2,2,128,128]{4,3,2,1,0:T(8,128)S(1)}, f32[2,2,2,128,128]{4,3,2,1,0:T(8,128)S(1)}, u32[]{:S(2)}, u32[]{:S(2)}) collective-permute-start(f32[2,2,2,128,128]{4,3,2,1,0:T(8,128)S(1)} %get-tuple-element.70.refs_2_), channel_id=1, source_target_pairs={{12,14},{14,12},{13,15},{15,13},{28,30},{30,28},{29,31},{31,29}} | collective-permute-start | bytes 1572872 | tf_op jit(solution)/shard_map/ppermute | solution.py:491
  104.7 8.3 %collective-permute-start.8 = (f32[2,2,128,128]{3,2,1,0:T(8,128)S(1)}, f32[2,2,128,128]{3,2,1,0:T(8,128)S(1)}, u32[]{:S(2)}, u32[]{:S(2)}) collective-permute-start(f32[2,2,128,128]{3,2,1,0:T(8,128)S(1)} %get-tuple-element.72.refs_3_), channel_id=1, source_target_pairs={{0,4},{4,8},{8,12},{1,5},{5,9},{9,13},{2,6},{6,10},{10,14},{3,7},{... | collective-permute-start | bytes 786440 | tf_op jit(solution)/shard_map/ppermute | solution.py:482
  109.6 9.6 %collective-permute-start.7 = (f32[2,2,128,128]{3,2,1,0:T(8,128)S(1)}, f32[2,2,128,128]{3,2,1,0:T(8,128)S(1)}, u32[]{:S(2)}, u32[]{:S(2)}) collective-permute-start(f32[2,2,128,128]{3,2,1,0:T(8,128)S(1)} %get-tuple-element.74), channel_id=1, source_target_pairs={{8,4},{12,8},{9,5},{13,9},{10,6},{14,10},{11,7},{15,11},{24,20},{2... | collective-permute-start | bytes 786440 | tf_op jit(solution)/shard_map/ppermute | solution.py:482
  110.3 30.8 %collective-permute-start.14 = (f32[2,2,2,128,128]{4,3,2,1,0:T(8,128)S(1)}, f32[2,2,2,128,128]{4,3,2,1,0:T(8,128)S(1)}, u32[]{:S(2)}, u32[]{:S(2)}) collective-permute-start(f32[2,2,2,128,128]{4,3,2,1,0:T(8,128)S(1)} %get-tuple-element.75.refs_2_), channel_id=1, source_target_pairs={{8,10},{10,8},{12,14},{14,12},{9,11},{11,9},{13,15},{15,13},{24,26... | collective-permute-start | bytes 1572872 | tf_op jit(solution)/shard_map/ppermute | solution.py:491
  114.8 11.2 %collective-permute-start.10 = (f32[2,2,128,128]{3,2,1,0:T(8,128)S(1)}, f32[2,2,128,128]{3,2,1,0:T(8,128)S(1)}, u32[]{:S(2)}, u32[]{:S(2)}) collective-permute-start(f32[2,2,128,128]{3,2,1,0:T(8,128)S(1)} %get-tuple-element.77.refs_3_), channel_id=1, source_target_pairs={{0,4},{4,8},{8,12},{1,5},{5,9},{9,13},{2,6},{6,10},{10,14},{3,7},{... | collective-permute-start | bytes 786440 | tf_op jit(solution)/shard_map/ppermute | solution.py:482
  119.8 17.1 %collective-permute-start.9 = (f32[2,2,128,128]{3,2,1,0:T(8,128)S(1)}, f32[2,2,128,128]{3,2,1,0:T(8,128)S(1)}, u32[]{:S(2)}, u32[]{:S(2)}) collective-permute-start(f32[2,2,128,128]{3,2,1,0:T(8,128)S(1)} %get-tuple-element.79), channel_id=1, source_target_pairs={{4,0},{8,4},{12,8},{5,1},{9,5},{13,9},{6,2},{10,6},{14,10},{7,3},{... | collective-permute-start | bytes 786440 | tf_op jit(solution)/shard_map/ppermute | solution.py:482
  121.1 3.6 %collective-permute-start = (s32[32]{0:T(128)S(1)}, s32[32]{0:T(128)S(1)}, u32[]{:S(2)}, u32[]{:S(2)}) collective-permute-start(s32[32]{0:T(128)S(1)} %reshape.7.refs_1_), channel_id=1, source_target_pairs={{0,2},{2,0},{1,3},{3,1},{4,6},{6,4},{5,7},{7,5},{8,10},{10,8},{9,1... | collective-permute-start | bytes 392 | tf_op jit(solution)/shard_map/ppermute | solution.py:447
  124.7 28.1 %collective-permute-start.17 = (f32[2,2,2,128,128]{4,3,2,1,0:T(8,128)S(1)}, f32[2,2,2,128,128]{4,3,2,1,0:T(8,128)S(1)}, u32[]{:S(2)}, u32[]{:S(2)}) collective-permute-start(f32[2,2,2,128,128]{4,3,2,1,0:T(8,128)S(1)} %get-tuple-element.80.refs_3_), channel_id=1, source_target_pairs={{4,6},{6,4},{8,10},{10,8},{12,14},{14,12},{5,7},{7,5},{9,11},{11,9... | collective-permute-start | bytes 1572872 | tf_op jit(solution)/shard_map/ppermute | solution.py:491
  128.0 13.9 %collective-permute-start.13 = (f32[2,2,128,128]{3,2,1,0:T(8,128)S(1)}, f32[2,2,128,128]{3,2,1,0:T(8,128)S(1)}, u32[]{:S(2)}, u32[]{:S(2)}) collective-permute-start(f32[2,2,128,128]{3,2,1,0:T(8,128)S(1)} %get-tuple-element.82.refs_3_), channel_id=1, source_target_pairs={{0,4},{4,8},{8,12},{1,5},{5,9},{9,13},{2,6},{6,10},{10,14},{3,7},{... | collective-permute-start | bytes 786440 | tf_op jit(solution)/shard_map/ppermute | solution.py:482
  138.9 9.5 %collective-permute-start.12 = (f32[2,2,128,128]{3,2,1,0:T(8,128)S(1)}, f32[2,2,128,128]{3,2,1,0:T(8,128)S(1)}, u32[]{:S(2)}, u32[]{:S(2)}) collective-permute-start(f32[2,2,128,128]{3,2,1,0:T(8,128)S(1)} %get-tuple-element.84), channel_id=1, source_target_pairs={{4,0},{8,4},{12,8},{5,1},{9,5},{13,9},{6,2},{10,6},{14,10},{7,3},{... | collective-permute-start | bytes 786440 | tf_op jit(solution)/shard_map/ppermute | solution.py:482
  140.2 22.3 %collective-permute-start.20 = (f32[2,2,2,128,128]{4,3,2,1,0:T(8,128)S(1)}, f32[2,2,2,128,128]{4,3,2,1,0:T(8,128)S(1)}, u32[]{:S(2)}, u32[]{:S(2)}) collective-permute-start(f32[2,2,2,128,128]{4,3,2,1,0:T(8,128)S(1)} %get-tuple-element.85.refs_3_), channel_id=1, source_target_pairs={{0,2},{2,0},{4,6},{6,4},{8,10},{10,8},{12,14},{14,12},{1,3},{3,1},... | collective-permute-start | bytes 1572872 | tf_op jit(solution)/shard_map/ppermute | solution.py:491
  143.7 9.9 %collective-permute-start.16 = (f32[2,2,128,128]{3,2,1,0:T(8,128)S(1)}, f32[2,2,128,128]{3,2,1,0:T(8,128)S(1)}, u32[]{:S(2)}, u32[]{:S(2)}) collective-permute-start(f32[2,2,128,128]{3,2,1,0:T(8,128)S(1)} %get-tuple-element.87.refs_3_), channel_id=1, source_target_pairs={{0,4},{4,8},{8,12},{1,5},{5,9},{9,13},{2,6},{6,10},{10,14},{3,7},{... | collective-permute-start | bytes 786440 | tf_op jit(solution)/shard_map/ppermute | solution.py:482
  150.3 9.0 %collective-permute-start.15 = (f32[2,2,128,128]{3,2,1,0:T(8,128)S(1)}, f32[2,2,128,128]{3,2,1,0:T(8,128)S(1)}, u32[]{:S(2)}, u32[]{:S(2)}) collective-permute-start(f32[2,2,128,128]{3,2,1,0:T(8,128)S(1)} %get-tuple-element.89), channel_id=1, source_target_pairs={{4,0},{8,4},{12,8},{5,1},{9,5},{13,9},{6,2},{10,6},{14,10},{7,3},{... | collective-permute-start | bytes 786440 | tf_op jit(solution)/shard_map/ppermute | solution.py:482
  151.6 23.5 %collective-permute-start.23 = (f32[2,2,2,128,128]{4,3,2,1,0:T(8,128)S(1)}, f32[2,2,2,128,128]{4,3,2,1,0:T(8,128)S(1)}, u32[]{:S(2)}, u32[]{:S(2)}) collective-permute-start(f32[2,2,2,128,128]{4,3,2,1,0:T(8,128)S(1)} %get-tuple-element.90.refs_3_), channel_id=1, source_target_pairs={{0,2},{2,0},{4,6},{6,4},{8,10},{10,8},{12,14},{14,12},{1,3},{3,1},... | collective-permute-start | bytes 1572872 | tf_op jit(solution)/shard_map/ppermute | solution.py:491
  154.2 9.4 %collective-permute-start.19 = (f32[2,2,128,128]{3,2,1,0:T(8,128)S(1)}, f32[2,2,128,128]{3,2,1,0:T(8,128)S(1)}, u32[]{:S(2)}, u32[]{:S(2)}) collective-permute-start(f32[2,2,128,128]{3,2,1,0:T(8,128)S(1)} %get-tuple-element.92.refs_3_), channel_id=1, source_target_pairs={{4,8},{8,12},{5,9},{9,13},{6,10},{10,14},{7,11},{11,15},{20,24},{2... | collective-permute-start | bytes 786440 | tf_op jit(solution)/shard_map/ppermute | solution.py:482
  161.2 10.1 %collective-permute-start.18 = (f32[2,2,128,128]{3,2,1,0:T(8,128)S(1)}, f32[2,2,128,128]{3,2,1,0:T(8,128)S(1)}, u32[]{:S(2)}, u32[]{:S(2)}) collective-permute-start(f32[2,2,128,128]{3,2,1,0:T(8,128)S(1)} %get-tuple-element.94), channel_id=1, source_target_pairs={{4,0},{8,4},{12,8},{5,1},{9,5},{13,9},{6,2},{10,6},{14,10},{7,3},{... | collective-permute-start | bytes 786440 | tf_op jit(solution)/shard_map/ppermute | solution.py:482
  164.2 12.0 %collective-permute-start.22 = (f32[2,2,128,128]{3,2,1,0:T(8,128)S(1)}, f32[2,2,128,128]{3,2,1,0:T(8,128)S(1)}, u32[]{:S(2)}, u32[]{:S(2)}) collective-permute-start(f32[2,2,128,128]{3,2,1,0:T(8,128)S(1)} %get-tuple-element.97.refs_3_), channel_id=1, source_target_pairs={{8,12},{9,13},{10,14},{11,15},{24,28},{25,29},{26,30},{27,31}} | collective-permute-start | bytes 786440 | tf_op jit(solution)/shard_map/ppermute | solution.py:482
  173.1 8.3 %collective-permute-start.21 = (f32[2,2,128,128]{3,2,1,0:T(8,128)S(1)}, f32[2,2,128,128]{3,2,1,0:T(8,128)S(1)}, u32[]{:S(2)}, u32[]{:S(2)}) collective-permute-start(f32[2,2,128,128]{3,2,1,0:T(8,128)S(1)} %get-tuple-element.99), channel_id=1, source_target_pairs={{4,0},{8,4},{12,8},{5,1},{9,5},{13,9},{6,2},{10,6},{14,10},{7,3},{... | collective-permute-start | bytes 786440 | tf_op jit(solution)/shard_map/ppermute | solution.py:482
  174.4 13.1 %collective-permute-start.25 = (f32[2,2,2,128,128]{4,3,2,1,0:T(8,128)S(1)}, f32[2,2,2,128,128]{4,3,2,1,0:T(8,128)S(1)}, u32[]{:S(2)}, u32[]{:S(2)}) collective-permute-start(f32[2,2,2,128,128]{4,3,2,1,0:T(8,128)S(1)} %get-tuple-element.95.refs_3_), channel_id=1, source_target_pairs={{0,2},{2,0},{4,6},{6,4},{8,10},{10,8},{12,14},{14,12},{1,3},{3,1},... | collective-permute-start | bytes 1572872 | tf_op jit(solution)/shard_map/ppermute | solution.py:491
  183.2 9.2 %collective-permute-start.24 = (f32[2,2,128,128]{3,2,1,0:T(8,128)S(1)}, f32[2,2,128,128]{3,2,1,0:T(8,128)S(1)}, u32[]{:S(2)}, u32[]{:S(2)}) collective-permute-start(f32[2,2,128,128]{3,2,1,0:T(8,128)S(1)} %get-tuple-element.104), channel_id=1, source_target_pairs={{4,0},{8,4},{12,8},{5,1},{9,5},{13,9},{6,2},{10,6},{14,10},{7,3},{... | collective-permute-start | bytes 786440 | tf_op jit(solution)/shard_map/ppermute | solution.py:482
  184.5 14.9 %collective-permute-start.27 = (f32[2,2,2,128,128]{4,3,2,1,0:T(8,128)S(1)}, f32[2,2,2,128,128]{4,3,2,1,0:T(8,128)S(1)}, u32[]{:S(2)}, u32[]{:S(2)}) collective-permute-start(f32[2,2,2,128,128]{4,3,2,1,0:T(8,128)S(1)} %get-tuple-element.100.refs_3_), channel_id=1, source_target_pairs={{0,2},{2,0},{4,6},{6,4},{8,10},{10,8},{12,14},{14,12},{1,3},{3,1},... | collective-permute-start | bytes 1572872 | tf_op jit(solution)/shard_map/ppermute | solution.py:491
  194.2 10.8 %collective-permute-start.26 = (f32[2,2,128,128]{3,2,1,0:T(8,128)S(1)}, f32[2,2,128,128]{3,2,1,0:T(8,128)S(1)}, u32[]{:S(2)}, u32[]{:S(2)}) collective-permute-start(f32[2,2,128,128]{3,2,1,0:T(8,128)S(1)} %get-tuple-element.107), channel_id=1, source_target_pairs={{4,0},{8,4},{5,1},{9,5},{6,2},{10,6},{7,3},{11,7},{20,16},{24,20},... | collective-permute-start | bytes 786440 | tf_op jit(solution)/shard_map/ppermute | solution.py:482
  195.5 19.2 %collective-permute-start.29 = (f32[2,2,2,128,128]{4,3,2,1,0:T(8,128)S(1)}, f32[2,2,2,128,128]{4,3,2,1,0:T(8,128)S(1)}, u32[]{:S(2)}, u32[]{:S(2)}) collective-permute-start(f32[2,2,2,128,128]{4,3,2,1,0:T(8,128)S(1)} %get-tuple-element.105.refs_3_), channel_id=1, source_target_pairs={{0,2},{2,0},{4,6},{6,4},{8,10},{10,8},{12,14},{14,12},{1,3},{3,1},... | collective-permute-start | bytes 1572872 | tf_op jit(solution)/shard_map/ppermute | solution.py:491
  206.8 9.0 %collective-permute-start.28 = (f32[2,2,128,128]{3,2,1,0:T(8,128)S(1)}, f32[2,2,128,128]{3,2,1,0:T(8,128)S(1)}, u32[]{:S(2)}, u32[]{:S(2)}) collective-permute-start(f32[2,2,128,128]{3,2,1,0:T(8,128)S(1)} %get-tuple-element.110), channel_id=1, source_target_pairs={{4,0},{5,1},{6,2},{7,3},{20,16},{21,17},{22,18},{23,19}} | collective-permute-start | bytes 786440 | tf_op jit(solution)/shard_map/ppermute | solution.py:482
  208.1 17.5 %collective-permute-start.32 = (f32[2,2,2,128,128]{4,3,2,1,0:T(8,128)S(1)}, f32[2,2,2,128,128]{4,3,2,1,0:T(8,128)S(1)}, u32[]{:S(2)}, u32[]{:S(2)}) collective-permute-start(f32[2,2,2,128,128]{4,3,2,1,0:T(8,128)S(1)} %get-tuple-element.108.refs_3_), channel_id=1, source_target_pairs={{0,2},{2,0},{4,6},{6,4},{8,10},{10,8},{1,3},{3,1},{5,7},{7,5},{9,1... | collective-permute-start | bytes 1572872 | tf_op jit(solution)/shard_map/ppermute | solution.py:491
  212.8 21.5 %collective-permute-start.31 = (f32[2,2,2,128,128]{4,3,2,1,0:T(8,128)S(1)}, f32[2,2,2,128,128]{4,3,2,1,0:T(8,128)S(1)}, u32[]{:S(2)}, u32[]{:S(2)}) collective-permute-start(f32[2,2,2,128,128]{4,3,2,1,0:T(8,128)S(1)} %get-tuple-element.111.refs_3_), channel_id=1, source_target_pairs={{0,2},{2,0},{4,6},{6,4},{1,3},{3,1},{5,7},{7,5},{16,18},{18,16},{2... | collective-permute-start | bytes 1572872 | tf_op jit(solution)/shard_map/ppermute | solution.py:491
  218.4 21.5 %collective-permute-start.30 = (f32[2,2,2,128,128]{4,3,2,1,0:T(8,128)S(1)}, f32[2,2,2,128,128]{4,3,2,1,0:T(8,128)S(1)}, u32[]{:S(2)}, u32[]{:S(2)}) collective-permute-start(f32[2,2,2,128,128]{4,3,2,1,0:T(8,128)S(1)} %get-tuple-element.113.refs_3_), channel_id=1, source_target_pairs={{0,2},{2,0},{1,3},{3,1},{16,18},{18,16},{17,19},{19,17}} | collective-permute-start | bytes 1572872 | tf_op jit(solution)/shard_map/ppermute | solution.py:491
  242.2 4.6 %collective-permute-start.33 = (f32[2,2,192,768]{3,2,1,0:T(8,128)S(1)}, f32[2,2,192,768]{3,2,1,0:T(8,128)S(1)}, u32[]{:S(2)}, u32[]{:S(2)}) collective-permute-start(f32[2,2,192,768]{3,2,1,0:T(8,128)S(1)} %bitcast.9), channel_id=1, source_target_pairs={{0,1},{1,0},{2,3},{3,2},{4,5},{5,4},{6,7},{7,6},{8,9},{9,8},{10,11... | collective-permute-start | bytes 7077896 | tf_op jit(solution)/shard_map/ppermute | solution.py:447

commit v5 on v4

--- a/solution.py
+++ b/solution.py
@@ -11,6 +11,7 @@
 from jax.sharding import PartitionSpec as P
 
 FRESNEL = 8.0
+SCOPED = 8 << 20
 CROSSING = 2
 F32 = jnp.float32
 BF16 = jnp.bfloat16
@@ -128,14 +129,15 @@
         block = (part * self.layers + layer) * self.blocks + block
         return self.total_from + block * self.deep + row
 
-    def window(self, corners, probe):
-        row, column = corners[2 * probe], corners[2 * probe + 1]
+    def window(self, info, probe, partner=False):
+        at = 3 + 2 * (probe + partner * self.probes)
+        row, column = info[at], info[at + 1]
         row0 = jnp.minimum(row // 8 * 8, self.height - self.tall)
         block = jnp.minimum(column // self.pixels, self.blocks - 2)
         return row0, row - row0, block, column - block * self.pixels
 
 
-def call(lay, body, state, before, outs, scratch=(), grid=(), prefetch=(), limit=4, flops=0, moved=0, name=None):
+def call(lay, body, state, before, outs, scratch=(), grid=(), prefetch=(), flops=0, moved=0, name=None):
     spaces = {"hbm": (HBM, in_hbm), "vmem": (VMEM, in_vmem), "smem": (SMEM, lambda x: x)}
     specs = [spaces[kind][0] for kind, _ in before]
     operands = [spaces[kind][1](x) for kind, x in before]
@@ -155,7 +157,7 @@
         ),
         out_shape=[pltpu.VMEM(shape, F32) for shape in (lay.shape, *outs)],
         input_output_aliases={at: 0},
-        compiler_params=pltpu.CompilerParams(vmem_limit_bytes=limit << 20),
+        compiler_params=pltpu.CompilerParams(vmem_limit_bytes=SCOPED),
         cost_estimate=pl.CostEstimate(flops=flops, bytes_accessed=moved, transcendentals=0),
         name=name,
     )(*prefetch, *operands, in_vmem(state))
@@ -178,7 +180,7 @@
         out_specs=VMEM,
         out_shape=pltpu.VMEM(lay.shape, F32),
         scratch_shapes=[pltpu.SemaphoreType.DMA(())],
-        compiler_params=pltpu.CompilerParams(vmem_limit_bytes=4 << 20),
+        compiler_params=pltpu.CompilerParams(vmem_limit_bytes=SCOPED),
         name="make_state",
     )(in_hbm(frames.reshape((-1, lay.pixels))))
 
@@ -192,7 +194,7 @@
         steps = pl.num_programs(0)
 
         def copies(step, slot, act):
-            row0, _, block, _ = lay.window(info.at[pl.ds(3, 2 * lay.probes)], begin + step)
+            row0, _, block, _ = lay.window(info, begin + step)
             own_top = info[1] == 0
             for source, is_top, sem in ((own, own_top, 0), (other, jnp.logical_not(own_top), 1)):
                 start = jnp.clip(row0 - jnp.where(is_top, 0, half), 0, half - tall)
@@ -224,7 +226,7 @@
             copies(step + 1, 1 - slot, lambda copy: copy.start())
 
         copies(step, slot, lambda copy: copy.wait())
-        row0, down, _, shift = lay.window(info.at[pl.ds(3, 2 * lay.probes)], begin + step)
+        row0, down, _, shift = lay.window(info, begin + step)
         offset = jnp.where(row0 < half, jnp.maximum(row0 - (half - tall), 0), tall)
         offset = pl.multiple_of(offset, 8)
         turn = (pixels - shift) % pixels
@@ -244,7 +246,7 @@
         lay,
         body,
         state,
-        [("hbm", own), ("hbm", other)],
+        [("hbm", own), ("vmem", other)],
         [],
         scratch=[
             pltpu.VMEM((2, 2, lay.layers, 2 * tall, 2 * pixels), F32),
@@ -252,7 +254,6 @@
         ],
         grid=(end - begin,),
         prefetch=(info,),
-        limit=8,
         flops=size * 4,
         moved=size * 12,
         name="cut_patches",
@@ -370,16 +371,15 @@
     pixels, tall = lay.pixels, lay.tall
 
     def body(info, *refs):
-        state = refs[2 * n]
+        state = refs[n]
         lane = lax.broadcasted_iota(jnp.int32, (tall, pixels), 1)
         blank = jnp.zeros((8, pixels), F32)
-        for which, (tick, _, _) in enumerate(sources):
-            corners, grads = refs[which], refs[n + which]
+        for grads, (tick, partner, _) in zip(refs, sources):
             group = tick - (2 * (sections - 1) - info[0])
             active = (group >= 0) & (group < lay.groups)
             for i in range(lay.count):
                 probe = jnp.clip(group, 0, lay.groups - 1) * lay.count + i
-                row0, down, block, shift = lay.window(corners, probe)
+                row0, down, block, shift = lay.window(info, probe, partner)
                 start = row0 - info[2] + tall
 
                 @pl.when(active & (start > 0) & (start < lay.rows + tall))
@@ -398,9 +398,7 @@
         lay,
         body,
         state,
-        [("smem", info)]
-        + [("smem", corners) for _, corners, _ in sources]
-        + [("vmem", grads) for *_, grads in sources],
+        [("smem", info)] + [("vmem", grads) for *_, grads in sources],
         [],
         flops=size * 8,
         moved=size * 12,
@@ -438,7 +436,7 @@
         out_specs=[VMEM, VMEM],
         out_shape=[pltpu.VMEM(half, F32), pltpu.VMEM(half, F32)],
         scratch_shapes=[pltpu.SemaphoreType.DMA((4 * owners * lay.layers * lay.blocks,))],
-        compiler_params=pltpu.CompilerParams(vmem_limit_bytes=4 << 20),
+        compiler_params=pltpu.CompilerParams(vmem_limit_bytes=SCOPED),
         name="split_rows",
     )(info, in_vmem(state))
 
@@ -464,8 +462,9 @@
     base = lax.axis_index("probe") * half if paired else 0
     lay = Layout(probes, count, layers, pixels, half if paired else height, width)
     lay.height = height
-    info = jnp.concatenate([jnp.stack([section, lax.axis_index("lat"), jnp.int32(base)]), corners])
     partner = swap(corners, "probe") if paired else corners
+    place = jnp.stack([section, lax.axis_index("lat"), jnp.int32(base)])
+    info = jnp.concatenate([place, corners, partner])
     state = make_state(lay, frames)
     state = cut_patches(lay, info, specimen, other, state, 0, count)
 
@@ -504,9 +503,9 @@
         if tick >= sections - 1:
             state, rising, grads = run_backward(lay, tick, sections, info, tables, state, up, own)
             up = pass_on(rising, tick, -1)
-            sources = [(tick, corners, grads)]
+            sources = [(tick, False, grads)]
             if paired:
-                crossing.append((tick, partner, cross(grads, tick)))
+                crossing.append((tick, True, cross(grads, tick)))
                 if len(crossing) > CROSSING:
                     sources.append(crossing.pop(0))
             state = deposit(lay, sections, info, sources, state)

time: 250 us -> 214 us (0.86)
  local copies, waits for them, and re-layouts: 49.6 us -> 13.6 us
  starting transfers between devices: 68.3 us -> 63.6 us
  waiting for transfers between devices: 66.5 us -> 69.8 us
    unnamed x21 -> x9, local copies, waits for them, and re-layouts: 48.9 us -> 12.8 us
    ppermute x20, waiting for transfers between devices: 39.5 us -> 45.2 us  [pass_on(): return lax.ppermute(wave, 'depth', pairs) if pairs else None]
    ppermute x11, starting transfers between devices: 17.7 us -> 14.5 us  [cross(): return lax.ppermute(grads, ('depth', 'probe'), pairs)]
    ppermute x20, starting transfers between devices: 48.7 us -> 46 us  [pass_on(): return lax.ppermute(wave, 'depth', pairs) if pairs else None]
  transfers between devices with their start and end apart: 34 -> 34, of which waited for: 16 -> 17; matrix products, arithmetic and copies ran while one was open for 1% -> 1% of each run, Pallas kernels for 20% -> 23%
where the time goes in v5:
time: 214 us; the launch traced here: 213 us
  waiting for transfers between devices  69.8 us (33%)
  starting transfers between devices  63.6 us (30%)
  Pallas kernels  62.6 us (29%)
  local copies, waits for them, and re-layouts  13.6 us (6%)
  other arithmetic  2.36 us (1%)
    pallas_call x37, Pallas kernels, call(): pl.pallas_call(kernel, grid_spec=pltpu.PrefetchScalarGridSpec(num_scalar_...  59.9 us
    ppermute x20, starting transfers between devices, pass_on(): return lax.ppermute(wave, 'depth', pairs) if pairs else None  46 us
    ppermute x20, waiting for transfers between devices, pass_on(): return lax.ppermute(wave, 'depth', pairs) if pairs else None  45.2 us
    ppermute x11, waiting for transfers between devices, cross(): return lax.ppermute(grads, ('depth', 'probe'), pairs)  20.1 us
    ppermute x11, starting transfers between devices, cross(): return lax.ppermute(grads, ('depth', 'probe'), pairs)  14.5 us
    unnamed x9, local copies, waits for them, and re-layouts  12.8 us
    ppermute x3, waiting for transfers between devices, swap(): return lax.ppermute(shard, axis, [(0, 1), (1, 0)])  4.53 us
  transfers between devices with their start and end apart: 34, of which 17 were waited for; matrix products, arithmetic and copies ran while one was open for 1% of the time, Pallas kernels for 23%

profile of v5, /device:TPU:0, one launch (start us, length us, event | category | flops | bytes accessed | tf_op | source)
XLA Modules:
  0.0 212.5 jit_solution(13945520267832616377)
XLA Ops:
  2.6 2.6 %collective-permute-start = (s32[32]{0:T(128)S(1)}, s32[32]{0:T(128)S(1)}, u32[]{:S(2)}, u32[]{:S(2)}) collective-permute-start(s32[32]{0:T(128)S(1)} %reshape.7), channel_id=1, source_target_pairs={{0,2},{2,0},{1,3},{3,1},{4,6},{6,4},{5,7},{7,5},{8,10},{10,8},{9,1... | collective-permute-start | bytes 392 | tf_op jit(solution)/shard_map/ppermute | solution.py:445
  6.4 6.0 %copy-done = f32[34176,128]{1,0:T(8,128)} copy-done((f32[34176,128]{1,0:T(8,128)}, f32[34176,128]{1,0:T(8,128)S(1)}, u32[]{:S(2)}) %copy-start) | copy-done | bytes 17498136
  12.5 6.0 %copy-done.1 = f32[34176,128]{1,0:T(8,128)S(1)} copy-done((f32[34176,128]{1,0:T(8,128)S(1)}, f32[34176,128]{1,0:T(8,128)}, u32[]{:S(2)}) %copy-start.1) | copy-done | bytes 17498136
  18.5 4.5 %cut_patches.2.refs_3_ = f32[34176,128]{1,0:T(8,128)S(1)} custom-call(s32[67]{0:T(128)S(1)} %concatenate.3.refs_0_.info, f32[2,2,384,768]{3,2,1,0:T(8,128)} %refs_1_.25, f32[2,2,384,768]{3,2,1,0:T(8,128)} %collective-permute-done.1.refs_2_, f32[34176,128]{1,0:T(8,128)S(1)} %copy-done.1), custom_call_target="tpu_custom_call", output_to_operand_aliasing={{}: (3, {})} | custom-call | flops 524288 | bytes 1572864 | tf_op jit(solution)/shard_map/cut_patches/pallas_call | solution.py:149
  23.0 1.9 forward_section.11
  24.9 2.2 %collective-permute-start.2 = (f32[2,2,128,128]{3,2,1,0:T(8,128)S(1)}, f32[2,2,128,128]{3,2,1,0:T(8,128)S(1)}, u32[]{:S(2)}, u32[]{:S(2)}) collective-permute-start(f32[2,2,128,128]{3,2,1,0:T(8,128)S(1)} %get-tuple-element.61), channel_id=1, source_target_pairs={{0,4},{1,5},{2,6},{3,7},{16,20},{17,21},{18,22},{19,23}} | collective-permute-start | bytes 786440 | tf_op jit(solution)/shard_map/ppermute | solution.py:481
  27.1 10.4 %cut_patches.3.refs_4_ = f32[34176,128]{1,0:T(8,128)S(1)} custom-call(s32[67]{0:T(128)S(1)} %concatenate.3.refs_0_.info, f32[2,2,384,768]{3,2,1,0:T(8,128)} %refs_1_.25, f32[2,2,384,768]{3,2,1,0:T(8,128)} %collective-permute-done.1.refs_2_, f32[34176,128]{1,0:T(8,128)S(1)} %get-tuple-element.62.refs_3_), custom_call_target="tpu_custom_call", output_to_operand_aliasing={{}: (3, {})} | custom-call | flops 3670016 | bytes 11010048 | tf_op jit(solution)/shard_map/cut_patches/pallas_call | solution.py:149
  37.5 1.9 forward_section.12
  40.7 5.1 %collective-permute-done.3.refs_2_ = f32[2,2,128,128]{3,2,1,0:T(8,128)S(1)} collective-permute-done((f32[2,2,128,128]{3,2,1,0:T(8,128)S(1)}, f32[2,2,128,128]{3,2,1,0:T(8,128)S(1)}, u32[]{:S(2)}, u32[]{:S(2)}) %collective-permute-start.3) | collective-permute-done | bytes 262176 | tf_op jit(solution)/shard_map/ppermute | solution.py:481
  45.9 1.9 forward_section.13
  47.8 4.4 %collective-permute-start.4 = (f32[2,2,128,128]{3,2,1,0:T(8,128)S(1)}, f32[2,2,128,128]{3,2,1,0:T(8,128)S(1)}, u32[]{:S(2)}, u32[]{:S(2)}) collective-permute-start(f32[2,2,128,128]{3,2,1,0:T(8,128)S(1)} %get-tuple-element.65), channel_id=1, source_target_pairs={{0,4},{4,8},{8,12},{1,5},{5,9},{9,13},{2,6},{6,10},{10,14},{3,7},{... | collective-permute-start | bytes 786440 | tf_op jit(solution)/shard_map/ppermute | solution.py:481
  52.2 6.4 %collective-permute-done.4.refs_2_ = f32[2,2,128,128]{3,2,1,0:T(8,128)S(1)} collective-permute-done((f32[2,2,128,128]{3,2,1,0:T(8,128)S(1)}, f32[2,2,128,128]{3,2,1,0:T(8,128)S(1)}, u32[]{:S(2)}, u32[]{:S(2)}) %collective-permute-start.4) | collective-permute-done | bytes 262176 | tf_op jit(solution)/shard_map/ppermute | solution.py:481
  58.6 1.9 forward_section.14
  60.4 4.4 %collective-permute-start.6 = (f32[2,2,128,128]{3,2,1,0:T(8,128)S(1)}, f32[2,2,128,128]{3,2,1,0:T(8,128)S(1)}, u32[]{:S(2)}, u32[]{:S(2)}) collective-permute-start(f32[2,2,128,128]{3,2,1,0:T(8,128)S(1)} %get-tuple-element.67.refs_2_), channel_id=1, source_target_pairs={{0,4},{4,8},{8,12},{1,5},{5,9},{9,13},{2,6},{6,10},{10,14},{3,7},{... | collective-permute-start | bytes 786440 | tf_op jit(solution)/shard_map/ppermute | solution.py:481
  67.4 3.3 %collective-permute-done.6.refs_2_ = f32[2,2,128,128]{3,2,1,0:T(8,128)S(1)} collective-permute-done((f32[2,2,128,128]{3,2,1,0:T(8,128)S(1)}, f32[2,2,128,128]{3,2,1,0:T(8,128)S(1)}, u32[]{:S(2)}, u32[]{:S(2)}) %collective-permute-start.6) | collective-permute-done | bytes 262176 | tf_op jit(solution)/shard_map/ppermute | solution.py:481
  70.7 1.9 forward_section.15
  72.5 4.4 %collective-permute-start.8 = (f32[2,2,128,128]{3,2,1,0:T(8,128)S(1)}, f32[2,2,128,128]{3,2,1,0:T(8,128)S(1)}, u32[]{:S(2)}, u32[]{:S(2)}) collective-permute-start(f32[2,2,128,128]{3,2,1,0:T(8,128)S(1)} %get-tuple-element.72.refs_3_), channel_id=1, source_target_pairs={{0,4},{4,8},{8,12},{1,5},{5,9},{9,13},{2,6},{6,10},{10,14},{3,7},{... | collective-permute-start | bytes 786440 | tf_op jit(solution)/shard_map/ppermute | solution.py:481
  79.5 2.4 %collective-permute-done.8.refs_2_ = f32[2,2,128,128]{3,2,1,0:T(8,128)S(1)} collective-permute-done((f32[2,2,128,128]{3,2,1,0:T(8,128)S(1)}, f32[2,2,128,128]{3,2,1,0:T(8,128)S(1)}, u32[]{:S(2)}, u32[]{:S(2)}) %collective-permute-start.8) | collective-permute-done | bytes 262176 | tf_op jit(solution)/shard_map/ppermute | solution.py:481
  81.9 1.9 forward_section.16
  83.8 4.4 %collective-permute-start.10 = (f32[2,2,128,128]{3,2,1,0:T(8,128)S(1)}, f32[2,2,128,128]{3,2,1,0:T(8,128)S(1)}, u32[]{:S(2)}, u32[]{:S(2)}) collective-permute-start(f32[2,2,128,128]{3,2,1,0:T(8,128)S(1)} %get-tuple-element.77.refs_3_), channel_id=1, source_target_pairs={{0,4},{4,8},{8,12},{1,5},{5,9},{9,13},{2,6},{6,10},{10,14},{3,7},{... | collective-permute-start | bytes 786440 | tf_op jit(solution)/shard_map/ppermute | solution.py:481
  92.3 1.9 forward_section.17
  94.2 7.3 %collective-permute-start.13 = (f32[2,2,128,128]{3,2,1,0:T(8,128)S(1)}, f32[2,2,128,128]{3,2,1,0:T(8,128)S(1)}, u32[]{:S(2)}, u32[]{:S(2)}) collective-permute-start(f32[2,2,128,128]{3,2,1,0:T(8,128)S(1)} %get-tuple-element.82.refs_3_), channel_id=1, source_target_pairs={{0,4},{4,8},{8,12},{1,5},{5,9},{9,13},{2,6},{6,10},{10,14},{3,7},{... | collective-permute-start | bytes 786440 | tf_op jit(solution)/shard_map/ppermute | solution.py:481
  101.5 2.0 backward_section.14
  107.1 1.9 forward_section.18
  109.0 4.6 %collective-permute-start.16 = (f32[2,2,128,128]{3,2,1,0:T(8,128)S(1)}, f32[2,2,128,128]{3,2,1,0:T(8,128)S(1)}, u32[]{:S(2)}, u32[]{:S(2)}) collective-permute-start(f32[2,2,128,128]{3,2,1,0:T(8,128)S(1)} %get-tuple-element.87.refs_3_), channel_id=1, source_target_pairs={{0,4},{4,8},{8,12},{1,5},{5,9},{9,13},{2,6},{6,10},{10,14},{3,7},{... | collective-permute-start | bytes 786440 | tf_op jit(solution)/shard_map/ppermute | solution.py:481
  113.5 1.8 backward_section.15
  119.7 4.3 %collective-permute-done.15.refs_2_ = f32[2,2,128,128]{3,2,1,0:T(8,128)S(1)} collective-permute-done((f32[2,2,128,128]{3,2,1,0:T(8,128)S(1)}, f32[2,2,128,128]{3,2,1,0:T(8,128)S(1)}, u32[]{:S(2)}, u32[]{:S(2)}) %collective-permute-start.15) | collective-permute-done | bytes 262176 | tf_op jit(solution)/shard_map/ppermute | solution.py:481
  123.9 1.8 backward_section.16
  129.4 6.0 %collective-permute-done.18.refs_2_ = f32[2,2,128,128]{3,2,1,0:T(8,128)S(1)} collective-permute-done((f32[2,2,128,128]{3,2,1,0:T(8,128)S(1)}, f32[2,2,128,128]{3,2,1,0:T(8,128)S(1)}, u32[]{:S(2)}, u32[]{:S(2)}) %collective-permute-start.18) | collective-permute-done | bytes 262176 | tf_op jit(solution)/shard_map/ppermute | solution.py:481
  135.5 1.8 backward_section.17
  138.6 1.3 collective-permute-start.25
  141.3 4.5 %collective-permute-done.21.refs_2_ = f32[2,2,128,128]{3,2,1,0:T(8,128)S(1)} collective-permute-done((f32[2,2,128,128]{3,2,1,0:T(8,128)S(1)}, f32[2,2,128,128]{3,2,1,0:T(8,128)S(1)}, u32[]{:S(2)}, u32[]{:S(2)}) %collective-permute-start.21) | collective-permute-done | bytes 262176 | tf_op jit(solution)/shard_map/ppermute | solution.py:481
  145.9 1.8 backward_section.18
  152.1 5.3 %collective-permute-done.24.refs_2_ = f32[2,2,128,128]{3,2,1,0:T(8,128)S(1)} collective-permute-done((f32[2,2,128,128]{3,2,1,0:T(8,128)S(1)}, f32[2,2,128,128]{3,2,1,0:T(8,128)S(1)}, u32[]{:S(2)}, u32[]{:S(2)}) %collective-permute-start.24) | collective-permute-done | bytes 262176 | tf_op jit(solution)/shard_map/ppermute | solution.py:481
  157.4 1.8 backward_section.19
  160.6 2.4 %collective-permute-done.27.refs_2_ = f32[2,2,2,128,128]{4,3,2,1,0:T(8,128)S(1)} collective-permute-done((f32[2,2,2,128,128]{4,3,2,1,0:T(8,128)S(1)}, f32[2,2,2,128,128]{4,3,2,1,0:T(8,128)S(1)}, u32[]{:S(2)}, u32[]{:S(2)}) %collective-permute-start.27) | collective-permute-done | bytes 524320 | tf_op jit(solution)/shard_map/ppermute | solution.py:490
  164.2 6.7 %collective-permute-done.26.refs_2_ = f32[2,2,128,128]{3,2,1,0:T(8,128)S(1)} collective-permute-done((f32[2,2,128,128]{3,2,1,0:T(8,128)S(1)}, f32[2,2,128,128]{3,2,1,0:T(8,128)S(1)}, u32[]{:S(2)}, u32[]{:S(2)}) %collective-permute-start.26) | collective-permute-done | bytes 262176 | tf_op jit(solution)/shard_map/ppermute | solution.py:481
  170.9 1.8 backward_section.20
  174.0 1.9 collective-permute-start.32
  176.0 3.9 %collective-permute-start.31 = (f32[2,2,2,128,128]{4,3,2,1,0:T(8,128)S(1)}, f32[2,2,2,128,128]{4,3,2,1,0:T(8,128)S(1)}, u32[]{:S(2)}, u32[]{:S(2)}) collective-permute-start(f32[2,2,2,128,128]{4,3,2,1,0:T(8,128)S(1)} %get-tuple-element.111.refs_1_), channel_id=1, source_target_pairs={{0,2},{2,0},{4,6},{6,4},{1,3},{3,1},{5,7},{7,5},{16,18},{18,16},{2... | collective-permute-start | bytes 1572872 | tf_op jit(solution)/shard_map/ppermute | solution.py:490
  181.0 2.5 %backward_section.21 = (f32[34176,128]{1,0:T(8,128)S(1)}, f32[2,2,128,128]{3,2,1,0:T(8,128)}, f32[2,2,2,128,128]{4,3,2,1,0:T(8,128)S(1)}) custom-call(s32[67]{0:T(128)S(1)} %concatenate.3.refs_0_.info, bf16[2,2,2,256,256]{4,3,2,1,0:T(8,128)(2,1)S(1)} %copy-done.2, ...), custom_call_target="tpu_custom_call", output_to_operand_aliasing={{0}: (3, {})} | custom-call | flops 402653184 | bytes 2097152 | tf_op jit(solution)/shard_map/backward_section/pallas_call | solution.py:149
  183.5 1.9 collective-permute-start.30
  185.5 5.3 %collective-permute-done.32.refs_2_ = f32[2,2,2,128,128]{4,3,2,1,0:T(8,128)S(1)} collective-permute-done((f32[2,2,2,128,128]{4,3,2,1,0:T(8,128)S(1)}, f32[2,2,2,128,128]{4,3,2,1,0:T(8,128)S(1)}, u32[]{:S(2)}, u32[]{:S(2)}) %collective-permute-start.32) | collective-permute-done | bytes 524320 | tf_op jit(solution)/shard_map/ppermute | solution.py:490
  191.7 6.7 %collective-permute-done.31.refs_1_ = f32[2,2,2,128,128]{4,3,2,1,0:T(8,128)S(1)} collective-permute-done((f32[2,2,2,128,128]{4,3,2,1,0:T(8,128)S(1)}, f32[2,2,2,128,128]{4,3,2,1,0:T(8,128)S(1)}, u32[]{:S(2)}, u32[]{:S(2)}) %collective-permute-start.31) | collective-permute-done | bytes 524320 | tf_op jit(solution)/shard_map/ppermute | solution.py:490
  199.3 4.7 %collective-permute-done.30.refs_1_ = f32[2,2,2,128,128]{4,3,2,1,0:T(8,128)S(1)} collective-permute-done((f32[2,2,2,128,128]{4,3,2,1,0:T(8,128)S(1)}, f32[2,2,2,128,128]{4,3,2,1,0:T(8,128)S(1)}, u32[]{:S(2)}, u32[]{:S(2)}) %collective-permute-start.30) | collective-permute-done | bytes 524320 | tf_op jit(solution)/shard_map/ppermute | solution.py:490
  204.8 1.4 split_rows.1
  206.3 4.5 %collective-permute-done.33 = f32[2,2,192,768]{3,2,1,0:T(8,128)S(1)} collective-permute-done((f32[2,2,192,768]{3,2,1,0:T(8,128)S(1)}, f32[2,2,192,768]{3,2,1,0:T(8,128)S(1)}, u32[]{:S(2)}, u32[]{:S(2)}) %collective-permute-start.33) | collective-permute-done | bytes 2359328 | tf_op jit(solution)/shard_map/ppermute | solution.py:445
  210.8 1.7 bitcast_add_fusion
  (74 shorter events, 40.2 us)
Async XLA Ops:
  0.0 12.5 %collective-permute-start.1 = (f32[2,2,384,768]{3,2,1,0:T(8,128)}, f32[2,2,384,768]{3,2,1,0:T(8,128)}, u32[]{:S(2)}, u32[]{:S(2)}) collective-permute-start(f32[2,2,384,768]{3,2,1,0:T(8,128)} %refs_1_.25), channel_id=1, source_target_pairs={{0,1},{1,0},{2,3},{3,2},{4,5},{5,4},{6,7},{7,6},{8,9},{9,8},{10,11... | collective-permute-start | bytes 14155784 | tf_op jit(solution)/shard_map/ppermute | solution.py:445
  2.6 9.8 %collective-permute-start = (s32[32]{0:T(128)S(1)}, s32[32]{0:T(128)S(1)}, u32[]{:S(2)}, u32[]{:S(2)}) collective-permute-start(s32[32]{0:T(128)S(1)} %reshape.7), channel_id=1, source_target_pairs={{0,2},{2,0},{1,3},{3,1},{4,6},{6,4},{5,7},{7,5},{8,10},{10,8},{9,1... | collective-permute-start | bytes 392 | tf_op jit(solution)/shard_map/ppermute | solution.py:445
  6.4 6.0 %copy-start = (f32[34176,128]{1,0:T(8,128)}, f32[34176,128]{1,0:T(8,128)S(1)}, u32[]{:S(2)}) copy-start(f32[34176,128]{1,0:T(8,128)S(1)} %make_state.1.refs_3_) | copy-start | bytes 52494340
  12.5 6.0 %copy-start.1 = (f32[34176,128]{1,0:T(8,128)S(1)}, f32[34176,128]{1,0:T(8,128)}, u32[]{:S(2)}) copy-start(f32[34176,128]{1,0:T(8,128)} %copy-done) | copy-start | bytes 52494340
  18.5 4.5 %copy-start.2 = (bf16[2,2,2,256,256]{4,3,2,1,0:T(8,128)(2,1)S(1)}, bf16[2,2,2,256,256]{4,3,2,1,0:T(8,128)(2,1)}, u32[]{:S(2)}) copy-start(bf16[2,2,2,256,256]{4,3,2,1,0:T(8,128)(2,1)} %constant.19.clone.refs_1_) | copy-start | bytes 3145732
  18.5 4.5 %copy-start.3 = (f32[2,128,128]{2,1,0:T(8,128)S(1)}, f32[2,128,128]{2,1,0:T(8,128)}, u32[]{:S(2)}) copy-start(f32[2,128,128]{2,1,0:T(8,128)} %refs_3_.13) | copy-start | bytes 393220
  24.9 12.6 %collective-permute-start.2 = (f32[2,2,128,128]{3,2,1,0:T(8,128)S(1)}, f32[2,2,128,128]{3,2,1,0:T(8,128)S(1)}, u32[]{:S(2)}, u32[]{:S(2)}) collective-permute-start(f32[2,2,128,128]{3,2,1,0:T(8,128)S(1)} %get-tuple-element.61), channel_id=1, source_target_pairs={{0,4},{1,5},{2,6},{3,7},{16,20},{17,21},{18,22},{19,23}} | collective-permute-start | bytes 786440 | tf_op jit(solution)/shard_map/ppermute | solution.py:481
  39.4 6.5 %collective-permute-start.3 = (f32[2,2,128,128]{3,2,1,0:T(8,128)S(1)}, f32[2,2,128,128]{3,2,1,0:T(8,128)S(1)}, u32[]{:S(2)}, u32[]{:S(2)}) collective-permute-start(f32[2,2,128,128]{3,2,1,0:T(8,128)S(1)} %get-tuple-element.63), channel_id=1, source_target_pairs={{0,4},{4,8},{1,5},{5,9},{2,6},{6,10},{3,7},{7,11},{16,20},{20,24},... | collective-permute-start | bytes 786440 | tf_op jit(solution)/shard_map/ppermute | solution.py:481
  47.8 10.8 %collective-permute-start.4 = (f32[2,2,128,128]{3,2,1,0:T(8,128)S(1)}, f32[2,2,128,128]{3,2,1,0:T(8,128)S(1)}, u32[]{:S(2)}, u32[]{:S(2)}) collective-permute-start(f32[2,2,128,128]{3,2,1,0:T(8,128)S(1)} %get-tuple-element.65), channel_id=1, source_target_pairs={{0,4},{4,8},{8,12},{1,5},{5,9},{9,13},{2,6},{6,10},{10,14},{3,7},{... | collective-permute-start | bytes 786440 | tf_op jit(solution)/shard_map/ppermute | solution.py:481
  60.4 10.2 %collective-permute-start.6 = (f32[2,2,128,128]{3,2,1,0:T(8,128)S(1)}, f32[2,2,128,128]{3,2,1,0:T(8,128)S(1)}, u32[]{:S(2)}, u32[]{:S(2)}) collective-permute-start(f32[2,2,128,128]{3,2,1,0:T(8,128)S(1)} %get-tuple-element.67.refs_2_), channel_id=1, source_target_pairs={{0,4},{4,8},{8,12},{1,5},{5,9},{9,13},{2,6},{6,10},{10,14},{3,7},{... | collective-permute-start | bytes 786440 | tf_op jit(solution)/shard_map/ppermute | solution.py:481
  65.4 11.6 %collective-permute-start.5 = (f32[2,2,128,128]{3,2,1,0:T(8,128)S(1)}, f32[2,2,128,128]{3,2,1,0:T(8,128)S(1)}, u32[]{:S(2)}, u32[]{:S(2)}) collective-permute-start(f32[2,2,128,128]{3,2,1,0:T(8,128)S(1)} %get-tuple-element.69), channel_id=1, source_target_pairs={{12,8},{13,9},{14,10},{15,11},{28,24},{29,25},{30,26},{31,27}} | collective-permute-start | bytes 786440 | tf_op jit(solution)/shard_map/ppermute | solution.py:481
  66.1 24.7 %collective-permute-start.11 = (f32[2,2,2,128,128]{4,3,2,1,0:T(8,128)S(1)}, f32[2,2,2,128,128]{4,3,2,1,0:T(8,128)S(1)}, u32[]{:S(2)}, u32[]{:S(2)}) collective-permute-start(f32[2,2,2,128,128]{4,3,2,1,0:T(8,128)S(1)} %get-tuple-element.70.refs_1_), channel_id=1, source_target_pairs={{12,14},{14,12},{13,15},{15,13},{28,30},{30,28},{29,31},{31,29}} | collective-permute-start | bytes 1572872 | tf_op jit(solution)/shard_map/ppermute | solution.py:490
  72.5 9.4 %collective-permute-start.8 = (f32[2,2,128,128]{3,2,1,0:T(8,128)S(1)}, f32[2,2,128,128]{3,2,1,0:T(8,128)S(1)}, u32[]{:S(2)}, u32[]{:S(2)}) collective-permute-start(f32[2,2,128,128]{3,2,1,0:T(8,128)S(1)} %get-tuple-element.72.refs_3_), channel_id=1, source_target_pairs={{0,4},{4,8},{8,12},{1,5},{5,9},{9,13},{2,6},{6,10},{10,14},{3,7},{... | collective-permute-start | bytes 786440 | tf_op jit(solution)/shard_map/ppermute | solution.py:481
  77.5 10.7 %collective-permute-start.7 = (f32[2,2,128,128]{3,2,1,0:T(8,128)S(1)}, f32[2,2,128,128]{3,2,1,0:T(8,128)S(1)}, u32[]{:S(2)}, u32[]{:S(2)}) collective-permute-start(f32[2,2,128,128]{3,2,1,0:T(8,128)S(1)} %get-tuple-element.74), channel_id=1, source_target_pairs={{8,4},{12,8},{9,5},{13,9},{10,6},{14,10},{11,7},{15,11},{24,20},{2... | collective-permute-start | bytes 786440 | tf_op jit(solution)/shard_map/ppermute | solution.py:481
  78.2 27.9 %collective-permute-start.14 = (f32[2,2,2,128,128]{4,3,2,1,0:T(8,128)S(1)}, f32[2,2,2,128,128]{4,3,2,1,0:T(8,128)S(1)}, u32[]{:S(2)}, u32[]{:S(2)}) collective-permute-start(f32[2,2,2,128,128]{4,3,2,1,0:T(8,128)S(1)} %get-tuple-element.75.refs_1_), channel_id=1, source_target_pairs={{8,10},{10,8},{12,14},{14,12},{9,11},{11,9},{13,15},{15,13},{24,26... | collective-permute-start | bytes 1572872 | tf_op jit(solution)/shard_map/ppermute | solution.py:490
  83.8 8.5 %collective-permute-start.10 = (f32[2,2,128,128]{3,2,1,0:T(8,128)S(1)}, f32[2,2,128,128]{3,2,1,0:T(8,128)S(1)}, u32[]{:S(2)}, u32[]{:S(2)}) collective-permute-start(f32[2,2,128,128]{3,2,1,0:T(8,128)S(1)} %get-tuple-element.77.refs_3_), channel_id=1, source_target_pairs={{0,4},{4,8},{8,12},{1,5},{5,9},{9,13},{2,6},{6,10},{10,14},{3,7},{... | collective-permute-start | bytes 786440 | tf_op jit(solution)/shard_map/ppermute | solution.py:481
  88.8 12.7 %collective-permute-start.9 = (f32[2,2,128,128]{3,2,1,0:T(8,128)S(1)}, f32[2,2,128,128]{3,2,1,0:T(8,128)S(1)}, u32[]{:S(2)}, u32[]{:S(2)}) collective-permute-start(f32[2,2,128,128]{3,2,1,0:T(8,128)S(1)} %get-tuple-element.79), channel_id=1, source_target_pairs={{4,0},{8,4},{12,8},{5,1},{9,5},{13,9},{6,2},{10,6},{14,10},{7,3},{... | collective-permute-start | bytes 786440 | tf_op jit(solution)/shard_map/ppermute | solution.py:481
  90.1 27.5 %collective-permute-start.17 = (f32[2,2,2,128,128]{4,3,2,1,0:T(8,128)S(1)}, f32[2,2,2,128,128]{4,3,2,1,0:T(8,128)S(1)}, u32[]{:S(2)}, u32[]{:S(2)}) collective-permute-start(f32[2,2,2,128,128]{4,3,2,1,0:T(8,128)S(1)} %get-tuple-element.80.refs_1_), channel_id=1, source_target_pairs={{4,6},{6,4},{8,10},{10,8},{12,14},{14,12},{5,7},{7,5},{9,11},{11,9... | collective-permute-start | bytes 1572872 | tf_op jit(solution)/shard_map/ppermute | solution.py:490
  94.2 12.9 %collective-permute-start.13 = (f32[2,2,128,128]{3,2,1,0:T(8,128)S(1)}, f32[2,2,128,128]{3,2,1,0:T(8,128)S(1)}, u32[]{:S(2)}, u32[]{:S(2)}) collective-permute-start(f32[2,2,128,128]{3,2,1,0:T(8,128)S(1)} %get-tuple-element.82.refs_3_), channel_id=1, source_target_pairs={{0,4},{4,8},{8,12},{1,5},{5,9},{9,13},{2,6},{6,10},{10,14},{3,7},{... | collective-permute-start | bytes 786440 | tf_op jit(solution)/shard_map/ppermute | solution.py:481
  103.6 9.9 %collective-permute-start.12 = (f32[2,2,128,128]{3,2,1,0:T(8,128)S(1)}, f32[2,2,128,128]{3,2,1,0:T(8,128)S(1)}, u32[]{:S(2)}, u32[]{:S(2)}) collective-permute-start(f32[2,2,128,128]{3,2,1,0:T(8,128)S(1)} %get-tuple-element.84), channel_id=1, source_target_pairs={{4,0},{8,4},{12,8},{5,1},{9,5},{13,9},{6,2},{10,6},{14,10},{7,3},{... | collective-permute-start | bytes 786440 | tf_op jit(solution)/shard_map/ppermute | solution.py:481
  104.9 22.2 %collective-permute-start.20 = (f32[2,2,2,128,128]{4,3,2,1,0:T(8,128)S(1)}, f32[2,2,2,128,128]{4,3,2,1,0:T(8,128)S(1)}, u32[]{:S(2)}, u32[]{:S(2)}) collective-permute-start(f32[2,2,2,128,128]{4,3,2,1,0:T(8,128)S(1)} %get-tuple-element.85.refs_1_), channel_id=1, source_target_pairs={{0,2},{2,0},{4,6},{6,4},{8,10},{10,8},{12,14},{14,12},{1,3},{3,1},... | collective-permute-start | bytes 1572872 | tf_op jit(solution)/shard_map/ppermute | solution.py:490
  109.0 9.5 %collective-permute-start.16 = (f32[2,2,128,128]{3,2,1,0:T(8,128)S(1)}, f32[2,2,128,128]{3,2,1,0:T(8,128)S(1)}, u32[]{:S(2)}, u32[]{:S(2)}) collective-permute-start(f32[2,2,128,128]{3,2,1,0:T(8,128)S(1)} %get-tuple-element.87.refs_3_), channel_id=1, source_target_pairs={{0,4},{4,8},{8,12},{1,5},{5,9},{9,13},{2,6},{6,10},{10,14},{3,7},{... | collective-permute-start | bytes 786440 | tf_op jit(solution)/shard_map/ppermute | solution.py:481
  115.4 8.6 %collective-permute-start.15 = (f32[2,2,128,128]{3,2,1,0:T(8,128)S(1)}, f32[2,2,128,128]{3,2,1,0:T(8,128)S(1)}, u32[]{:S(2)}, u32[]{:S(2)}) collective-permute-start(f32[2,2,128,128]{3,2,1,0:T(8,128)S(1)} %get-tuple-element.89), channel_id=1, source_target_pairs={{4,0},{8,4},{12,8},{5,1},{9,5},{13,9},{6,2},{10,6},{14,10},{7,3},{... | collective-permute-start | bytes 786440 | tf_op jit(solution)/shard_map/ppermute | solution.py:481
  116.7 23.3 %collective-permute-start.23 = (f32[2,2,2,128,128]{4,3,2,1,0:T(8,128)S(1)}, f32[2,2,2,128,128]{4,3,2,1,0:T(8,128)S(1)}, u32[]{:S(2)}, u32[]{:S(2)}) collective-permute-start(f32[2,2,2,128,128]{4,3,2,1,0:T(8,128)S(1)} %get-tuple-element.90.refs_1_), channel_id=1, source_target_pairs={{0,2},{2,0},{4,6},{6,4},{8,10},{10,8},{12,14},{14,12},{1,3},{3,1},... | collective-permute-start | bytes 1572872 | tf_op jit(solution)/shard_map/ppermute | solution.py:490
  119.0 9.2 %collective-permute-start.19 = (f32[2,2,128,128]{3,2,1,0:T(8,128)S(1)}, f32[2,2,128,128]{3,2,1,0:T(8,128)S(1)}, u32[]{:S(2)}, u32[]{:S(2)}) collective-permute-start(f32[2,2,128,128]{3,2,1,0:T(8,128)S(1)} %get-tuple-element.92.refs_3_), channel_id=1, source_target_pairs={{4,8},{8,12},{5,9},{9,13},{6,10},{10,14},{7,11},{11,15},{20,24},{2... | collective-permute-start | bytes 786440 | tf_op jit(solution)/shard_map/ppermute | solution.py:481
  125.8 9.7 %collective-permute-start.18 = (f32[2,2,128,128]{3,2,1,0:T(8,128)S(1)}, f32[2,2,128,128]{3,2,1,0:T(8,128)S(1)}, u32[]{:S(2)}, u32[]{:S(2)}) collective-permute-start(f32[2,2,128,128]{3,2,1,0:T(8,128)S(1)} %get-tuple-element.94), channel_id=1, source_target_pairs={{4,0},{8,4},{12,8},{5,1},{9,5},{13,9},{6,2},{10,6},{14,10},{7,3},{... | collective-permute-start | bytes 786440 | tf_op jit(solution)/shard_map/ppermute | solution.py:481
  128.8 12.0 %collective-permute-start.22 = (f32[2,2,128,128]{3,2,1,0:T(8,128)S(1)}, f32[2,2,128,128]{3,2,1,0:T(8,128)S(1)}, u32[]{:S(2)}, u32[]{:S(2)}) collective-permute-start(f32[2,2,128,128]{3,2,1,0:T(8,128)S(1)} %get-tuple-element.97.refs_3_), channel_id=1, source_target_pairs={{8,12},{9,13},{10,14},{11,15},{24,28},{25,29},{26,30},{27,31}} | collective-permute-start | bytes 786440 | tf_op jit(solution)/shard_map/ppermute | solution.py:481
  137.3 8.6 %collective-permute-start.21 = (f32[2,2,128,128]{3,2,1,0:T(8,128)S(1)}, f32[2,2,128,128]{3,2,1,0:T(8,128)S(1)}, u32[]{:S(2)}, u32[]{:S(2)}) collective-permute-start(f32[2,2,128,128]{3,2,1,0:T(8,128)S(1)} %get-tuple-element.99), channel_id=1, source_target_pairs={{4,0},{8,4},{12,8},{5,1},{9,5},{13,9},{6,2},{10,6},{14,10},{7,3},{... | collective-permute-start | bytes 786440 | tf_op jit(solution)/shard_map/ppermute | solution.py:481
  138.6 12.4 %collective-permute-start.25 = (f32[2,2,2,128,128]{4,3,2,1,0:T(8,128)S(1)}, f32[2,2,2,128,128]{4,3,2,1,0:T(8,128)S(1)}, u32[]{:S(2)}, u32[]{:S(2)}) collective-permute-start(f32[2,2,2,128,128]{4,3,2,1,0:T(8,128)S(1)} %get-tuple-element.95.refs_1_), channel_id=1, source_target_pairs={{0,2},{2,0},{4,6},{6,4},{8,10},{10,8},{12,14},{14,12},{1,3},{3,1},... | collective-permute-start | bytes 1572872 | tf_op jit(solution)/shard_map/ppermute | solution.py:490
  147.7 9.7 %collective-permute-start.24 = (f32[2,2,128,128]{3,2,1,0:T(8,128)S(1)}, f32[2,2,128,128]{3,2,1,0:T(8,128)S(1)}, u32[]{:S(2)}, u32[]{:S(2)}) collective-permute-start(f32[2,2,128,128]{3,2,1,0:T(8,128)S(1)} %get-tuple-element.104), channel_id=1, source_target_pairs={{4,0},{8,4},{12,8},{5,1},{9,5},{13,9},{6,2},{10,6},{14,10},{7,3},{... | collective-permute-start | bytes 786440 | tf_op jit(solution)/shard_map/ppermute | solution.py:481
  149.0 14.0 %collective-permute-start.27 = (f32[2,2,2,128,128]{4,3,2,1,0:T(8,128)S(1)}, f32[2,2,2,128,128]{4,3,2,1,0:T(8,128)S(1)}, u32[]{:S(2)}, u32[]{:S(2)}) collective-permute-start(f32[2,2,2,128,128]{4,3,2,1,0:T(8,128)S(1)} %get-tuple-element.100.refs_1_), channel_id=1, source_target_pairs={{0,2},{2,0},{4,6},{6,4},{8,10},{10,8},{12,14},{14,12},{1,3},{3,1},... | collective-permute-start | bytes 1572872 | tf_op jit(solution)/shard_map/ppermute | solution.py:490
  159.3 11.6 %collective-permute-start.26 = (f32[2,2,128,128]{3,2,1,0:T(8,128)S(1)}, f32[2,2,128,128]{3,2,1,0:T(8,128)S(1)}, u32[]{:S(2)}, u32[]{:S(2)}) collective-permute-start(f32[2,2,128,128]{3,2,1,0:T(8,128)S(1)} %get-tuple-element.107), channel_id=1, source_target_pairs={{4,0},{8,4},{5,1},{9,5},{6,2},{10,6},{7,3},{11,7},{20,16},{24,20},... | collective-permute-start | bytes 786440 | tf_op jit(solution)/shard_map/ppermute | solution.py:481
  160.6 19.3 %collective-permute-start.29 = (f32[2,2,2,128,128]{4,3,2,1,0:T(8,128)S(1)}, f32[2,2,2,128,128]{4,3,2,1,0:T(8,128)S(1)}, u32[]{:S(2)}, u32[]{:S(2)}) collective-permute-start(f32[2,2,2,128,128]{4,3,2,1,0:T(8,128)S(1)} %get-tuple-element.105.refs_1_), channel_id=1, source_target_pairs={{0,2},{2,0},{4,6},{6,4},{8,10},{10,8},{12,14},{14,12},{1,3},{3,1},... | collective-permute-start | bytes 1572872 | tf_op jit(solution)/shard_map/ppermute | solution.py:490
  172.7 8.3 %collective-permute-start.28 = (f32[2,2,128,128]{3,2,1,0:T(8,128)S(1)}, f32[2,2,128,128]{3,2,1,0:T(8,128)S(1)}, u32[]{:S(2)}, u32[]{:S(2)}) collective-permute-start(f32[2,2,128,128]{3,2,1,0:T(8,128)S(1)} %get-tuple-element.110), channel_id=1, source_target_pairs={{4,0},{5,1},{6,2},{7,3},{20,16},{21,17},{22,18},{23,19}} | collective-permute-start | bytes 786440 | tf_op jit(solution)/shard_map/ppermute | solution.py:481
  174.0 16.8 %collective-permute-start.32 = (f32[2,2,2,128,128]{4,3,2,1,0:T(8,128)S(1)}, f32[2,2,2,128,128]{4,3,2,1,0:T(8,128)S(1)}, u32[]{:S(2)}, u32[]{:S(2)}) collective-permute-start(f32[2,2,2,128,128]{4,3,2,1,0:T(8,128)S(1)} %get-tuple-element.108.refs_1_), channel_id=1, source_target_pairs={{0,2},{2,0},{4,6},{6,4},{8,10},{10,8},{1,3},{3,1},{5,7},{7,5},{9,1... | collective-permute-start | bytes 1572872 | tf_op jit(solution)/shard_map/ppermute | solution.py:490
  176.0 22.4 %collective-permute-start.31 = (f32[2,2,2,128,128]{4,3,2,1,0:T(8,128)S(1)}, f32[2,2,2,128,128]{4,3,2,1,0:T(8,128)S(1)}, u32[]{:S(2)}, u32[]{:S(2)}) collective-permute-start(f32[2,2,2,128,128]{4,3,2,1,0:T(8,128)S(1)} %get-tuple-element.111.refs_1_), channel_id=1, source_target_pairs={{0,2},{2,0},{4,6},{6,4},{1,3},{3,1},{5,7},{7,5},{16,18},{18,16},{2... | collective-permute-start | bytes 1572872 | tf_op jit(solution)/shard_map/ppermute | solution.py:490
  183.5 20.5 %collective-permute-start.30 = (f32[2,2,2,128,128]{4,3,2,1,0:T(8,128)S(1)}, f32[2,2,2,128,128]{4,3,2,1,0:T(8,128)S(1)}, u32[]{:S(2)}, u32[]{:S(2)}) collective-permute-start(f32[2,2,2,128,128]{4,3,2,1,0:T(8,128)S(1)} %get-tuple-element.113.refs_1_), channel_id=1, source_target_pairs={{0,2},{2,0},{1,3},{3,1},{16,18},{18,16},{17,19},{19,17}} | collective-permute-start | bytes 1572872 | tf_op jit(solution)/shard_map/ppermute | solution.py:490
  206.2 4.6 %collective-permute-start.33 = (f32[2,2,192,768]{3,2,1,0:T(8,128)S(1)}, f32[2,2,192,768]{3,2,1,0:T(8,128)S(1)}, u32[]{:S(2)}, u32[]{:S(2)}) collective-permute-start(f32[2,2,192,768]{3,2,1,0:T(8,128)S(1)} %bitcast.9), channel_id=1, source_target_pairs={{0,1},{1,0},{2,3},{3,2},{4,5},{5,4},{6,7},{7,6},{8,9},{9,8},{10,11... | collective-permute-start | bytes 7077896 | tf_op jit(solution)/shard_map/ppermute | solution.py:445

commit v6 on v5

v6 whole, which is shorter than its diff:
```python
import functools
import math

import jax
import jax.numpy as jnp
import ml_dtypes
import numpy as np
from jax import lax
from jax.experimental import pallas as pl
from jax.experimental.pallas import tpu as pltpu
from jax.sharding import PartitionSpec as P

FRESNEL = 8.0
SCOPED = 8 << 20
CROSSING = 3
F32 = jnp.float32
BF16 = jnp.bfloat16
HBM = pl.BlockSpec(memory_space=pl.ANY)
VMEM = pl.BlockSpec(memory_space=pltpu.VMEM)
SMEM = pl.BlockSpec(memory_space=pltpu.SMEM)


def in_hbm(x):
    return pltpu.with_memory_space_constraint(x, pltpu.HBM)


def in_vmem(x):
    return pltpu.with_memory_space_constraint(x, pltpu.VMEM)


def real_blocks(matrix):
    real, imag = matrix.real, matrix.imag
    left = np.block([[real, -imag], [imag, real]])
    right = np.block([[real, imag], [-imag, real]])
    return np.stack([left, right])


@functools.lru_cache(maxsize=None)
def make_tables(pixels):
    index = np.arange(pixels)
    freq = np.where(index < pixels // 2, index, index - pixels) / pixels
    spread = index[:, None] - index[None, :]
    phase = 2.0 * math.pi * freq * spread[:, :, None] - math.pi * FRESNEL * freq * freq
    propagator = np.mean(np.exp(1j * phase), axis=-1)
    turns = index[:, None] * index[None, :] % pixels
    fourier = np.exp(-2j * math.pi * turns / pixels) / math.sqrt(pixels)
    blocks = np.stack([real_blocks(propagator), real_blocks(fourier)]).astype(np.float32)
    high = blocks.astype(ml_dtypes.bfloat16)
    low = (blocks - high.astype(np.float32)).astype(ml_dtypes.bfloat16)
    return np.stack([high, low], axis=2)


def halves(x):
    high = x.astype(BF16)
    return high, (x - high.astype(F32)).astype(BF16)


def dot(a, b):
    return jnp.dot(a, b, preferred_element_type=F32)


def transform(left, right, fields):
    size = fields[0][0].shape[0]
    stacked = jnp.concatenate(
        [
            jnp.concatenate([real for real, _ in fields], axis=1),
            jnp.concatenate([imag for _, imag in fields], axis=1),
        ],
        axis=0,
    )
    high, low = halves(stacked)
    mid = dot(left[0], high) + (dot(left[1], high) + dot(left[0], low))
    rows = jnp.concatenate(
        [
            jnp.concatenate(
                [mid[:size, i * size : (i + 1) * size], mid[size:, i * size : (i + 1) * size]], axis=1
            )
            for i in range(len(fields))
        ],
        axis=0,
    )
    high, low = halves(rows)
    out = dot(high, right[0]) + (dot(high, right[1]) + dot(low, right[0]))
    return [
        (out[i * size : (i + 1) * size, :size], out[i * size : (i + 1) * size, size:])
        for i in range(len(fields))
    ]


def times(a, b):
    return a[0] * b[0] - a[1] * b[1], a[0] * b[1] + a[1] * b[0]


def times_conj(a, b):
    return a[0] * b[0] + a[1] * b[1], a[1] * b[0] - a[0] * b[1]


class Layout:
    def __init__(self, probes, count, layers, pixels, rows, height, width, only_sums=False):
        self.probes, self.count, self.layers, self.pixels = probes, count, layers, pixels
        self.groups = probes // count
        self.tall = pixels + 8
        self.rows, self.height, self.width = rows, height, width
        self.blocks = width // pixels
        self.deep = rows + 2 * self.tall
        self.column_bits = (width - 1).bit_length()
        self.name_bits = (4 * probes - 1).bit_length()
        self.stack = probes * layers * 2 * pixels
        self.seen_from = self.stack
        self.grads_from = 2 * self.stack
        self.frames_from = 3 * self.stack
        self.total_from = 0 if only_sums else self.frames_from + probes * pixels
        self.shape = (self.total_from + 2 * layers * self.blocks * self.deep, pixels)

    def stacked(self, group, i, layer, part):
        probe = group * self.count + i
        return ((probe * self.layers + layer) * 2 + part) * self.pixels

    def tile(self, start):
        return pl.ds(pl.multiple_of(start, 8), self.pixels)

    def patch(self, group, i, layer, part):
        return self.tile(self.stacked(group, i, layer, part))

    def seen(self, group, i, layer, part):
        return self.tile(self.seen_from + self.stacked(group, i, layer, part))

    def grad(self, group, i, layer, part):
        return self.tile(self.grads_from + self.stacked(group, i, layer, part))

    def grads_of(self, begin, end):
        each = self.stack // self.groups
        return self.grads_from + begin * each, self.grads_from + end * each

    def frame(self, group, i):
        return self.tile(self.frames_from + (group * self.count + i) * self.pixels)

    def total(self, part, layer, block, row):
        block = (part * self.layers + layer) * self.blocks + block
        return self.total_from + block * self.deep + row

    def pack(self, row, column, name):
        return (((row << self.column_bits) + column) << self.name_bits) + name

    def row(self, key):
        return key >> (self.column_bits + self.name_bits)

    def window(self, info, probe, partner=False):
        key = info[0, probe + partner * self.probes]
        row = self.row(key)
        column = (key >> self.name_bits) & ((1 << self.column_bits) - 1)
        row0 = jnp.minimum(row // 8 * 8, self.height - self.tall)
        block = jnp.minimum(column // self.pixels, self.blocks - 2)
        return row0, row - row0, block, column - block * self.pixels


def call(lay, body, state, before, outs, scratch=(), grid=(), flops=0, moved=0, name=None):
    spaces = {"hbm": (HBM, in_hbm), "vmem": (VMEM, in_vmem), "smem": (SMEM, lambda x: x)}
    specs = [spaces[kind][0] for kind, _ in before]
    operands = [spaces[kind][1](x) for kind, x in before]
    at = len(before)
    aliases = {}
    if state is not None:
        specs.append(VMEM)
        operands.append(in_vmem(state))
        aliases = {at: 0}

    def kernel(*refs):
        body(*refs[:at], *refs[at + len(aliases) :])

    return pl.pallas_call(
        kernel,
        grid=grid,
        in_specs=specs,
        out_specs=[VMEM] * (1 + len(outs)),
        out_shape=[pltpu.VMEM(shape, F32) for shape in (lay.shape, *outs)],
        scratch_shapes=list(scratch),
        input_output_aliases=aliases,
        compiler_params=pltpu.CompilerParams(vmem_limit_bytes=SCOPED),
        cost_estimate=pl.CostEstimate(flops=flops, bytes_accessed=moved, transcendentals=0),
        name=name,
    )(*operands)


def clear_total(lay, state):
    start = lay.total_from

    def body(state):
        state[pl.ds(start, lay.shape[0] - start), :] = jnp.zeros((lay.shape[0] - start, lay.pixels), F32)

    return call(lay, body, state, [], [], name="clear_total")[0]


def place_frames(lay, info, pools, state):
    def body(info, *refs):
        *pools, state, sems = refs
        lat, side = lax.axis_index("lat"), lax.axis_index("probe")
        for act in ("start", "wait"):
            for probe in range(lay.probes):
                name = info[0, probe] & ((1 << lay.name_bits) - 1)
                owner = name // lay.probes
                slot = name % lay.probes
                if len(pools) > 1:
                    slot += ((owner // 2) ^ side) * lay.probes + ((owner % 2) ^ lat) * 2 * lay.probes
                first = 0
                for pool in pools:
                    size = pool.shape[0] // lay.pixels

                    @pl.when((slot >= first) & (slot < first + size))
                    def _(pool=pool, first=first, probe=probe, slot=slot):
                        copy = pltpu.make_async_copy(
                            pool.at[lay.tile((slot - first) * lay.pixels), :],
                            state.at[lay.frame(0, probe), :],
                            sems.at[probe],
                        )
                        getattr(copy, act)()

                    first += size

    pools = [("hbm", pool.reshape((-1, lay.pixels))) for pool in pools]
    return call(
        lay,
        body,
        state,
        [("smem", info), *pools],
        [],
        scratch=[pltpu.SemaphoreType.DMA((lay.probes,))],
        moved=lay.probes * lay.pixels**2 * 8,
        name="place_frames",
    )[0]


def cut_patches(lay, info, own, other, state, begin, end):
    half = own.shape[2]
    tall, pixels = lay.tall, lay.pixels

    def body(info, own, other, state, window):
        probe = begin + pl.program_id(0)
        row0, down, block, shift = lay.window(info, probe)
        own_top = lax.axis_index("lat") == 0
        near_at = pl.ds(pl.multiple_of(block * pixels, pixels), pixels)
        far_at = pl.ds(pl.multiple_of((block + 1) * pixels, pixels), pixels)
        for source, is_top in ((own, own_top), (other, jnp.logical_not(own_top))):
            start = jnp.clip(row0 - jnp.where(is_top, 0, half), 0, half - tall)
            to = pl.ds(pl.multiple_of(jnp.where(is_top, 0, tall), 8), tall)
            rows = pl.ds(pl.multiple_of(start, 8), tall)

            @pl.when(jnp.where(is_top, row0 < half, row0 + tall > half))
            def _(source=source, rows=rows, to=to):
                for part in range(2):
                    for layer in range(lay.layers):
                        window[part, layer, to, 0:pixels] = source[part, layer, rows, near_at]
                        window[part, layer, to, pixels : 2 * pixels] = source[part, layer, rows, far_at]

        offset = jnp.where(row0 < half, jnp.maximum(row0 - (half - tall), 0), tall)
        rows = pl.ds(pl.multiple_of(offset, 8), tall)
        turn = (pixels - shift) % pixels
        lane = lax.broadcasted_iota(jnp.int32, (tall, pixels), 1)
        for part in range(2):
            for layer in range(lay.layers):
                near = pltpu.roll(window[part, layer, rows, 0:pixels], turn, 1)
                far = pltpu.roll(window[part, layer, rows, pixels : 2 * pixels], turn, 1)
                patch = jnp.where(lane < pixels - shift, near, far)
                patch = pltpu.roll(patch, (tall - down) % tall, 0)[:pixels]
                state[lay.patch(0, probe, layer, part), :] = patch

    size = (end - begin) * lay.layers * 2 * pixels * pixels
    return call(
        lay,
        body,
        state,
        [("smem", info), ("vmem", own), ("vmem", other)],
        [],
        scratch=[pltpu.VMEM((2, lay.layers, 2 * tall, 2 * pixels), F32)],
        grid=(end - begin,),
        flops=size * 4,
        moved=size * 12,
        name="cut_patches",
    )[0]


def section_cost(lay):
    size = lay.count * lay.pixels**2
    return dict(flops=lay.layers * 2 * 3 * 8 * size * lay.pixels, moved=(lay.layers * 2 + 4) * 8 * size)


def pair(ref, at):
    return ref[at(0), :], ref[at(1), :]


def run_forward(lay, tick, sections, tables, state, arrived, start_wave):
    def body(tables, *refs):
        arrived_ref = refs[0] if arrived is not None else None
        start_ref = refs[-3] if start_wave is not None else None
        state, leave = refs[-2:]
        section = lax.axis_index("depth")
        group = tick - section
        final = (section == sections - 1).astype(jnp.int32)

        @pl.when((group >= 0) & (group < lay.groups))
        def _():
            wave = []
            for i in range(lay.count):
                if arrived is None:
                    wave.append((start_ref[0], start_ref[1]))
                elif start_wave is None:
                    wave.append((arrived_ref[i, 0], arrived_ref[i, 1]))
                else:
                    wave.append(
                        tuple(jnp.where(section == 0, start_ref[p], arrived_ref[i, p]) for p in range(2))
                    )
            for layer in range(lay.layers):
                chi = []
                for i in range(lay.count):
                    for part in range(2):
                        state[lay.seen(group, i, layer, part), :] = wave[i][part]
                    chi.append(times(pair(state, functools.partial(lay.patch, group, i, layer)), wave[i]))
                at = final if layer == lay.layers - 1 else 0
                wave = transform((tables[at, 0, 0], tables[at, 0, 1]), (tables[at, 1, 0], tables[at, 1, 1]), chi)
            for i in range(lay.count):
                real, imag = wave[i]
                misfit = real * real + imag * imag - state[lay.frame(group, i), :]
                factor = jnp.where(final == 1, misfit, 1.0)
                leave[i, 0] = real * factor
                leave[i, 1] = imag * factor

    waves = [("vmem", x) for x in (arrived, start_wave) if x is not None]
    return call(
        lay,
        body,
        state,
        [("vmem", tables), *waves],
        [(lay.count, 2, lay.pixels, lay.pixels)],
        name="forward_section",
        **section_cost(lay),
    )


def run_backward(lay, tick, sections, tables, state, arrived, own):
    def body(tables, *refs):
        arrived_ref = refs[0] if arrived is not None else None
        own_ref = refs[-3] if own is not None else None
        state, leave = refs[-2:]
        section = lax.axis_index("depth")
        group = tick - (2 * (sections - 1) - section)
        final = (section == sections - 1).astype(jnp.int32)

        @pl.when((group >= 0) & (group < lay.groups))
        def _():
            wave = []
            for i in range(lay.count):
                if arrived is None:
                    wave.append((own_ref[i, 0], own_ref[i, 1]))
                elif own is None:
                    wave.append((arrived_ref[i, 0], arrived_ref[i, 1]))
                else:
                    wave.append(
                        tuple(jnp.where(final == 1, own_ref[i, p], arrived_ref[i, p]) for p in range(2))
                    )
            for layer in reversed(range(lay.layers)):
                at = final if layer == lay.layers - 1 else 0
                chi = transform((tables[at, 1, 0], tables[at, 1, 1]), (tables[at, 0, 0], tables[at, 0, 1]), wave)
                wave = []
                for i in range(lay.count):
                    real, imag = times_conj(chi[i], pair(state, functools.partial(lay.seen, group, i, layer)))
                    state[lay.grad(group, i, layer, 0), :] = real
                    state[lay.grad(group, i, layer, 1), :] = imag
                    wave.append(times_conj(chi[i], pair(state, functools.partial(lay.patch, group, i, layer))))
            for i in range(lay.count):
                leave[i, 0] = wave[i][0]
                leave[i, 1] = wave[i][1]

    waves = [("vmem", x) for x in (arrived, own) if x is not None]
    return call(
        lay,
        body,
        state,
        [("vmem", tables), *waves],
        [(lay.count, 2, lay.pixels, lay.pixels)],
        name="backward_section",
        **section_cost(lay),
    )


def deposit(lay, tick, sections, info, received, state):
    pixels, tall = lay.pixels, lay.tall

    def body(info, *refs):
        state = refs[-1]
        lane = lax.broadcasted_iota(jnp.int32, (tall, pixels), 1)
        blank = jnp.zeros((8, pixels), F32)
        base = lax.axis_index("probe") * lay.rows if lay.rows < lay.height else 0

        def add(probe, partner, active, load):
            row0, down, block, shift = lay.window(info, probe, partner)
            start = row0 - base + tall

            @pl.when(active & (start > 0) & (start < lay.rows + tall))
            def _():
                for layer in range(lay.layers):
                    for part in range(2):
                        padded = jnp.concatenate([load(layer, part), blank], axis=0)
                        turned = pltpu.roll(pltpu.roll(padded, down, 0), shift % pixels, 1)
                        near = pl.ds(pl.multiple_of(lay.total(part, layer, block, start), 8), tall)
                        far = pl.ds(pl.multiple_of(lay.total(part, layer, block + 1, start), 8), tall)
                        state[near, :] += jnp.where(lane >= shift, turned, 0.0)
                        state[far, :] += jnp.where(lane >= shift, 0.0, turned)

        if tick is not None:
            group = tick - (2 * (sections - 1) - lax.axis_index("depth"))
            active = (group >= 0) & (group < lay.groups)
            group = jnp.clip(group, 0, lay.groups - 1)
            for i in range(lay.count):
                add(
                    group * lay.count + i,
                    False,
                    active,
                    lambda layer, part, i=i: state[lay.grad(group, i, layer, part), :],
                )
        for ref, (first, grads) in zip(refs, received):

            def one(i, _, ref=ref, first=first):
                add(
                    first * lay.count + i,
                    True,
                    True,
                    lambda layer, part: ref[lay.patch(0, i, layer, part), :],
                )
                return 0

            lax.fori_loop(0, grads.shape[0] // (lay.layers * 2 * pixels), one, 0)

    size = lay.count * lay.layers * 2 * pixels**2 + sum(grads.size for _, grads in received)
    return call(
        lay,
        body,
        state,
        [("smem", info)] + [("vmem", grads) for _, grads in received],
        [],
        flops=size * 8,
        moved=size * 12,
        name="deposit_patches",
    )[0]


def split_rows(lay, state, owners):
    rows = lay.rows // (2 * owners)

    def body(state, keep, send, sems):
        lat = lax.axis_index("lat")
        copies = []
        for owner in range(owners):
            for kind, target in ((lat, keep), (1 - lat, send)):
                for part in range(2):
                    for layer in range(lay.layers):
                        for block in range(lay.blocks):
                            start = lay.total(part, layer, block, lay.tall + (2 * owner + kind) * rows)
                            copies.append(
                                pltpu.make_async_copy(
                                    state.at[pl.ds(pl.multiple_of(start, 8), rows), :],
                                    target.at[part, layer, owner, :, pl.ds(block * lay.pixels, lay.pixels)],
                                    sems.at[len(copies)],
                                )
                            )
        for copy in copies:
            copy.start()
        for copy in copies:
            copy.wait()

    half = (2, lay.layers, owners, rows, lay.width)
    return pl.pallas_call(
        body,
        in_specs=[VMEM],
        out_specs=[VMEM, VMEM],
        out_shape=[pltpu.VMEM(half, F32), pltpu.VMEM(half, F32)],
        scratch_shapes=[pltpu.SemaphoreType.DMA((4 * owners * lay.layers * lay.blocks,))],
        compiler_params=pltpu.CompilerParams(vmem_limit_bytes=SCOPED),
        name="split_rows",
    )(in_vmem(state))


def swap(shard, axis):
    return lax.ppermute(shard, axis, [(0, 1), (1, 0)])


def sort_probes(lay, early, positions, indices, specimen):
    n = lay.probes
    total = 4 * n

    def body(positions, *refs):
        *scans, specimen, info, brought, sem = refs
        copy = pltpu.make_async_copy(specimen, brought, sem)
        copy.start()
        lat, side = lax.axis_index("lat"), lax.axis_index("probe")
        lane = lax.broadcasted_iota(jnp.int32, (1, 128), 1)
        at = lax.broadcasted_iota(jnp.int32, (total, 128), 0)
        across = jnp.full((1, 128), jnp.iinfo(jnp.int32).max, jnp.int32)
        down = jnp.zeros((total, 128), jnp.int32)
        for which, scan in enumerate(scans):
            owner = (side ^ (which % 2)) * 2 + (lat ^ (which // 2))
            for i in range(n):
                place = scan[i]
                key = lay.pack(positions[0, place], positions[1, place], owner * n + i)
                across = jnp.where(lane == which * n + i, key, across)
                down = jnp.where(at == which * n + i, key, down)
        rank = jnp.sum((across < down).astype(jnp.int32), axis=1, keepdims=True)
        partner = lane // n
        order = 2 * (lane % n) + lat
        wanted = jnp.where((side ^ partner) == 0, 2 * n - 1 - order, 2 * n + order)
        reach = 2 * early * lay.count
        wanted = jnp.where(lane == 2 * n, 2 * n - 1 - reach, wanted)
        wanted = jnp.where(lane == 2 * n + 1, 2 * n + reach, wanted)
        wanted = jnp.where(lane > 2 * n + 1, -1, wanted)
        info[...] = jnp.sum(jnp.where(rank == wanted, down, 0), axis=0, keepdims=True)
        copy.wait()

    return pl.pallas_call(
        body,
        in_specs=[SMEM] * 5 + [HBM],
        out_specs=[VMEM, VMEM],
        out_shape=[jax.ShapeDtypeStruct((1, 128), jnp.int32), pltpu.VMEM(specimen.shape, F32)],
        scratch_shapes=[pltpu.SemaphoreType.DMA(())],
        compiler_params=pltpu.CompilerParams(vmem_limit_bytes=SCOPED),
        name="sort_probes",
    )(positions.T, *indices, in_hbm(specimen))


def local(specimen, illumination, positions, scan_index, frames):
    pixels = illumination.shape[-1]
    _, layers, half, width = specimen.shape
    height = 2 * half
    tables = jnp.asarray(make_tables(pixels))
    sections = lax.axis_size("depth")
    owners = lax.axis_size("probe")
    paired = owners == 2 and lax.axis_size("groups") <= 2
    probes = scan_index.size
    count = 2 if probes % 4 == 0 else 1
    lay = Layout(probes, count, layers, pixels, half if paired else height, height, width)
    early = lay.groups // 2

    other = swap(specimen, "lat")
    if paired:
        scan = scan_index.reshape(-1)
        others = [scan, swap(scan, "probe"), swap(scan, "lat")]
        others.append(lax.ppermute(scan, ("probe", "lat"), [(i, 3 - i) for i in range(4)]))
        info, specimen = sort_probes(lay, early, positions, others, specimen)
        measured, _ = lax.optimization_barrier((frames, info))
        end = sections - 1
        ends = [(2 * end, 2 * end + 1), (2 * end + 1, 2 * end)]
        mine = lax.ppermute(measured, ("depth", "probe"), ends)
        crossed = lax.ppermute(jnp.concatenate([frames, mine]), ("depth", "lat"), ends)
        pools = [frames, mine, crossed]
        everyone = swap(info, "groups") if lax.axis_size("groups") == 2 else info
    else:
        corners = positions[scan_index.reshape(-1)]
        info = lay.pack(corners[:, 0], corners[:, 1], jnp.arange(probes, dtype=jnp.int32))
        info = jnp.pad(info, (0, -probes % 128))[None]
        pools = [frames]
    state = cut_patches(lay, info, specimen, other, None, 0, count)

    def busy(tick, source, by):
        delay = source if by > 0 else 2 * (sections - 1) - source
        return 0 <= tick - delay < lay.groups

    def pass_on(wave, tick, by):
        pairs = [
            (source, source + by)
            for source in range(sections)
            if 0 <= source + by < sections and busy(tick, source, by)
        ]
        return lax.ppermute(wave, "depth", pairs) if pairs else None

    def grads_of(state, begin, end):
        begin, end = lay.grads_of(begin, end)
        return lax.slice_in_dim(state, begin, end)

    fill = sections - 1
    portion = -(-(lay.groups - 1) // fill) * count
    parts = [(0, early // 2), (early // 2, early)] if paired else []
    crossing = {}
    down = up = None
    cut = count
    for tick in range(lay.groups + 2 * fill):
        own = None
        if tick < lay.groups + fill:
            start_wave = illumination if tick < lay.groups else None
            state, own = run_forward(lay, tick, sections, tables, state, down, start_wave)
            down = pass_on(own, tick, 1)
            if cut < probes:
                state = cut_patches(lay, info, specimen, other, state, cut, min(cut + portion, probes))
                cut += portion
            if tick == 0:
                state = clear_total(lay, state)
            if tick == fill - 1:
                if paired:
                    state, everyone = lax.optimization_barrier((state, everyone))
                state = place_frames(lay, info, pools, state)
        if tick >= fill:
            state, rising = run_backward(lay, tick, sections, tables, state, up, own)
            up = pass_on(rising, tick, -1)
            received = crossing.pop(tick, [])
            for begin, end in parts:
                if tick == end - 1 + 2 * fill:
                    due = min(tick + CROSSING, lay.groups + 2 * fill - 1)
                    crossing.setdefault(due, []).append((begin, swap(grads_of(state, begin, end), "probe")))
            state = deposit(lay, tick, sections, info, received, state)
    if not paired:
        keep, send = split_rows(lay, state, owners)
        return lax.psum_scatter(keep + swap(send, "lat"), "probe", scatter_dimension=2, tiled=False)

    keep, send = split_rows(lay, state, 1)
    late_grads = grads_of(state, early, lay.groups)

    def reaches(info):
        nearest = lay.row(info[0, 2 * probes : 2 * probes + 2])
        return (nearest[0] + pixels > half) | (nearest[1] < half)

    def as_they_are(keep, received, grads):
        return keep + received

    def with_partners(keep, received, grads):
        sums = Layout(probes, count, layers, pixels, half, height, width, only_sums=True)
        state = clear_total(sums, None)
        state = deposit(sums, None, sections, info, [(early, swap(grads, "probe"))], state)
        more, send = split_rows(sums, state, 1)
        return (keep + received) + (more + swap(send, "lat"))

    late = reaches(info) | reaches(everyone)
    result = lax.cond(late, with_partners, as_they_are, keep, swap(send, "lat"), late_grads)
    return result[:, :, 0]


def solution(mesh):
    return jax.shard_map(
        local,
        mesh=mesh,
        in_specs=(
            P(None, ("groups", "depth"), "lat", None),
            P(),
            P("groups", None),
            P("groups", ("probe", "lat")),
            P("groups", ("probe", "lat"), None, None),
        ),
        out_specs=P(None, ("groups", "depth"), ("probe", "lat"), None),
        check_vma=False,
    )
```

time: 214 us -> 182 us (0.85)
  waiting for transfers between devices: 69.8 us -> 51.5 us
  Pallas kernels: 62.6 us -> 49.7 us
  local copies, waits for them, and re-layouts: 13.6 us -> 3.99 us
  starting transfers between devices: 63.6 us -> 69.3 us
  between operations: 0.67 us -> 3.25 us
    ppermute x11 -> x3, waiting for transfers between devices: 20.1 us -> 0.01 us  [the longest x1 0.01 us: local(): lax.ppermute(scan, ('probe', 'lat'), [(i, 3 - i) for i in range(4)])]
    ppermute x20, starting transfers between devices: 46 us -> 60.8 us  [pass_on(): return lax.ppermute(wave, 'depth', pairs) if pairs else None]
    ppermute x11 -> x3, starting transfers between devices: 14.5 us -> 1.56 us  [the longest x1 0.8 us: local(): lax.ppermute(jnp.concatenate([frames, mine]), ('depth', 'lat'), ends)]
    pallas_call x39 -> x41, Pallas kernels: 62.6 us -> 49.7 us  [the longest x39 45.6 us: call(): pl.pallas_call(kernel, grid=grid, in_specs=specs, out_specs=[VMEM] * (1 +...]
    unnamed x9 -> x16, local copies, waits for them, and re-layouts: 12.8 us -> 2.68 us
    ppermute x3 -> x7, starting transfers between devices: 3.08 us -> 6.98 us  [swap(): return lax.ppermute(shard, axis, [(0, 1), (1, 0)])]
    ppermute x3 -> x7, waiting for transfers between devices: 4.53 us -> 6.48 us  [swap(): return lax.ppermute(shard, axis, [(0, 1), (1, 0)])]
  transfers between devices with their start and end apart: 34 -> 30, of which waited for: 17 -> 15; matrix products, arithmetic and copies ran while one was open for 1% -> 2% of each run, Pallas kernels for 23% -> 24%
where the time goes in v6:
time: 182 us; the launch traced here: 181 us
  starting transfers between devices  69.3 us (38%)
  waiting for transfers between devices  51.5 us (28%)
  Pallas kernels  49.7 us (27%)
  local copies, waits for them, and re-layouts  3.99 us (2%)
  other arithmetic  3.6 us (2%)
  between operations  3.25 us (2%)
    ppermute x20, starting transfers between devices, pass_on(): return lax.ppermute(wave, 'depth', pairs) if pairs else None  60.8 us
    pallas_call x39, Pallas kernels, call(): pl.pallas_call(kernel, grid=grid, in_specs=specs, out_specs=[VMEM] * (1 +...  45.6 us
    ppermute x20, waiting for transfers between devices, pass_on(): return lax.ppermute(wave, 'depth', pairs) if pairs else None  45 us
    ppermute x7, starting transfers between devices, swap(): return lax.ppermute(shard, axis, [(0, 1), (1, 0)])  6.98 us
    ppermute x7, waiting for transfers between devices, swap(): return lax.ppermute(shard, axis, [(0, 1), (1, 0)])  6.48 us
  transfers between devices with their start and end apart: 30, of which 15 were waited for; matrix products, arithmetic and copies ran while one was open for 2% of the time, Pallas kernels for 24%

profile of v6, /device:TPU:0, one launch (start us, length us, event | category | flops | bytes accessed | tf_op | source)
XLA Modules:
  0.0 181.4 jit_solution(15338391768656936980)
XLA Ops:
  0.5 2.6 %collective-permute-start.2 = (s32[16]{0:T(128)}, s32[16]{0:T(128)S(1)}, u32[]{:S(2)}, u32[]{:S(2)}) collective-permute-start(s32[16]{0:T(128)} %bitcast.25), channel_id=1, source_target_pairs={{0,2},{2,0},{1,3},{3,1},{4,6},{6,4},{5,7},{7,5},{8,10},{10,8},{9,1... | collective-permute-start | bytes 200 | tf_op jit(solution)/shard_map/ppermute | solution.py:483
  3.2 1.5 collective-permute-done.2.refs_1_
  4.7 3.5 %collective-permute-done.3.refs_2_ = s32[16]{0:T(128)S(1)} collective-permute-done((s32[16]{0:T(128)}, s32[16]{0:T(128)S(1)}, u32[]{:S(2)}, u32[]{:S(2)}) %collective-permute-start.3) | collective-permute-done | bytes 96 | tf_op jit(solution)/shard_map/ppermute | solution.py:483
  9.6 3.2 %sort_probes.1 = (s32[1,128]{1,0:T(1,128)S(1)}, f32[2,2,384,768]{3,2,1,0:T(8,128)S(1)}) custom-call(s32[2,512]{1,0:T(2,128)S(1)} %bitcast.24, s32[16]{0:T(128)S(1)} %bitcast.28, s32[16]{0:T(128)S(1)} %collective-permute-done.2.refs_1_, s32[16]{0:T(128)S(1)} %collective-permute-done.3.refs_2_, s32[16]{0:T(128)S(1)} %collective-permute-done.4.refs_3_, ...), custom_call_target="tpu_custom_call" | custom-call | tf_op jit(solution)/shard_map/sort_probes/pallas_call | solution.py:517
  13.6 1.7 pad_maximum_fusion
  17.4 1.3 forward_section.11
  18.7 3.6 %collective-permute-start.6 = (f32[2,2,128,128]{3,2,1,0:T(8,128)S(1)}, f32[2,2,128,128]{3,2,1,0:T(8,128)S(1)}, u32[]{:S(2)}, u32[]{:S(2)}) collective-permute-start(f32[2,2,128,128]{3,2,1,0:T(8,128)S(1)} %get-tuple-element.81), channel_id=1, source_target_pairs={{0,4},{1,5},{2,6},{3,7},{16,20},{17,21},{18,22},{19,23}} | collective-permute-start | bytes 786440 | tf_op jit(solution)/shard_map/ppermute | solution.py:571
  22.3 2.4 %cut_patches.5.refs_0_ = f32[42368,128]{1,0:T(8,128)S(1)} custom-call(s32[1,128]{1,0:T(1,128)S(1)} %get-tuple-element.150.refs_0_, f32[2,2,384,768]{3,2,1,0:T(8,128)S(1)} %get-tuple-element.80.refs_1_, f32[2,2,384,768]{3,2,1,0:T(8,128)S(1)} %collective-permute-done.5.refs_2_, f32[42368,128]{1,0:T(8,128)S(1)} %get-tuple-element.82.refs_3_), custom_call_target="tpu_custom_call", output_to_operand_aliasing={{}: (3, {})} | custom-call | flops 1572864 | bytes 4718592 | tf_op jit(solution)/shard_map/cut_patches/pallas_call | solution.py:171
  25.3 2.9 %collective-permute-done.6.refs_1_ = f32[2,2,128,128]{3,2,1,0:T(8,128)S(1)} collective-permute-done((f32[2,2,128,128]{3,2,1,0:T(8,128)S(1)}, f32[2,2,128,128]{3,2,1,0:T(8,128)S(1)}, u32[]{:S(2)}, u32[]{:S(2)}) %collective-permute-start.6) | collective-permute-done | bytes 262176 | tf_op jit(solution)/shard_map/ppermute | solution.py:571
  28.1 1.3 forward_section.12
  29.5 4.4 %collective-permute-start.7 = (f32[2,2,128,128]{3,2,1,0:T(8,128)S(1)}, f32[2,2,128,128]{3,2,1,0:T(8,128)S(1)}, u32[]{:S(2)}, u32[]{:S(2)}) collective-permute-start(f32[2,2,128,128]{3,2,1,0:T(8,128)S(1)} %get-tuple-element.83), channel_id=1, source_target_pairs={{0,4},{4,8},{1,5},{5,9},{2,6},{6,10},{3,7},{7,11},{16,20},{20,24},... | collective-permute-start | bytes 786440 | tf_op jit(solution)/shard_map/ppermute | solution.py:571
  33.9 2.4 %cut_patches.6.refs_3_ = f32[42368,128]{1,0:T(8,128)S(1)} custom-call(s32[1,128]{1,0:T(1,128)S(1)} %get-tuple-element.150.refs_0_, f32[2,2,384,768]{3,2,1,0:T(8,128)S(1)} %get-tuple-element.80.refs_1_, f32[2,2,384,768]{3,2,1,0:T(8,128)S(1)} %collective-permute-done.5.refs_2_, f32[42368,128]{1,0:T(8,128)S(1)} %get-tuple-element.84.refs_3_), custom_call_target="tpu_custom_call", output_to_operand_aliasing={{}: (3, {})} | custom-call | flops 1572864 | bytes 4718592 | tf_op jit(solution)/shard_map/cut_patches/pallas_call | solution.py:171
  36.3 2.6 %collective-permute-done.7.refs_1_ = f32[2,2,128,128]{3,2,1,0:T(8,128)S(1)} collective-permute-done((f32[2,2,128,128]{3,2,1,0:T(8,128)S(1)}, f32[2,2,128,128]{3,2,1,0:T(8,128)S(1)}, u32[]{:S(2)}, u32[]{:S(2)}) %collective-permute-start.7) | collective-permute-done | bytes 262176 | tf_op jit(solution)/shard_map/ppermute | solution.py:571
  38.9 1.3 forward_section.13
  40.2 4.4 %collective-permute-start.9 = (f32[2,2,128,128]{3,2,1,0:T(8,128)S(1)}, f32[2,2,128,128]{3,2,1,0:T(8,128)S(1)}, u32[]{:S(2)}, u32[]{:S(2)}) collective-permute-start(f32[2,2,128,128]{3,2,1,0:T(8,128)S(1)} %get-tuple-element.87), channel_id=1, source_target_pairs={{0,4},{4,8},{8,12},{1,5},{5,9},{9,13},{2,6},{6,10},{10,14},{3,7},{... | collective-permute-start | bytes 786440 | tf_op jit(solution)/shard_map/ppermute | solution.py:571
  44.6 1.6 collective-permute-start.8
  49.6 2.0 %place_frames.1.refs_3_ = f32[42368,128]{1,0:T(8,128)S(1)} custom-call(s32[1,128]{1,0:T(1,128)S(1)} %get-tuple-element.150.refs_0_, f32[2048,128]{1,0:T(8,128)} %bitcast.29, f32[2048,128]{1,0:T(8,128)} %bitcast.30, f32[4096,128]{1,0:T(8,128)} %bitcast.31, f32[42368,128]{1,0:T(8,128)S(1)} %cut_patches.7.refs_4_), custom_call_target="tpu_custom_call", output_to_operand_aliasing={{}: (4, {})} | custom-call | bytes 2097152 | tf_op jit(solution)/shard_map/place_frames/pallas_call | solution.py:171
  51.6 1.3 forward_section.14
  52.9 2.2 %collective-permute-start.13 = (f32[2,2,128,128]{3,2,1,0:T(8,128)S(1)}, f32[2,2,128,128]{3,2,1,0:T(8,128)S(1)}, u32[]{:S(2)}, u32[]{:S(2)}) collective-permute-start(f32[2,2,128,128]{3,2,1,0:T(8,128)S(1)} %get-tuple-element.90.refs_1_), channel_id=1, source_target_pairs={{0,4},{4,8},{8,12},{1,5},{5,9},{9,13},{2,6},{6,10},{10,14},{3,7},{... | collective-permute-start | bytes 786440 | tf_op jit(solution)/shard_map/ppermute | solution.py:571
  56.4 2.5 %collective-permute-done.13.refs_1_ = f32[2,2,128,128]{3,2,1,0:T(8,128)S(1)} collective-permute-done((f32[2,2,128,128]{3,2,1,0:T(8,128)S(1)}, f32[2,2,128,128]{3,2,1,0:T(8,128)S(1)}, u32[]{:S(2)}, u32[]{:S(2)}) %collective-permute-start.13) | collective-permute-done | bytes 262176 | tf_op jit(solution)/shard_map/ppermute | solution.py:571
  59.0 1.3 forward_section.15
  60.3 18.0 %collective-permute-start.15 = (f32[2,2,128,128]{3,2,1,0:T(8,128)S(1)}, f32[2,2,128,128]{3,2,1,0:T(8,128)S(1)}, u32[]{:S(2)}, u32[]{:S(2)}) collective-permute-start(f32[2,2,128,128]{3,2,1,0:T(8,128)S(1)} %get-tuple-element.94.refs_2_), channel_id=1, source_target_pairs={{0,4},{4,8},{8,12},{1,5},{5,9},{9,13},{2,6},{6,10},{10,14},{3,7},{... | collective-permute-start | bytes 786440 | tf_op jit(solution)/shard_map/ppermute | solution.py:571
  79.6 2.6 %collective-permute-done.15.refs_1_ = f32[2,2,128,128]{3,2,1,0:T(8,128)S(1)} collective-permute-done((f32[2,2,128,128]{3,2,1,0:T(8,128)S(1)}, f32[2,2,128,128]{3,2,1,0:T(8,128)S(1)}, u32[]{:S(2)}, u32[]{:S(2)}) %collective-permute-start.15) | collective-permute-done | bytes 262176 | tf_op jit(solution)/shard_map/ppermute | solution.py:571
  82.2 1.3 forward_section.16
  83.6 4.8 %collective-permute-start.17 = (f32[2,2,128,128]{3,2,1,0:T(8,128)S(1)}, f32[2,2,128,128]{3,2,1,0:T(8,128)S(1)}, u32[]{:S(2)}, u32[]{:S(2)}) collective-permute-start(f32[2,2,128,128]{3,2,1,0:T(8,128)S(1)} %get-tuple-element.98.refs_2_), channel_id=1, source_target_pairs={{0,4},{4,8},{8,12},{1,5},{5,9},{9,13},{2,6},{6,10},{10,14},{3,7},{... | collective-permute-start | bytes 786440 | tf_op jit(solution)/shard_map/ppermute | solution.py:571
  90.5 1.7 collective-permute-done.17.refs_1_
  92.3 1.3 forward_section.17
  93.6 5.8 %collective-permute-start.19 = (f32[2,2,128,128]{3,2,1,0:T(8,128)S(1)}, f32[2,2,128,128]{3,2,1,0:T(8,128)S(1)}, u32[]{:S(2)}, u32[]{:S(2)}) collective-permute-start(f32[2,2,128,128]{3,2,1,0:T(8,128)S(1)} %get-tuple-element.102.refs_2_), channel_id=1, source_target_pairs={{0,4},{4,8},{8,12},{1,5},{5,9},{9,13},{2,6},{6,10},{10,14},{3,7},{... | collective-permute-start | bytes 786440 | tf_op jit(solution)/shard_map/ppermute | solution.py:571
  102.0 1.4 deposit_patches.16.refs_3_
  103.4 1.3 forward_section.18
  104.7 4.6 %collective-permute-start.21 = (f32[2,2,128,128]{3,2,1,0:T(8,128)S(1)}, f32[2,2,128,128]{3,2,1,0:T(8,128)S(1)}, u32[]{:S(2)}, u32[]{:S(2)}) collective-permute-start(f32[2,2,128,128]{3,2,1,0:T(8,128)S(1)} %get-tuple-element.106.refs_2_), channel_id=1, source_target_pairs={{0,4},{4,8},{8,12},{1,5},{5,9},{9,13},{2,6},{6,10},{10,14},{3,7},{... | collective-permute-start | bytes 786440 | tf_op jit(solution)/shard_map/ppermute | solution.py:571
  112.0 1.6 collective-permute-start.27
  113.6 1.4 deposit_patches.17.refs_2_
  115.7 3.2 %collective-permute-done.20.refs_1_ = f32[2,2,128,128]{3,2,1,0:T(8,128)S(1)} collective-permute-done((f32[2,2,128,128]{3,2,1,0:T(8,128)S(1)}, f32[2,2,128,128]{3,2,1,0:T(8,128)S(1)}, u32[]{:S(2)}, u32[]{:S(2)}) %collective-permute-start.20) | collective-permute-done | bytes 262176 | tf_op jit(solution)/shard_map/ppermute | solution.py:571
  121.5 1.4 deposit_patches.18.refs_2_
  123.6 6.9 %collective-permute-done.22.refs_1_ = f32[2,2,128,128]{3,2,1,0:T(8,128)S(1)} collective-permute-done((f32[2,2,128,128]{3,2,1,0:T(8,128)S(1)}, f32[2,2,128,128]{3,2,1,0:T(8,128)S(1)}, u32[]{:S(2)}, u32[]{:S(2)}) %collective-permute-start.22) | collective-permute-done | bytes 262176 | tf_op jit(solution)/shard_map/ppermute | solution.py:571
  133.8 1.4 deposit_patches.19.refs_2_
  135.2 4.9 %collective-permute-done.24.refs_1_ = f32[2,2,128,128]{3,2,1,0:T(8,128)S(1)} collective-permute-done((f32[2,2,128,128]{3,2,1,0:T(8,128)S(1)}, f32[2,2,128,128]{3,2,1,0:T(8,128)S(1)}, u32[]{:S(2)}, u32[]{:S(2)}) %collective-permute-start.24) | collective-permute-done | bytes 262176 | tf_op jit(solution)/shard_map/ppermute | solution.py:571
  142.6 2.1 %deposit_patches.20.refs_2_ = f32[42368,128]{1,0:T(8,128)S(1)} custom-call(s32[1,128]{1,0:T(1,128)S(1)} %get-tuple-element.150.refs_0_, f32[2048,128]{1,0:T(8,128)S(1)} %collective-permute-done.27.refs_1_, f32[42368,128]{1,0:T(8,128)S(1)} %get-tuple-element.121.refs_2_), custom_call_target="tpu_custom_call", output_to_operand_aliasing={{}: (2, {})} | custom-call | flops 3145728 | bytes 4718592 | tf_op jit(solution)/shard_map/deposit_patches/pallas_call | solution.py:171
  144.7 5.4 %collective-permute-done.26.refs_1_ = f32[2,2,128,128]{3,2,1,0:T(8,128)S(1)} collective-permute-done((f32[2,2,128,128]{3,2,1,0:T(8,128)S(1)}, f32[2,2,128,128]{3,2,1,0:T(8,128)S(1)}, u32[]{:S(2)}, u32[]{:S(2)}) %collective-permute-start.26) | collective-permute-done | bytes 262176 | tf_op jit(solution)/shard_map/ppermute | solution.py:571
  152.7 1.4 deposit_patches.21.refs_2_
  154.1 7.1 %collective-permute-done.28.refs_1_ = f32[2,2,128,128]{3,2,1,0:T(8,128)S(1)} collective-permute-done((f32[2,2,128,128]{3,2,1,0:T(8,128)S(1)}, f32[2,2,128,128]{3,2,1,0:T(8,128)S(1)}, u32[]{:S(2)}, u32[]{:S(2)}) %collective-permute-start.28) | collective-permute-done | bytes 262176 | tf_op jit(solution)/shard_map/ppermute | solution.py:571
  163.8 1.8 deposit_patches.22.refs_2_
  165.6 5.2 %collective-permute-done.29.refs_1_ = f32[2,2,128,128]{3,2,1,0:T(8,128)S(1)} collective-permute-done((f32[2,2,128,128]{3,2,1,0:T(8,128)S(1)}, f32[2,2,128,128]{3,2,1,0:T(8,128)S(1)}, u32[]{:S(2)}, u32[]{:S(2)}) %collective-permute-start.29) | collective-permute-done | bytes 262176 | tf_op jit(solution)/shard_map/ppermute | solution.py:571
  170.8 2.0 %backward_section.21 = (f32[42368,128]{1,0:T(8,128)S(1)}, f32[2,2,128,128]{3,2,1,0:T(8,128)}) custom-call(bf16[2,2,2,256,256]{4,3,2,1,0:T(8,128)(2,1)S(1)} %copy-done, f32[2,2,128,128]{3,2,1,0:T(8,128)S(1)} %collective-permute-done.29.refs_1_, f32[42368,128]{1,0:T(8,128)S(1)} %deposit_patches.22.refs_2_), custom_call_target="tpu_custom_call", output_to_operand_aliasing={{0}: (2, {})} | custom-call | flops 402653184 | bytes 2097152 | tf_op jit(solution)/shard_map/backward_section/pallas_call | solution.py:171
  172.8 1.4 deposit_patches.23.state
  179.7 1.7 conditional.1
  179.7 1.7 fusion
  (78 shorter events, 36.5 us)
Async XLA Ops:
  0.0 17.4 %copy-start = (bf16[2,2,2,256,256]{4,3,2,1,0:T(8,128)(2,1)S(1)}, bf16[2,2,2,256,256]{4,3,2,1,0:T(8,128)(2,1)}, u32[]{:S(2)}) copy-start(bf16[2,2,2,256,256]{4,3,2,1,0:T(8,128)(2,1)} %constant.20.clone.refs_0_) | copy-start | bytes 3145732
  0.0 17.4 %copy-start.1 = (f32[2,128,128]{2,1,0:T(8,128)S(1)}, f32[2,128,128]{2,1,0:T(8,128)}, u32[]{:S(2)}) copy-start(f32[2,128,128]{2,1,0:T(8,128)} %refs_2_.13) | copy-start | bytes 393220
  0.0 16.1 %collective-permute-start.5 = (f32[2,2,384,768]{3,2,1,0:T(8,128)}, f32[2,2,384,768]{3,2,1,0:T(8,128)S(1)}, u32[]{:S(2)}, u32[]{:S(2)}) collective-permute-start(f32[2,2,384,768]{3,2,1,0:T(8,128)} %refs_4_.1), channel_id=1, source_target_pairs={{0,1},{1,0},{2,3},{3,2},{4,5},{5,4},{6,7},{7,6},{8,9},{9,8},{10,11... | collective-permute-start | bytes 14155784 | tf_op jit(solution)/shard_map/ppermute | solution.py:483
  0.5 4.2 %collective-permute-start.2 = (s32[16]{0:T(128)}, s32[16]{0:T(128)S(1)}, u32[]{:S(2)}, u32[]{:S(2)}) collective-permute-start(s32[16]{0:T(128)} %bitcast.25), channel_id=1, source_target_pairs={{0,2},{2,0},{1,3},{3,1},{4,6},{6,4},{5,7},{7,5},{8,10},{10,8},{9,1... | collective-permute-start | bytes 200 | tf_op jit(solution)/shard_map/ppermute | solution.py:483
  3.0 5.2 %collective-permute-start.3 = (s32[16]{0:T(128)}, s32[16]{0:T(128)S(1)}, u32[]{:S(2)}, u32[]{:S(2)}) collective-permute-start(s32[16]{0:T(128)} %bitcast.26), channel_id=1, source_target_pairs={{0,1},{1,0},{2,3},{3,2},{4,5},{5,4},{6,7},{7,6},{8,9},{9,8},{10,11... | collective-permute-start | bytes 200 | tf_op jit(solution)/shard_map/ppermute | solution.py:483
  3.2 5.0 %collective-permute-start.4 = (s32[16]{0:T(128)}, s32[16]{0:T(128)S(1)}, u32[]{:S(2)}, u32[]{:S(2)}) collective-permute-start(s32[16]{0:T(128)} %bitcast.27), channel_id=1, source_target_pairs={{0,3},{1,2},{2,1},{3,0},{4,7},{5,6},{6,5},{7,4},{8,11},{9,10},{10,... | collective-permute-start | bytes 200 | tf_op jit(solution)/shard_map/ppermute | solution.py:545
  8.2 0.7 copy-start.2
  8.9 0.7 copy-start.3
  12.8 0.7 collective-permute-start.10
  13.5 5.2 %copy-start.6 = (f32[16,1,128,128]{3,2,1,0:T(8,128)}, f32[16,1,128,128]{3,2,1,0:T(8,128)S(1)}, u32[]{:S(2)}) copy-start(f32[16,1,128,128]{3,2,1,0:T(8,128)S(1)} %collective-permute-done.10) | copy-start | bytes 3145732
  15.3 32.9 %collective-permute-start.11 = (f32[32,1,128,128]{3,2,1,0:T(8,128)S(1)}, f32[32,1,128,128]{3,2,1,0:T(8,128)S(1)}, u32[]{:S(2)}, u32[]{:S(2)}) collective-permute-start(f32[32,1,128,128]{3,2,1,0:T(8,128)S(1)} %pad_maximum_fusion), channel_id=1, source_target_pairs={{12,13},{13,12},{14,15},{15,14},{28,29},{29,28},{30,31},{31,30}} | collective-permute-start | bytes 6291464 | tf_op jit(solution)/shard_map/ppermute | solution.py:551
  18.7 9.4 %collective-permute-start.6 = (f32[2,2,128,128]{3,2,1,0:T(8,128)S(1)}, f32[2,2,128,128]{3,2,1,0:T(8,128)S(1)}, u32[]{:S(2)}, u32[]{:S(2)}) collective-permute-start(f32[2,2,128,128]{3,2,1,0:T(8,128)S(1)} %get-tuple-element.81), channel_id=1, source_target_pairs={{0,4},{1,5},{2,6},{3,7},{16,20},{17,21},{18,22},{19,23}} | collective-permute-start | bytes 786440 | tf_op jit(solution)/shard_map/ppermute | solution.py:571
  29.5 9.4 %collective-permute-start.7 = (f32[2,2,128,128]{3,2,1,0:T(8,128)S(1)}, f32[2,2,128,128]{3,2,1,0:T(8,128)S(1)}, u32[]{:S(2)}, u32[]{:S(2)}) collective-permute-start(f32[2,2,128,128]{3,2,1,0:T(8,128)S(1)} %get-tuple-element.83), channel_id=1, source_target_pairs={{0,4},{4,8},{1,5},{5,9},{2,6},{6,10},{3,7},{7,11},{16,20},{20,24},... | collective-permute-start | bytes 786440 | tf_op jit(solution)/shard_map/ppermute | solution.py:571
  40.2 11.4 %collective-permute-start.9 = (f32[2,2,128,128]{3,2,1,0:T(8,128)S(1)}, f32[2,2,128,128]{3,2,1,0:T(8,128)S(1)}, u32[]{:S(2)}, u32[]{:S(2)}) collective-permute-start(f32[2,2,128,128]{3,2,1,0:T(8,128)S(1)} %get-tuple-element.87), channel_id=1, source_target_pairs={{0,4},{4,8},{8,12},{1,5},{5,9},{9,13},{2,6},{6,10},{10,14},{3,7},{... | collective-permute-start | bytes 786440 | tf_op jit(solution)/shard_map/ppermute | solution.py:571
  44.6 3.6 %collective-permute-start.8 = (s32[1,128]{1,0:T(1,128)S(1)}, s32[1,128]{1,0:T(1,128)S(1)}, u32[]{:S(2)}, u32[]{:S(2)}) collective-permute-start(s32[1,128]{1,0:T(1,128)S(1)} %get-tuple-element.150.refs_0_), channel_id=1, source_target_pairs={{0,16},{16,0},{1,17},{17,1},{2,18},{18,2},{3,19},{19,3},{4,20},{20... | collective-permute-start | bytes 1544 | tf_op jit(solution)/shard_map/ppermute | solution.py:483
  48.2 3.3 %copy-start.8 = (s32[1,128]{1,0:T(1,128)}, s32[1,128]{1,0:T(1,128)S(1)}, u32[]{:S(2)}) copy-start(s32[1,128]{1,0:T(1,128)S(1)} %collective-permute-done.8) | copy-start | bytes 1540
  48.2 1.3 copy-start.7
  52.9 6.1 %collective-permute-start.13 = (f32[2,2,128,128]{3,2,1,0:T(8,128)S(1)}, f32[2,2,128,128]{3,2,1,0:T(8,128)S(1)}, u32[]{:S(2)}, u32[]{:S(2)}) collective-permute-start(f32[2,2,128,128]{3,2,1,0:T(8,128)S(1)} %get-tuple-element.90.refs_1_), channel_id=1, source_target_pairs={{0,4},{4,8},{8,12},{1,5},{5,9},{9,13},{2,6},{6,10},{10,14},{3,7},{... | collective-permute-start | bytes 786440 | tf_op jit(solution)/shard_map/ppermute | solution.py:571
  55.1 23.2 %collective-permute-start.12 = (f32[2,2,128,128]{3,2,1,0:T(8,128)S(1)}, f32[2,2,128,128]{3,2,1,0:T(8,128)S(1)}, u32[]{:S(2)}, u32[]{:S(2)}) collective-permute-start(f32[2,2,128,128]{3,2,1,0:T(8,128)S(1)} %get-tuple-element.92), channel_id=1, source_target_pairs={{12,8},{13,9},{14,10},{15,11},{28,24},{29,25},{30,26},{31,27}} | collective-permute-start | bytes 786440 | tf_op jit(solution)/shard_map/ppermute | solution.py:571
  60.3 21.9 %collective-permute-start.15 = (f32[2,2,128,128]{3,2,1,0:T(8,128)S(1)}, f32[2,2,128,128]{3,2,1,0:T(8,128)S(1)}, u32[]{:S(2)}, u32[]{:S(2)}) collective-permute-start(f32[2,2,128,128]{3,2,1,0:T(8,128)S(1)} %get-tuple-element.94.refs_2_), channel_id=1, source_target_pairs={{0,4},{4,8},{8,12},{1,5},{5,9},{9,13},{2,6},{6,10},{10,14},{3,7},{... | collective-permute-start | bytes 786440 | tf_op jit(solution)/shard_map/ppermute | solution.py:571
  78.3 10.1 %collective-permute-start.14 = (f32[2,2,128,128]{3,2,1,0:T(8,128)S(1)}, f32[2,2,128,128]{3,2,1,0:T(8,128)S(1)}, u32[]{:S(2)}, u32[]{:S(2)}) collective-permute-start(f32[2,2,128,128]{3,2,1,0:T(8,128)S(1)} %get-tuple-element.96), channel_id=1, source_target_pairs={{8,4},{12,8},{9,5},{13,9},{10,6},{14,10},{11,7},{15,11},{24,20},{2... | collective-permute-start | bytes 786440 | tf_op jit(solution)/shard_map/ppermute | solution.py:571
  83.6 8.7 %collective-permute-start.17 = (f32[2,2,128,128]{3,2,1,0:T(8,128)S(1)}, f32[2,2,128,128]{3,2,1,0:T(8,128)S(1)}, u32[]{:S(2)}, u32[]{:S(2)}) collective-permute-start(f32[2,2,128,128]{3,2,1,0:T(8,128)S(1)} %get-tuple-element.98.refs_2_), channel_id=1, source_target_pairs={{0,4},{4,8},{8,12},{1,5},{5,9},{9,13},{2,6},{6,10},{10,14},{3,7},{... | collective-permute-start | bytes 786440 | tf_op jit(solution)/shard_map/ppermute | solution.py:571
  88.4 11.0 %collective-permute-start.16 = (f32[2,2,128,128]{3,2,1,0:T(8,128)S(1)}, f32[2,2,128,128]{3,2,1,0:T(8,128)S(1)}, u32[]{:S(2)}, u32[]{:S(2)}) collective-permute-start(f32[2,2,128,128]{3,2,1,0:T(8,128)S(1)} %get-tuple-element.100), channel_id=1, source_target_pairs={{4,0},{8,4},{12,8},{5,1},{9,5},{13,9},{6,2},{10,6},{14,10},{7,3},{... | collective-permute-start | bytes 786440 | tf_op jit(solution)/shard_map/ppermute | solution.py:571
  93.6 9.8 %collective-permute-start.19 = (f32[2,2,128,128]{3,2,1,0:T(8,128)S(1)}, f32[2,2,128,128]{3,2,1,0:T(8,128)S(1)}, u32[]{:S(2)}, u32[]{:S(2)}) collective-permute-start(f32[2,2,128,128]{3,2,1,0:T(8,128)S(1)} %get-tuple-element.102.refs_2_), channel_id=1, source_target_pairs={{0,4},{4,8},{8,12},{1,5},{5,9},{9,13},{2,6},{6,10},{10,14},{3,7},{... | collective-permute-start | bytes 786440 | tf_op jit(solution)/shard_map/ppermute | solution.py:571
  100.7 8.6 %collective-permute-start.18 = (f32[2,2,128,128]{3,2,1,0:T(8,128)S(1)}, f32[2,2,128,128]{3,2,1,0:T(8,128)S(1)}, u32[]{:S(2)}, u32[]{:S(2)}) collective-permute-start(f32[2,2,128,128]{3,2,1,0:T(8,128)S(1)} %get-tuple-element.104), channel_id=1, source_target_pairs={{4,0},{8,4},{12,8},{5,1},{9,5},{13,9},{6,2},{10,6},{14,10},{7,3},{... | collective-permute-start | bytes 786440 | tf_op jit(solution)/shard_map/ppermute | solution.py:571
  104.7 10.2 %collective-permute-start.21 = (f32[2,2,128,128]{3,2,1,0:T(8,128)S(1)}, f32[2,2,128,128]{3,2,1,0:T(8,128)S(1)}, u32[]{:S(2)}, u32[]{:S(2)}) collective-permute-start(f32[2,2,128,128]{3,2,1,0:T(8,128)S(1)} %get-tuple-element.106.refs_2_), channel_id=1, source_target_pairs={{0,4},{4,8},{8,12},{1,5},{5,9},{9,13},{2,6},{6,10},{10,14},{3,7},{... | collective-permute-start | bytes 786440 | tf_op jit(solution)/shard_map/ppermute | solution.py:571
  110.6 8.3 %collective-permute-start.20 = (f32[2,2,128,128]{3,2,1,0:T(8,128)S(1)}, f32[2,2,128,128]{3,2,1,0:T(8,128)S(1)}, u32[]{:S(2)}, u32[]{:S(2)}) collective-permute-start(f32[2,2,128,128]{3,2,1,0:T(8,128)S(1)} %get-tuple-element.108), channel_id=1, source_target_pairs={{4,0},{8,4},{12,8},{5,1},{9,5},{13,9},{6,2},{10,6},{14,10},{7,3},{... | collective-permute-start | bytes 786440 | tf_op jit(solution)/shard_map/ppermute | solution.py:571
  112.0 30.6 %collective-permute-start.27 = (f32[2048,128]{1,0:T(8,128)S(1)}, f32[2048,128]{1,0:T(8,128)S(1)}, u32[]{:S(2)}, u32[]{:S(2)}) collective-permute-start(f32[2048,128]{1,0:T(8,128)S(1)} %slice.38), channel_id=1, source_target_pairs={{0,2},{2,0},{1,3},{3,1},{4,6},{6,4},{5,7},{7,5},{8,10},{10,8},{9,1... | collective-permute-start | bytes 3145736 | tf_op jit(solution)/shard_map/ppermute | solution.py:483
  115.0 7.9 %collective-permute-start.23 = (f32[2,2,128,128]{3,2,1,0:T(8,128)S(1)}, f32[2,2,128,128]{3,2,1,0:T(8,128)S(1)}, u32[]{:S(2)}, u32[]{:S(2)}) collective-permute-start(f32[2,2,128,128]{3,2,1,0:T(8,128)S(1)} %get-tuple-element.110.refs_2_), channel_id=1, source_target_pairs={{4,8},{8,12},{5,9},{9,13},{6,10},{10,14},{7,11},{11,15},{20,24},{2... | collective-permute-start | bytes 786440 | tf_op jit(solution)/shard_map/ppermute | solution.py:571
  120.2 10.3 %collective-permute-start.22 = (f32[2,2,128,128]{3,2,1,0:T(8,128)S(1)}, f32[2,2,128,128]{3,2,1,0:T(8,128)S(1)}, u32[]{:S(2)}, u32[]{:S(2)}) collective-permute-start(f32[2,2,128,128]{3,2,1,0:T(8,128)S(1)} %get-tuple-element.112), channel_id=1, source_target_pairs={{4,0},{8,4},{12,8},{5,1},{9,5},{13,9},{6,2},{10,6},{14,10},{7,3},{... | collective-permute-start | bytes 786440 | tf_op jit(solution)/shard_map/ppermute | solution.py:571
  122.9 12.2 %collective-permute-start.25 = (f32[2,2,128,128]{3,2,1,0:T(8,128)S(1)}, f32[2,2,128,128]{3,2,1,0:T(8,128)S(1)}, u32[]{:S(2)}, u32[]{:S(2)}) collective-permute-start(f32[2,2,128,128]{3,2,1,0:T(8,128)S(1)} %get-tuple-element.114.refs_2_), channel_id=1, source_target_pairs={{8,12},{9,13},{10,14},{11,15},{24,28},{25,29},{26,30},{27,31}} | collective-permute-start | bytes 786440 | tf_op jit(solution)/shard_map/ppermute | solution.py:571
  131.8 8.3 %collective-permute-start.24 = (f32[2,2,128,128]{3,2,1,0:T(8,128)S(1)}, f32[2,2,128,128]{3,2,1,0:T(8,128)S(1)}, u32[]{:S(2)}, u32[]{:S(2)}) collective-permute-start(f32[2,2,128,128]{3,2,1,0:T(8,128)S(1)} %get-tuple-element.116), channel_id=1, source_target_pairs={{4,0},{8,4},{12,8},{5,1},{9,5},{13,9},{6,2},{10,6},{14,10},{7,3},{... | collective-permute-start | bytes 786440 | tf_op jit(solution)/shard_map/ppermute | solution.py:571
  133.1 30.7 %collective-permute-start.30 = (f32[2048,128]{1,0:T(8,128)S(1)}, f32[2048,128]{1,0:T(8,128)S(1)}, u32[]{:S(2)}, u32[]{:S(2)}) collective-permute-start(f32[2048,128]{1,0:T(8,128)S(1)} %slice.39), channel_id=1, source_target_pairs={{0,2},{2,0},{1,3},{3,1},{4,6},{6,4},{5,7},{7,5},{8,10},{10,8},{9,1... | collective-permute-start | bytes 3145736 | tf_op jit(solution)/shard_map/ppermute | solution.py:483
  141.3 8.8 %collective-permute-start.26 = (f32[2,2,128,128]{3,2,1,0:T(8,128)S(1)}, f32[2,2,128,128]{3,2,1,0:T(8,128)S(1)}, u32[]{:S(2)}, u32[]{:S(2)}) collective-permute-start(f32[2,2,128,128]{3,2,1,0:T(8,128)S(1)} %get-tuple-element.120), channel_id=1, source_target_pairs={{4,0},{8,4},{12,8},{5,1},{9,5},{13,9},{6,2},{10,6},{14,10},{7,3},{... | collective-permute-start | bytes 786440 | tf_op jit(solution)/shard_map/ppermute | solution.py:571
  151.4 9.8 %collective-permute-start.28 = (f32[2,2,128,128]{3,2,1,0:T(8,128)S(1)}, f32[2,2,128,128]{3,2,1,0:T(8,128)S(1)}, u32[]{:S(2)}, u32[]{:S(2)}) collective-permute-start(f32[2,2,128,128]{3,2,1,0:T(8,128)S(1)} %get-tuple-element.122), channel_id=1, source_target_pairs={{4,0},{8,4},{5,1},{9,5},{6,2},{10,6},{7,3},{11,7},{20,16},{24,20},... | collective-permute-start | bytes 786440 | tf_op jit(solution)/shard_map/ppermute | solution.py:571
  162.5 8.3 %collective-permute-start.29 = (f32[2,2,128,128]{3,2,1,0:T(8,128)S(1)}, f32[2,2,128,128]{3,2,1,0:T(8,128)S(1)}, u32[]{:S(2)}, u32[]{:S(2)}) collective-permute-start(f32[2,2,128,128]{3,2,1,0:T(8,128)S(1)} %get-tuple-element.124), channel_id=1, source_target_pairs={{4,0},{5,1},{6,2},{7,3},{20,16},{21,17},{22,18},{23,19}} | collective-permute-start | bytes 786440 | tf_op jit(solution)/shard_map/ppermute | solution.py:571
  174.1 2.9 %copy-start.9 = (s32[1,128]{1,0:T(1,128)S(1)}, s32[1,128]{1,0:T(1,128)}, u32[]{:S(2)}) copy-start(s32[1,128]{1,0:T(1,128)} %copy-done.8) | copy-start | bytes 1540
  175.1 4.6 %collective-permute-start.31 = (f32[2,2,1,192,768]{4,3,2,1,0:T(8,128)S(1)}, f32[2,2,1,192,768]{4,3,2,1,0:T(8,128)S(1)}, u32[]{:S(2)}, u32[]{:S(2)}) collective-permute-start(f32[2,2,1,192,768]{4,3,2,1,0:T(8,128)S(1)} %get-tuple-element.128), channel_id=1, source_target_pairs={{0,1},{1,0},{2,3},{3,2},{4,5},{5,4},{6,7},{7,6},{8,9},{9,8},{10,11... | collective-permute-start | bytes 7077896 | tf_op jit(solution)/shard_map/ppermute | solution.py:483
